TPU v7x, 256 devices: a whole 4x4x8 slice. The times are simulated.
256 devices in a mesh: dp: 64 (over z, y, core), mp: 4 (over x).
Axes of the slice: x: 4, y: 4, z: 8, core: 2. Of those that a mesh axis runs over, the one named last changes fastest.
Arguments:
- left_factors: bfloat16 [128, 5, 16, 32, 1024], P('dp', None, 'mp'), may hold values from -1 to 1
- right_factors: bfloat16 [128, 5, 16, 32, 1024], P('dp', None, 'mp'), may hold values from -0.1875 to 0.1875
- observations: bfloat16 [128, 5, 64, 1024], P('dp'), may hold values from -40 to 40
Outputs:
- solution: float32 [16, 64, 1024], P('mp')
- direction: float32 [16, 64, 1024], P('mp')
- residual_estimate: float32 [64], replicated
All inputs are finite; a program needn't handle non-finite values.
Results may differ from a plain program's by a relative error of at most 0.035.
Values may be sent and summed in bfloat16 or wider, within the bound.
No kernel may reach another device: no remote copies, remote signals or barrier semaphores. Data moves between devices by JAX's collectives and lax.ppermute only.
A program may use at most 64 MiB of HBM per device.

v0:
```python
import jax
import jax.numpy as jnp
from jax import lax
from jax.sharding import PartitionSpec as P

ITERS = 2


EPSILON = 1e-06


def to_data(left_factors, coeffs):
    return jnp.einsum(
        "rctkb,rctkn->rcnb",
        left_factors,
        coeffs.astype(jnp.bfloat16),
        preferred_element_type=jnp.float32,
    )


def to_model(right_factors, coeffs):
    return jnp.einsum(
        "rctkb,rctkn->tnb",
        right_factors,
        coeffs.astype(jnp.bfloat16),
        preferred_element_type=jnp.float32,
    )


def model_coeffs(right_factors, model):
    model_half = model.astype(jnp.bfloat16)
    result = jnp.einsum(
        "rctkb,tnb->rctkn", right_factors, model_half, preferred_element_type=jnp.float32
    )
    return result


def data_coeffs(left_factors, data_share):
    return jnp.einsum(
        "rctkb,rcnb->rctkn",
        left_factors,
        lax.all_gather(data_share.astype(jnp.bfloat16), "mp", axis=3, tiled=True),
        preferred_element_type=jnp.float32,
    )


def model_normalize(partial_value, previous, data_len):
    total = lax.psum(partial_value, "dp")
    model_raw = total if previous is None else total - data_len[:, None] * previous
    squares = lax.psum(jnp.sum(model_raw * model_raw, axis=(0, 2)), "mp")
    model_len = jnp.sqrt(squares + EPSILON)
    return (model_raw / model_len[:, None], model_len)


def on_device(left_factors, right_factors, observations):
    values = observations.astype(jnp.float32)
    data_len = jnp.sqrt(lax.psum(jnp.sum(values * values, axis=(0, 1, 3)), "dp") + EPSILON)
    data_unit = values / data_len[:, None]
    share_width = observations.shape[3] // lax.axis_size("mp")
    data_share = lax.dynamic_slice_in_dim(
        data_unit, lax.axis_index("mp") * share_width, share_width, 3
    )
    start_coeffs = jnp.einsum(
        "rctkb,rcnb->rctkn",
        left_factors,
        data_unit.astype(jnp.bfloat16),
        preferred_element_type=jnp.float32,
    )
    model, model_len = model_normalize(to_model(right_factors, start_coeffs), None, data_len)
    solution = jnp.zeros_like(model)
    direction = model
    residual_estimate = data_len
    diagonal_bar = model_len
    for sweep in range(ITERS):
        partial_value = to_data(left_factors, model_coeffs(right_factors, model))
        shares = lax.psum_scatter(partial_value, "mp", scatter_dimension=3, tiled=True)
        data_raw = shares - model_len[:, None] * data_share
        squares = lax.psum(jnp.sum(data_raw * data_raw, axis=(0, 1, 3)), ("dp", "mp"))
        data_len = jnp.sqrt(squares + EPSILON)
        data_share = data_raw / data_len[:, None]
        partial_model = to_model(right_factors, data_coeffs(left_factors, data_share))
        model, model_len = model_normalize(partial_model, model, data_len)
        rotation = jnp.sqrt(diagonal_bar * diagonal_bar + data_len * data_len)
        cosine_term = diagonal_bar / rotation
        sine_term = data_len / rotation
        coupling = sine_term * model_len
        diagonal_bar = -cosine_term * model_len
        step_size = cosine_term * residual_estimate
        residual_estimate = sine_term * residual_estimate
        solution = solution + (step_size / rotation)[:, None] * direction
        direction = model - (coupling / rotation)[:, None] * direction
    return (solution, direction, residual_estimate)


def solution(mesh):
    in_specs = (
        P("dp", None, "mp", None, None),
        P("dp", None, "mp", None, None),
        P("dp", None, None, None),
    )
    out_specs = (P("mp", None, None), P("mp", None, None), P())
    return jax.shard_map(
        on_device, mesh=mesh, in_specs=in_specs, out_specs=out_specs, check_vma=False
    )
```

profile of v0, /device:TPU:1, one launch (start us, length us, event | category | flops | bytes accessed | tf_op | source)
XLA Modules:
  0.0 1045.8 jit_solution(3430945139245567649)
XLA Ops:
  7.2 0.0 copy-start
  7.2 0.0 all-reduce.4.cloned.1.call-start
  7.2 1.8 fusion
  9.1 128.3 %psum.63 = f32[64]{0:T(128)S(1)} all-reduce(f32[64]{0:T(128)S(1)} %fusion), channel_id=1, replica_groups=mesh['dp'=64,'mp'=4] {'dp'}, use_global_device_ids=true, to_apply=%region_1.0 | all-reduce | flops 64 | bytes 512 | tf_op jit(solution)/shard_map/psum | solution.py:57
  137.3 0.0 copy-start.1
  137.3 3.5 convert_divide_fusion
  140.9 0.0 copy-done.1
  140.9 0.8 fusion.52
  141.7 0.0 copy-done
  141.7 1.7 fusion.13
  143.4 0.0 all-reduce.4.cloned.1.call-update
  143.4 0.0 reduce-scatter.3.cloned.1.call-start
  143.5 182.9 %all-reduce.4.cloned.1.call-done = f32[4,64,1024]{2,1,0:T(8,128)} async-done(((f32[4,64,1024]{2,1,0:T(8,128)}), f32[4,64,1024]{2,1,0:T(8,128)}) %all-reduce.4.cloned.1.call-update) | async-done | bytes 1048592 | tf_op jit(solution)/shard_map/psum | solution.py:48
  326.4 1.4 multiply_reduce_fusion.2
  327.8 8.4 psum.65
  336.2 5.0 convolution_bitcast_fusion.1
  341.1 0.0 reduce-scatter.3.cloned.1.call-update
  341.2 0.0 all-gather.3.cloned.1.call-start
  341.2 35.7 %reduce-scatter.3.cloned.1.call-done = f32[2,5,64,256]{3,2,1,0:T(8,128)} async-done(((f32[2,5,64,1024]{3,2,1,0:T(8,128)}), f32[2,5,64,256]{3,2,1,0:T(8,128)}) %reduce-scatter.3.cloned.1.call-update) | async-done | bytes 655376 | tf_op jit(solution)/shard_map/reduce_scatter | solution.py:76
  376.9 1.6 multiply_reduce_fusion.4
  378.4 76.0 %psum.66 = f32[64]{0:T(128)S(1)} all-reduce(f32[64]{0:T(128)S(1)} %get-tuple-element.11), channel_id=1, replica_groups=mesh['dp'=64,'mp'=4] {'dp','mp'}, use_global_device_ids=true, to_apply=%region_7.0 | all-reduce | flops 64 | bytes 512 | tf_op jit(solution)/shard_map/psum | solution.py:78
  454.4 0.9 fusion.68
  455.3 0.0 all-gather.3.cloned.1.call-update
  455.3 0.0 all-reduce.6.cloned.1.call-start
  455.4 26.7 %all-gather.3.cloned.1.call-done = bf16[2,5,64,1024]{3,2,1,0:T(8,128)(2,1)} async-done(((bf16[2,5,64,256]{3,2,1,0:T(8,128)(2,1)}), bf16[2,5,64,1024]{3,2,1,0:T(8,128)(2,1)}) %all-gather.3.cloned.1.call-update) | async-done | bytes 1310736 | tf_op jit(solution)/shard_map/all_gather | solution.py:42
  482.0 3.0 fusion.47
  485.0 1.7 fusion.16
  486.7 0.0 all-reduce.6.cloned.1.call-update
  486.7 0.0 reduce-scatter.5.cloned.1.call-start
  486.8 185.8 %all-reduce.6.cloned.1.call-done = f32[4,64,1024]{2,1,0:T(8,128)} async-done(((f32[4,64,1024]{2,1,0:T(8,128)}), f32[4,64,1024]{2,1,0:T(8,128)}) %all-reduce.6.cloned.1.call-update) | async-done | bytes 1048592 | tf_op jit(solution)/shard_map/psum | solution.py:48
  672.6 1.9 multiply_reduce_fusion.1
  674.5 8.4 psum.68
  682.9 2.9 broadcast_divide_fusion
  685.8 4.9 convolution_bitcast_fusion
  690.7 0.0 reduce-scatter.5.cloned.1.call-update
  690.7 0.0 all-gather.5.cloned.1.call-start
  690.7 35.7 %reduce-scatter.5.cloned.1.call-done = f32[2,5,64,256]{3,2,1,0:T(8,128)} async-done(((f32[2,5,64,1024]{3,2,1,0:T(8,128)}), f32[2,5,64,256]{3,2,1,0:T(8,128)}) %reduce-scatter.5.cloned.1.call-update) | async-done | bytes 655376 | tf_op jit(solution)/shard_map/reduce_scatter | solution.py:76
  726.4 2.2 multiply_reduce_fusion.3
  728.6 76.0 %psum.69 = f32[64]{0:T(128)S(1)} all-reduce(f32[64]{0:T(128)S(1)} %get-tuple-element.9), channel_id=1, replica_groups=mesh['dp'=64,'mp'=4] {'dp','mp'}, use_global_device_ids=true, to_apply=%region_13.0 | all-reduce | flops 64 | bytes 512 | tf_op jit(solution)/shard_map/psum | solution.py:78
  804.6 0.6 multiply_multiply_fusion
  805.1 2.0 divide_convert_fusion
  807.1 0.0 all-gather.5.cloned.1.call-update
  807.1 0.0 all-reduce.8.cloned.1.call-start
  807.2 26.7 %all-gather.5.cloned.1.call-done = bf16[2,5,64,1024]{3,2,1,0:T(8,128)(2,1)} async-done(((bf16[2,5,64,256]{3,2,1,0:T(8,128)(2,1)}), bf16[2,5,64,1024]{3,2,1,0:T(8,128)(2,1)}) %all-gather.5.cloned.1.call-update) | async-done | bytes 1310736 | tf_op jit(solution)/shard_map/all_gather | solution.py:42
  833.8 3.0 fusion.42
  836.8 1.7 fusion.19
  838.5 0.0 all-reduce.8.cloned.1.call-update
  838.5 186.2 %all-reduce.8.cloned.1.call-done = f32[4,64,1024]{2,1,0:T(8,128)} async-done(((f32[4,64,1024]{2,1,0:T(8,128)}), f32[4,64,1024]{2,1,0:T(8,128)}) %all-reduce.8.cloned.1.call-update) | async-done | bytes 1048592 | tf_op jit(solution)/shard_map/psum | solution.py:48
  1024.7 1.9 multiply_reduce_fusion
  1026.6 8.4 psum.71
  1035.1 3.9 multiply_subtract_fusion
  (5 shorter events, 0.0 us)
Async XLA Ops:
  7.2 134.5 %copy-start = (bf16[2,5,4,32,1024]{4,3,2,1,0:T(8,128)(2,1)S(1)}, bf16[2,5,4,32,1024]{4,3,2,1,0:T(8,128)(2,1)}, u32[]{:S(2)}) copy-start(bf16[2,5,4,32,1024]{4,3,2,1,0:T(8,128)(2,1)} %param.4) | copy-start | bytes 7864324
  7.2 319.2 %all-reduce.4.cloned.1.call-start = ((), (), s32[]{:S(2)}) async-start(), calls=%async_computation.2 | async-start | bytes 2097152 | tf_op jit(solution)/shard_map/psum | solution.py:48
  137.3 3.5 copy-start.1
  143.4 233.5 %reduce-scatter.3.cloned.1.call-start = ((), (), s32[]{:S(2)}) async-start(), calls=%async_computation.3 | async-start | bytes 3276800 | tf_op jit(solution)/shard_map/reduce_scatter | solution.py:76
  341.2 140.9 %all-gather.3.cloned.1.call-start = ((), (), s32[]{:S(2)}) async-start(), calls=%async_computation.4 | async-start | bytes 1638400 | tf_op jit(solution)/shard_map/all_gather | solution.py:42
  455.3 217.3 %all-reduce.6.cloned.1.call-start = ((), (), s32[]{:S(2)}) async-start(), calls=%async_computation.5 | async-start | bytes 2097152 | tf_op jit(solution)/shard_map/psum | solution.py:48
  486.7 239.7 %reduce-scatter.5.cloned.1.call-start = ((), (), s32[]{:S(2)}) async-start(), calls=%async_computation.6 | async-start | bytes 3276800 | tf_op jit(solution)/shard_map/reduce_scatter | solution.py:76
  690.7 143.2 %all-gather.5.cloned.1.call-start = ((), (), s32[]{:S(2)}) async-start(), calls=%async_computation.7 | async-start | bytes 1638400 | tf_op jit(solution)/shard_map/all_gather | solution.py:42
  807.1 217.6 %all-reduce.8.cloned.1.call-start = ((), (), s32[]{:S(2)}) async-start(), calls=%async_computation.8 | async-start | bytes 2097152 | tf_op jit(solution)/shard_map/psum | solution.py:48
Sparse Core Ops, SparseCore 0:
  143.5 182.7 all-reduce.3
  341.3 35.5 reduce-scatter.2
  455.4 26.5 all-gather.2
  486.8 185.7 all-reduce.5
  690.8 35.5 reduce-scatter.4
  807.2 26.5 all-gather.4
  838.6 186.0 all-reduce.7
where the time goes:
time: 1050 us
  waiting for transfers between devices  680 us (65%)
  blocking collectives  305 us (29%)
  other arithmetic  24.5 us (2%)
  matrix products  21.6 us (2%)
  between operations  14.2 us (1%)
    psum x3, waiting for transfers between devices, model_normalize(): total = lax.psum(partial_value, 'dp')  555 us
    psum x2, blocking collectives, on_device(): lax.psum(jnp.sum(data_raw * data_raw, axis=(0, 1, 3)), ('dp', 'mp'))  152 us
    psum x1, blocking collectives, on_device(): lax.psum(jnp.sum(values * values, axis=(0, 1, 3)), 'dp') + EPSILON  128 us
    reduce_scatter x2, waiting for transfers between devices, on_device(): lax.psum_scatter(partial_value, 'mp', scatter_dimension=3, tiled=True)  71.3 us
    all_gather x2, waiting for transfers between devices, data_coeffs(): lax.all_gather(data_share.astype(jnp.bfloat16), 'mp', axis=3, tiled=True)  53.3 us
    psum x3, blocking collectives, model_normalize(): squares = lax.psum(jnp.sum(model_raw * model_raw, axis=(0, 2)), 'mp')  25.2 us
  transfers between devices with their start and end apart: 7, of which 7 were waited for; matrix products, arithmetic and copies ran while one was open for 0% of the time, Pallas kernels for 0%

commit v1 on v0

v1 whole, which is shorter than its diff:
```python
import functools

import jax
import jax.numpy as jnp
from jax import lax
from jax.experimental import pallas as pl
from jax.experimental.pallas import tpu as pltpu
from jax.sharding import Mesh
from jax.sharding import PartitionSpec as P

ITERS = 2
EPSILON = 1e-06
ORDER = (2, 1, 0, 5, 4, 3, 8, 7, 6, 9)
BF = jnp.bfloat16
F32 = jnp.float32
VMEM_LIMIT = 40 * 1024 * 1024


def call(kernel, outs, scratch=(), name=None):
    def run(places, *operands):
        return pl.pallas_call(
            kernel,
            out_shape=[jax.ShapeDtypeStruct(shape, dtype) for shape, dtype in outs],
            in_specs=[pl.BlockSpec(memory_space=pltpu.SMEM)]
            + [pl.BlockSpec(memory_space=pltpu.VMEM)] * len(operands),
            out_specs=[pl.BlockSpec(memory_space=pltpu.VMEM)] * len(outs),
            scratch_shapes=[pltpu.VMEM(shape, dtype) for shape, dtype in scratch],
            compiler_params=pltpu.CompilerParams(vmem_limit_bytes=VMEM_LIMIT),
            name=name,
        )(places, *operands)

    return run


def dot(first, second):
    return jnp.dot(first, second, preferred_element_type=F32)


def dot_nt(first, second):
    return lax.dot_general(
        first, second, (((1,), (1,)), ((), ())), preferred_element_type=F32
    )


def split(value):
    first = value.astype(BF).astype(F32)
    rest = value - first
    second = rest.astype(BF).astype(F32)
    return first, second, (rest - second).astype(BF).astype(F32)


def lane_sum(value):
    return jnp.sum(value, axis=-1, keepdims=True)


def pieces_in_lanes(column):
    first, second, third = split(column)
    lane = lax.broadcasted_iota(jnp.int32, (64, 128), 1)
    return jnp.where(
        lane == 0, first, jnp.where(lane == 1, second, jnp.where(lane == 2, third, 0.0))
    )


def pieces_in_rows(row):
    first, second, third = split(row)
    at = lax.broadcasted_iota(jnp.int32, (8, 128), 0)
    return jnp.where(
        at == 0, first, jnp.where(at == 1, second, jnp.where(at == 2, third, 0.0))
    )


def diagonal():
    return lax.broadcasted_iota(jnp.int32, (64, 128), 0) == lax.broadcasted_iota(
        jnp.int32, (64, 128), 1
    )


def to_row(column):
    return jnp.sum(jnp.where(diagonal(), column, 0.0), axis=0, keepdims=True)


def to_column(row):
    return lane_sum(jnp.where(diagonal(), row, 0.0))


def write_partial(places, coeffs, right, squares, keep, send, field):
    for t in range(4):
        factors = jnp.concatenate([right[pair, t] for pair in ORDER], axis=0)
        value = dot(coeffs(t), factors)
        for i in range(8):
            field[i % 4, pl.ds(2 * t + i // 4, 64, stride=8), :] = value[
                :, 128 * i : 128 * i + 128
            ]
    core = places[1]
    kept = pl.ds(pl.multiple_of(256 * core, 256), 256)
    sent = pl.ds(pl.multiple_of(256 * (1 - core), 256), 256)
    for i in range(4):
        keep[:, 128 * i : 128 * i + 128] = field[i, kept, :]
        send[:, 128 * i : 128 * i + 128] = field[i, sent, :].astype(BF)
    tail = jnp.concatenate([pieces_in_rows(to_row(squares))] * 32, axis=0)
    keep[:, 512:640] = tail
    send[:, 512:640] = tail.astype(BF)


def start_kernel(places, left, right, observations, keep, send, field, slots):
    total = jnp.zeros((64, 128), F32)
    for j, pair in enumerate(ORDER):
        values = observations[pair]
        wide = values.astype(F32)
        wide = wide * wide
        total = total + sum(wide[:, 128 * i : 128 * i + 128] for i in range(8))
        slots[j] = dot_nt(values, left[pair]).astype(BF)
    coeffs = lambda t: jnp.concatenate(
        [slots[j][:, 32 * t : 32 * t + 32] for j in range(10)], axis=1
    )
    write_partial(places, coeffs, right, lane_sum(total), keep, send, field)


def back_kernel(places, right, own, one, two, three, keep, send, field, slots):
    here = places[0]
    squares = jnp.zeros((64, 1), F32)
    for step, chunk in enumerate((own, one, two, three)):
        at = 3 * lax.rem(here + step, 4)
        for i in range(3):
            slots[at + i] = chunk[i]
        squares = squares + lane_sum(chunk[3].astype(F32))
    coeffs = lambda t: jnp.concatenate(
        [slots[j][:, 32 * t : 32 * t + 32] for j in range(10)], axis=1
    )
    write_partial(places, coeffs, right, squares, keep, send, field)


def core_kernel(places, keep, got, out):
    both = keep[...] + got[...].astype(F32)
    out[:, 0:512] = both[:, 0:512].astype(BF)
    tail = pieces_in_rows(jnp.sum(both[0:8, 512:640], axis=0, keepdims=True))
    out[:, 512:640] = jnp.concatenate([tail] * 32, axis=0).astype(BF)


def shard_kernel(first, places, got, *refs):
    previous, model_len = (None, None) if first else refs[:2]
    raw, data_len, send = refs[0 if first else 2 :][:3]
    total = jnp.sum(got[...].astype(F32).reshape(32, 8, 640), axis=0)
    squares = jnp.sum(total[:, 512:640], axis=0, keepdims=True)
    data_len[...] = jnp.broadcast_to(
        to_column(jnp.sqrt(squares + EPSILON)), (64, 128)
    )
    row = places[2]
    length = data_len[pl.ds(row, 1), 0:1]
    value = total[:, 0:512] / length
    if not first:
        value = value - (length / model_len[pl.ds(row, 1), 0:1]) * previous[...]
    raw[...] = value
    send[...] = jnp.concatenate([value] * 32, axis=0).astype(BF)


def read_model(places, mine, other, model, field):
    core = places[1]
    here = pl.ds(pl.multiple_of(256 * core, 256), 256)
    there = pl.ds(pl.multiple_of(256 * (1 - core), 256), 256)
    for i in range(4):
        field[i, here, :] = mine[:, 128 * i : 128 * i + 128].astype(F32)
        field[i, there, :] = other[:, 128 * i : 128 * i + 128].astype(F32)
    total = jnp.zeros((64, 128), F32)
    for at in range(32):
        value = field[at % 4, pl.ds(at // 4, 64, stride=8), :]
        model[:, 128 * at : 128 * at + 128] = value.astype(BF)
        total = total + value * value
    return lane_sum(total)


def forward_kernel(places, mine, other, right, model, own, one, two, three, field, slots):
    squares = read_model(places, mine, other, model, field)
    for t in range(4):
        factors = jnp.concatenate([right[pair, t] for pair in ORDER], axis=0)
        value = dot_nt(model[:, 1024 * t : 1024 * t + 1024], factors).astype(BF)
        for j in range(10):
            slots[j, :, 32 * t : 32 * t + 32] = value[:, 32 * j : 32 * j + 32]
    for j in (10, 11):
        slots[j] = jnp.zeros((64, 128), BF)
    tail = pieces_in_lanes(squares).astype(BF)
    here = places[0]
    for step, chunk in enumerate((own, one, two, three)):
        at = 3 * lax.rem(here + step, 4)
        for i in range(3):
            chunk[i] = slots[at + i]
        chunk[3] = tail


def data_kernel(last, places, *refs):
    coeffs, left, (field, data_len), refs = refs[:4], refs[4:8], refs[8:10], refs[10:]
    model_len, outs = refs[0], refs[1:5]
    squares = sum(lane_sum(chunk[3].astype(F32)) for chunk in coeffs)
    length = jnp.sqrt(squares + EPSILON)
    model_len[...] = jnp.broadcast_to(length, (64, 128))
    inverse = 1.0 / length
    ratio = length / data_len[:, 0:1]
    total = jnp.zeros((64, 128), F32)
    for i in range(3):
        factors = jnp.concatenate([block[2 - i] for block in left], axis=0)
        value = dot(jnp.concatenate([chunk[i] for chunk in coeffs], axis=1), factors)
        value = value * inverse - ratio * field[i]
        if not last:
            refs[5][i] = value
        back = dot_nt(value.astype(BF), factors).astype(BF)
        for step in range(4):
            outs[step][i] = back[:, 128 * step : 128 * step + 128]
        value = value * value
        total = total + sum(value[:, 128 * k : 128 * k + 128] for k in range(8))
    tail = pieces_in_lanes(lane_sum(total)).astype(BF)
    for step in range(4):
        outs[step][3] = tail


def last_model_kernel(places, mine, other, model, squares, field):
    squares[...] = jnp.broadcast_to(
        read_model(places, mine, other, model, field), (64, 128)
    )


def scalars(data_lens, model_lens):
    diagonal_bar, residual = model_lens[0], data_lens[0]
    out = []
    for sweep in range(ITERS):
        data_len = data_lens[sweep + 1]
        rotation = jnp.sqrt(diagonal_bar * diagonal_bar + data_len * data_len)
        cosine_term = diagonal_bar / rotation
        sine_term = data_len / rotation
        into_solution = (cosine_term * residual) / rotation
        residual = sine_term * residual
        into_direction = None
        if sweep + 1 < len(model_lens):
            into_direction = (sine_term * model_lens[sweep + 1]) / rotation
            diagonal_bar = -cosine_term * model_lens[sweep + 1]
        out.append((into_solution, into_direction))
    return out, residual


def solution_kernel(places, *refs):
    data_lens, model_lens, (first, second) = refs[:3], refs[3:5], refs[5:7]
    solved, residual_estimate, last_direction = refs[7:]
    model_lens = [ref[:, 0:1] for ref in model_lens]
    steps, residual = scalars([ref[:, 0:1] for ref in data_lens], model_lens)
    residual_estimate[...] = jnp.broadcast_to(residual, (64, 128))
    for t in range(4):
        part = slice(1024 * t, 1024 * t + 1024)
        direction = first[:, part].astype(F32) / model_lens[0]
        value = steps[0][0] * direction
        direction = second[:, part].astype(F32) / model_lens[1] - steps[0][1] * direction
        solved[t] = value + steps[1][0] * direction
        last_direction[t] = direction


def direction_kernel(places, *refs):
    data_lens, model_lens, squares, (third, last_direction, out) = (
        refs[:3],
        refs[3:5],
        refs[5:9],
        refs[9:],
    )
    length = jnp.sqrt(sum(ref[:, 0:1] for ref in squares) + EPSILON)
    model_lens = [ref[:, 0:1] for ref in model_lens] + [length]
    steps, residual = scalars([ref[:, 0:1] for ref in data_lens], model_lens)
    for t in range(4):
        model = third[:, 1024 * t : 1024 * t + 1024].astype(F32) / length
        out[t] = model - steps[1][1] * last_direction[t]


def shift(value, step):
    return lax.ppermute(value, "x", [(i, (i + step) % 4) for i in range(4)])


def swap_core(value):
    return lax.ppermute(value, "c", [(0, 1), (1, 0)])


def exchange(value):
    width = value.shape[1]
    value = lax.all_to_all(
        value.reshape(32, 8, width), ("z", "y"), split_axis=0, concat_axis=0, tiled=True
    )
    return value.reshape(256, width)


PARTIAL = [((256, 640), F32), ((256, 640), BF)]
PARTIAL_SCRATCH = [((4, 512, 128), F32), ((12, 64, 128), BF)]
CHUNKS = [((4, 64, 128), BF)] * 4
COLUMN = ((64, 128), F32)
MODEL = ((64, 4096), BF)


def on_device(left, right, observations):
    here = lax.axis_index("x")
    core = lax.axis_index("c")
    row = 32 * core + 4 * lax.axis_index("z") + lax.axis_index("y")
    places = jnp.stack([here, core, row]).astype(jnp.int32)
    left = left.reshape(10, 128, 1024)
    right = right.reshape(10, 4, 32, 1024)
    observations = observations.reshape(10, 64, 1024)
    own_first = lambda device: jnp.minimum(3 * device, 7)
    owned = []
    for step in range(4):
        block = lax.dynamic_slice_in_dim(left, own_first((here + step) % 4), 3, 0)
        owned.append(block if step == 0 else shift(block, step))
    field = lax.dynamic_slice_in_dim(observations, own_first(here), 3, 0)[::-1]
    valid = (here < 3) | (jnp.arange(3) == 0)
    field = jnp.where(valid[:, None, None], field.astype(F32), 0.0)

    def sum_dp(keep, send, first, *extra):
        whole = call(core_kernel, [((256, 640), BF)], name="core_sum")(
            places, keep, swap_core(send)
        )[0]
        raw, data_len, send = call(
            functools.partial(shard_kernel, first),
            [((8, 512), F32), COLUMN, ((256, 512), BF)],
            name="shard",
        )(places, exchange(whole), *extra)
        mine = exchange(send)
        return raw, data_len, mine, swap_core(mine)

    keep, send = call(start_kernel, PARTIAL, PARTIAL_SCRATCH, name="start")(
        places, left, right, observations
    )
    raw, data_len, mine, other = sum_dp(keep, send, True)
    models, model_lens, data_lens = [], [], [data_len]
    for sweep in range(ITERS):
        model, *chunks = call(
            forward_kernel,
            [MODEL] + CHUNKS,
            [((4, 512, 128), F32), ((12, 64, 128), BF)],
            name="forward",
        )(places, mine, other, right)
        models.append(model)
        chunks = [chunks[0]] + [shift(chunks[step], step) for step in (1, 2, 3)]
        last = sweep == ITERS - 1
        outs = call(
            functools.partial(data_kernel, last),
            [COLUMN] + CHUNKS + ([] if last else [((3, 64, 1024), F32)]),
            name="data",
        )(places, *chunks, *owned, field, data_lens[-1])
        model_lens.append(outs[0])
        field = None if last else outs[5]
        chunks = [outs[1]] + [shift(outs[1 + step], -step) for step in (1, 2, 3)]
        keep, send = call(back_kernel, PARTIAL, PARTIAL_SCRATCH, name="back")(
            places, right, *chunks
        )
        raw, data_len, mine, other = sum_dp(keep, send, False, raw, model_lens[-1])
        data_lens.append(data_len)

    model, squares = call(
        last_model_kernel, [MODEL, COLUMN], [((4, 512, 128), F32)], name="last_model"
    )(places, mine, other)
    squares = [squares] + [shift(squares, step) for step in (1, 2, 3)]
    solved, residual, last_direction = call(
        solution_kernel,
        [((4, 64, 1024), F32), COLUMN, ((4, 64, 1024), F32)],
        name="solve",
    )(places, *data_lens, *model_lens, *models)
    direction = call(direction_kernel, [((4, 64, 1024), F32)], name="direct")(
        places, *data_lens, *model_lens, *squares, model, last_direction
    )[0]
    return solved, direction, residual[:, 0]


def solution(mesh):
    fine = Mesh(mesh.devices.reshape(8, 4, 2, 4), ("z", "y", "c", "x"))
    rows = ("z", "y", "c")
    return jax.shard_map(
        on_device,
        mesh=fine,
        in_specs=(
            P(rows, None, "x", None, None),
            P(rows, None, "x", None, None),
            P(rows, None, None, None),
        ),
        out_specs=(P("x", None, None), P("x", None, None), P()),
        check_vma=False,
    )
```

time: 1050 us -> 214 us (0.20)
  waiting for transfers between devices: 680 us -> 51.3 us
  blocking collectives: 305 us -> 67.7 us
  starting transfers between devices: 0.29 us -> 56.3 us
  Pallas kernels: 0 us -> 26.2 us
  other arithmetic: 24.5 us -> 0.23 us
  matrix products: 21.6 us -> 0 us
  between operations: 14.2 us -> 0.87 us
  local copies, waits for them, and re-layouts: 0.01 us -> 10.6 us
    psum x3 -> x0, waiting for transfers between devices: 555 us -> none  [model_normalize(): total = lax.psum(partial_value, 'dp')]
    psum x6 -> x0, blocking collectives: 305 us -> none  [the longest x2 152 us: on_device(): lax.psum(jnp.sum(data_raw * data_raw, axis=(0, 1, 3)), ('dp', 'mp'))]
    reduce_scatter x2 -> x0, waiting for transfers between devices: 71.3 us -> none  [on_device(): lax.psum_scatter(partial_value, 'mp', scatter_dimension=3, tiled=True)]
    all_to_all x0 -> x4, blocking collectives: none -> 67.7 us  [exchange(): lax.all_to_all(value.reshape(32, 8, width), ('z', 'y'), split_axis=0, con...]
    all_gather x2 -> x0, waiting for transfers between devices: 53.3 us -> none  [data_coeffs(): lax.all_gather(data_share.astype(jnp.bfloat16), 'mp', axis=3, tiled=True)]
    ppermute x0 -> x24, starting transfers between devices: none -> 41.9 us  [the longest x6 22.2 us: swap_core(): return lax.ppermute(value, 'c', [(0, 1), (1, 0)])]
    ppermute x0 -> x24, waiting for transfers between devices: none -> 37.3 us  [the longest x18 31.9 us: shift(): return lax.ppermute(value, 'x', [(i, (i + step) % 4) for i in range(4)])]
    pallas_call x0 -> x16, Pallas kernels: none -> 26.2 us  [run(): pl.pallas_call(kernel, out_shape=[jax.ShapeDtypeStruct(shape, dtype) for...]
  transfers between devices with their start and end apart: 7 -> 26, of which waited for: 7 -> 19; matrix products, arithmetic and copies ran while one was open for 0% -> 2% of each run, Pallas kernels for 0% -> 3%
where the time goes in v1:
time: 214 us; the launch traced here: 213 us
  blocking collectives  67.7 us (32%)
  starting transfers between devices  56.3 us (26%)
  waiting for transfers between devices  51.3 us (24%)
  Pallas kernels  26.2 us (12%)
  local copies, waits for them, and re-layouts  10.6 us (5%)
    all_to_all x4, blocking collectives, exchange(): lax.all_to_all(value.reshape(32, 8, width), ('z', 'y'), split_axis=0, con...  67.7 us
    ppermute x18, waiting for transfers between devices, shift(): return lax.ppermute(value, 'x', [(i, (i + step) % 4) for i in range(4)])  31.9 us
    pallas_call x16, Pallas kernels, run(): pl.pallas_call(kernel, out_shape=[jax.ShapeDtypeStruct(shape, dtype) for...  26.2 us
    ppermute x6, starting transfers between devices, swap_core(): return lax.ppermute(value, 'c', [(0, 1), (1, 0)])  22.2 us
    ppermute x18, starting transfers between devices, shift(): return lax.ppermute(value, 'x', [(i, (i + step) % 4) for i in range(4)])  19.7 us
    all_to_all x2, starting transfers between devices, exchange(): lax.all_to_all(value.reshape(32, 8, width), ('z', 'y'), split_axis=0, con...  14.5 us
    all_to_all x2, waiting for transfers between devices, exchange(): lax.all_to_all(value.reshape(32, 8, width), ('z', 'y'), split_axis=0, con...  13.9 us
    unnamed x10, local copies, waits for them, and re-layouts  5.49 us
  transfers between devices with their start and end apart: 26, of which 19 were waited for; matrix products, arithmetic and copies ran while one was open for 2% of the time, Pallas kernels for 3%

profile of v1, /device:TPU:1, one launch (start us, length us, event | category | flops | bytes accessed | tf_op | source)
XLA Modules:
  0.0 213.2 jit_solution(12643840439938193629)
XLA Ops:
  0.7 1.7 copy-done
  2.5 1.7 copy-done.2
  4.2 1.3 copy-done.3
  5.5 2.4 %start.1 = (f32[256,640]{1,0:T(8,128)S(1)}, bf16[256,640]{1,0:T(8,128)(2,1)S(1)}) custom-call(s32[3]{0:T(128)S(1)} %pad_add_fusion.places, bf16[10,128,1024]{2,1,0:T(8,128)(2,1)S(1)} %bitcast.24, bf16[10,4,32,1024]{3,2,1,0:T(8,128)(2,1)S(1)} %bitcast.18, bf16[10,64,1024]{2,1,0:T(8,128)(2,1)S(1)} %bitcast.26), custom_call_target="tpu_custom_call" | custom-call | tf_op jit(solution)/shard_map/start/pallas_call | solution.py:21
  7.9 3.3 %collective-permute-start = (bf16[256,640]{1,0:T(8,128)(2,1)S(1)}, bf16[256,640]{1,0:T(8,128)(2,1)S(1)}, u32[]{:S(2)}, u32[]{:S(2)}) collective-permute-start(bf16[256,640]{1,0:T(8,128)(2,1)S(1)} %get-tuple-element.44), channel_id=1, source_target_pairs={{0,4},{4,0},{1,5},{5,1},{2,6},{6,2},{3,7},{7,3},{8,12},{12,8},{9,1... | collective-permute-start | bytes 983048 | tf_op jit(solution)/shard_map/ppermute | solution.py:274
  11.3 1.3 collective-permute-done.got
  12.5 1.3 core_sum.3
  13.9 9.6 %all-to-all-start = ((bf16[32,8,640]{2,1,0:T(8,128)(2,1)}), bf16[32,8,640]{2,1,0:T(8,128)(2,1)}, u32[]{:S(2)}, u32[]{:S(2)}) async-start(bf16[32,8,640]{2,1,0:T(8,128)(2,1)} %bitcast.6), calls=%async_computation | async-start | bytes 655360 | tf_op jit(solution)/shard_map/all_to_all | solution.py:279
  23.5 3.5 %constant_dynamic-slice_fusion.1 = (bf16[3,128,1024]{2,1,0:T(8,128)(2,1)}, bf16[3,128,1024]{2,1,0:T(8,128)(2,1)}, bf16[3,128,1024]{2,1,0:T(8,128)(2,1)}, bf16[3,128,1024]{2,1,0:T(8,128)(2,1)S(1)}) fusion(bf16[10,128,1024]{2,1,0:T(8,128)(2,1)} %bitcast.23, s32[]{:T(128)S(6)} %select_n.45, s32[]{:T(128)S(6)} %select_n.43, s32[]{:T(128)S(6)} %select_n.41, ...), kind=kLoop, calls=%fused_computation.4 | loop fusion | bytes 6291472 | tf_op jit(solution)/shard_map/dynamic_slice | solution.py:303
  27.0 2.5 %collective-permute-start.7 = (bf16[3,128,1024]{2,1,0:T(8,128)(2,1)}, bf16[3,128,1024]{2,1,0:T(8,128)(2,1)}, u32[]{:S(2)}, u32[]{:S(2)}) collective-permute-start(bf16[3,128,1024]{2,1,0:T(8,128)(2,1)} %get-tuple-element.83), channel_id=1, source_target_pairs={{0,3},{1,0},{2,1},{3,2},{4,7},{5,4},{6,5},{7,6},{8,11},{9,8},{10,9... | collective-permute-start | bytes 2359304 | tf_op jit(solution)/shard_map/ppermute | solution.py:270
  29.5 6.7 %all-to-all-done = bf16[32,8,640]{2,1,0:T(8,128)(2,1)} async-done(((bf16[32,8,640]{2,1,0:T(8,128)(2,1)}), bf16[32,8,640]{2,1,0:T(8,128)(2,1)}, u32[]{:S(2)}, u32[]{:S(2)}) %all-to-all-start) | async-done | bytes 327712 | tf_op jit(solution)/shard_map/all_to_all | solution.py:279
  36.2 1.2 shard.3
  37.4 0.7 copy-done.4
  38.1 4.9 %all-to-all-start.1 = ((bf16[32,8,512]{2,1,0:T(8,128)(2,1)}), bf16[32,8,512]{2,1,0:T(8,128)(2,1)}, u32[]{:S(2)}, u32[]{:S(2)}) async-start(bf16[32,8,512]{2,1,0:T(8,128)(2,1)} %bitcast.35), calls=%async_computation.1 | async-start | bytes 524288 | tf_op jit(solution)/shard_map/all_to_all | solution.py:279
  43.0 2.8 %collective-permute-start.6 = (bf16[3,128,1024]{2,1,0:T(8,128)(2,1)}, bf16[3,128,1024]{2,1,0:T(8,128)(2,1)}, u32[]{:S(2)}, u32[]{:S(2)}) collective-permute-start(bf16[3,128,1024]{2,1,0:T(8,128)(2,1)} %get-tuple-element.84), channel_id=1, source_target_pairs={{0,2},{1,3},{2,0},{3,1},{4,6},{5,7},{6,4},{7,5},{8,10},{9,11},{10,... | collective-permute-start | bytes 2359304 | tf_op jit(solution)/shard_map/ppermute | solution.py:270
  46.1 7.2 %all-to-all-done.1 = bf16[32,8,512]{2,1,0:T(8,128)(2,1)} async-done(((bf16[32,8,512]{2,1,0:T(8,128)(2,1)}), bf16[32,8,512]{2,1,0:T(8,128)(2,1)}, u32[]{:S(2)}, u32[]{:S(2)}) %all-to-all-start.1) | async-done | bytes 262176 | tf_op jit(solution)/shard_map/all_to_all | solution.py:279
  53.3 3.8 %collective-permute-start.1 = (bf16[256,512]{1,0:T(8,128)(2,1)}, bf16[256,512]{1,0:T(8,128)(2,1)}, u32[]{:S(2)}, u32[]{:S(2)}) collective-permute-start(bf16[256,512]{1,0:T(8,128)(2,1)} %bitcast.9.mine), channel_id=1, source_target_pairs={{0,4},{4,0},{1,5},{5,1},{2,6},{6,2},{3,7},{7,3},{8,12},{12,8},{9,1... | collective-permute-start | bytes 786440 | tf_op jit(solution)/shard_map/ppermute | solution.py:274
  57.1 1.0 constant_dynamic-slice_fusion
  58.6 2.3 %forward.2 = (bf16[64,4096]{1,0:T(8,128)(2,1)S(1)}, bf16[4,64,128]{2,1,0:T(8,128)(2,1)S(1)}, bf16[4,64,128]{2,1,0:T(8,128)(2,1)S(1)}, bf16[4,64,128]{2,1,0:T(8,128)(2,1)S(1)}, bf16[4,64,128]{2,1,0:T(8,128)(2,1)S(1)}) custom-call(s32[3]{0:T(128)S(1)} %pad_add_fusion.places, bf16[256,512]{1,0:T(8,128)(2,1)} %bitcast.9.mine, ...), custom_call_target="tpu_custom_call" | custom-call | tf_op jit(solution)/shard_map/forward/pallas_call | solution.py:21
  60.9 1.3 collective-permute-start.2
  62.2 2.5 %collective-permute-start.3 = (bf16[4,64,128]{2,1,0:T(8,128)(2,1)S(1)}, bf16[4,64,128]{2,1,0:T(8,128)(2,1)S(1)}, u32[]{:S(2)}, u32[]{:S(2)}) collective-permute-start(bf16[4,64,128]{2,1,0:T(8,128)(2,1)S(1)} %get-tuple-element.49), channel_id=1, source_target_pairs={{0,2},{1,3},{2,0},{3,1},{4,6},{5,7},{6,4},{7,5},{8,10},{9,11},{10,... | collective-permute-start | bytes 196616 | tf_op jit(solution)/shard_map/ppermute | solution.py:270
  64.6 1.2 collective-permute-start.4
  65.9 16.0 %collective-permute-done.5.refs_5_ = bf16[3,128,1024]{2,1,0:T(8,128)(2,1)} collective-permute-done((bf16[3,128,1024]{2,1,0:T(8,128)(2,1)}, bf16[3,128,1024]{2,1,0:T(8,128)(2,1)}, u32[]{:S(2)}, u32[]{:S(2)}) %collective-permute-start.5) | collective-permute-done | bytes 786464 | tf_op jit(solution)/shard_map/ppermute | solution.py:270
  81.9 1.3 collective-permute-done.2.refs_1_
  83.2 3.3 %data.2 = (f32[64,128]{1,0:T(8,128)S(1)}, bf16[4,64,128]{2,1,0:T(8,128)(2,1)S(1)}, bf16[4,64,128]{2,1,0:T(8,128)(2,1)S(1)}, bf16[4,64,128]{2,1,0:T(8,128)(2,1)S(...) custom-call(s32[3]{0:T(128)S(1)} %pad_add_fusion.places, ...), custom_call_target="tpu_custom_call" | custom-call | tf_op jit(solution)/shard_map/data/pallas_call | solution.py:21
  86.6 1.1 collective-permute-start.9
  87.6 0.8 collective-permute-start.10
  88.4 1.3 collective-permute-done.8.one
  89.7 1.6 collective-permute-done.9.two
  91.3 0.8 collective-permute-done.10.three
  92.1 1.4 back.2
  93.5 4.4 %collective-permute-start.11 = (bf16[256,640]{1,0:T(8,128)(2,1)S(1)}, bf16[256,640]{1,0:T(8,128)(2,1)S(1)}, u32[]{:S(2)}, u32[]{:S(2)}) collective-permute-start(bf16[256,640]{1,0:T(8,128)(2,1)S(1)} %get-tuple-element.56), channel_id=1, source_target_pairs={{0,4},{4,0},{1,5},{5,1},{2,6},{6,2},{3,7},{7,3},{8,12},{12,8},{9,1... | collective-permute-start | bytes 983048 | tf_op jit(solution)/shard_map/ppermute | solution.py:274
  97.9 1.3 collective-permute-done.11.got
  99.2 0.6 core_sum.4
  99.8 21.7 %all_to_all.30 = bf16[32,8,640]{2,1,0:T(8,128)(2,1)S(1)} all-to-all(bf16[32,8,640]{2,1,0:T(8,128)(2,1)S(1)} %bitcast.29), channel_id=1, replica_groups=mesh['z'=8,'y'=4,'c'=2,'x'=4] {'z','y'}, dimensions={0} | all-to-all | bytes 655360 | tf_op jit(solution)/shard_map/all_to_all | solution.py:279
  121.5 0.7 shard.4
  122.2 15.0 %all_to_all.31 = bf16[32,8,512]{2,1,0:T(8,128)(2,1)S(1)} all-to-all(bf16[32,8,512]{2,1,0:T(8,128)(2,1)S(1)} %bitcast.36), channel_id=1, replica_groups=mesh['z'=8,'y'=4,'c'=2,'x'=4] {'z','y'}, dimensions={0} | all-to-all | bytes 524288 | tf_op jit(solution)/shard_map/all_to_all | solution.py:279
  137.2 3.5 %collective-permute-start.12 = (bf16[256,512]{1,0:T(8,128)(2,1)S(1)}, bf16[256,512]{1,0:T(8,128)(2,1)S(1)}, u32[]{:S(2)}, u32[]{:S(2)}) collective-permute-start(bf16[256,512]{1,0:T(8,128)(2,1)S(1)} %bitcast.33), channel_id=1, source_target_pairs={{0,4},{4,0},{1,5},{5,1},{2,6},{6,2},{3,7},{7,3},{8,12},{12,8},{9,1... | collective-permute-start | bytes 786440 | tf_op jit(solution)/shard_map/ppermute | solution.py:274
  140.7 1.2 collective-permute-done.12.other
  141.9 1.8 forward.3
  143.8 1.6 collective-permute-start.14
  145.4 1.0 collective-permute-start.15
  146.4 3.5 %collective-permute-done.13.refs_1_ = bf16[4,64,128]{2,1,0:T(8,128)(2,1)S(1)} collective-permute-done((bf16[4,64,128]{2,1,0:T(8,128)(2,1)S(1)}, bf16[4,64,128]{2,1,0:T(8,128)(2,1)S(1)}, u32[]{:S(2)}, u32[]{:S(2)}) %collective-permute-start.13) | collective-permute-done | bytes 65568 | tf_op jit(solution)/shard_map/ppermute | solution.py:270
  150.0 3.3 %data.3 = (f32[64,128]{1,0:T(8,128)S(1)}, bf16[4,64,128]{2,1,0:T(8,128)(2,1)S(1)}, bf16[4,64,128]{2,1,0:T(8,128)(2,1)S(1)}, bf16[4,64,128]{2,1,0:T(8,128)(2,1)S(1)}, bf16[4,64,128]{2,1,0:T(8,128)(2,1)S(1)}) custom-call(s32[3]{0:T(128)S(1)} %pad_add_fusion.places, bf16[4,64,128]{2,1,0:T(8,128)(2,1)S(1)} %get-tuple-element.61.refs_0_, ...), custom_call_target="tpu_custom_call" | custom-call | tf_op jit(solution)/shard_map/data/pallas_call | solution.py:21
  153.3 1.6 collective-permute-start.16
  154.8 1.0 collective-permute-start.17
  155.8 0.7 collective-permute-done.16.one
  156.5 3.0 %collective-permute-done.17.two = bf16[4,64,128]{2,1,0:T(8,128)(2,1)S(1)} collective-permute-done((bf16[4,64,128]{2,1,0:T(8,128)(2,1)S(1)}, bf16[4,64,128]{2,1,0:T(8,128)(2,1)S(1)}, u32[]{:S(2)}, u32[]{:S(2)}) %collective-permute-start.17) | collective-permute-done | bytes 65568 | tf_op jit(solution)/shard_map/ppermute | solution.py:270
  159.4 0.7 collective-permute-done.18.three
  160.1 1.4 back.3
  161.6 3.6 %collective-permute-start.19 = (bf16[256,640]{1,0:T(8,128)(2,1)S(1)}, bf16[256,640]{1,0:T(8,128)(2,1)S(1)}, u32[]{:S(2)}, u32[]{:S(2)}) collective-permute-start(bf16[256,640]{1,0:T(8,128)(2,1)S(1)} %get-tuple-element.71), channel_id=1, source_target_pairs={{0,4},{4,0},{1,5},{5,1},{2,6},{6,2},{3,7},{7,3},{8,12},{12,8},{9,1... | collective-permute-start | bytes 983048 | tf_op jit(solution)/shard_map/ppermute | solution.py:274
  165.2 1.3 collective-permute-done.19.got
  167.0 16.0 %all_to_all.32 = bf16[32,8,640]{2,1,0:T(8,128)(2,1)S(1)} all-to-all(bf16[32,8,640]{2,1,0:T(8,128)(2,1)S(1)} %bitcast.30), channel_id=1, replica_groups=mesh['z'=8,'y'=4,'c'=2,'x'=4] {'z','y'}, dimensions={0} | all-to-all | bytes 655360 | tf_op jit(solution)/shard_map/all_to_all | solution.py:279
  183.1 1.3 shard.5
  184.4 15.0 %all_to_all.33 = bf16[32,8,512]{2,1,0:T(8,128)(2,1)S(1)} all-to-all(bf16[32,8,512]{2,1,0:T(8,128)(2,1)S(1)} %bitcast.37), channel_id=1, replica_groups=mesh['z'=8,'y'=4,'c'=2,'x'=4] {'z','y'}, dimensions={0} | all-to-all | bytes 524288 | tf_op jit(solution)/shard_map/all_to_all | solution.py:279
  199.4 3.5 %collective-permute-start.20 = (bf16[256,512]{1,0:T(8,128)(2,1)S(1)}, bf16[256,512]{1,0:T(8,128)(2,1)S(1)}, u32[]{:S(2)}, u32[]{:S(2)}) collective-permute-start(bf16[256,512]{1,0:T(8,128)(2,1)S(1)} %bitcast.31), channel_id=1, source_target_pairs={{0,4},{4,0},{1,5},{5,1},{2,6},{6,2},{3,7},{7,3},{8,12},{12,8},{9,1... | collective-permute-start | bytes 786440 | tf_op jit(solution)/shard_map/ppermute | solution.py:274
  202.9 2.0 solve.1
  204.9 0.9 last_model.1
  206.1 0.9 collective-permute-start.22
  207.0 0.8 collective-permute-start.21
  207.8 0.6 slice_reduce_fusion
  208.6 1.8 collective-permute-done.22.refs_7_
  210.4 1.0 collective-permute-done.21.refs_6_
  211.4 1.8 direct.1
  (24 shorter events, 2.4 us)
Async XLA Ops:
  0.7 1.7 copy-start
  2.5 1.7 copy-start.2
  4.2 1.3 copy-start.3
  7.9 4.6 %collective-permute-start = (bf16[256,640]{1,0:T(8,128)(2,1)S(1)}, bf16[256,640]{1,0:T(8,128)(2,1)S(1)}, u32[]{:S(2)}, u32[]{:S(2)}) collective-permute-start(bf16[256,640]{1,0:T(8,128)(2,1)S(1)} %get-tuple-element.44), channel_id=1, source_target_pairs={{0,4},{4,0},{1,5},{5,1},{2,6},{6,2},{3,7},{7,3},{8,12},{12,8},{9,1... | collective-permute-start | bytes 983048 | tf_op jit(solution)/shard_map/ppermute | solution.py:274
  13.9 22.3 %all-to-all-start = ((bf16[32,8,640]{2,1,0:T(8,128)(2,1)}), bf16[32,8,640]{2,1,0:T(8,128)(2,1)}, u32[]{:S(2)}, u32[]{:S(2)}) async-start(bf16[32,8,640]{2,1,0:T(8,128)(2,1)} %bitcast.6), calls=%async_computation | async-start | bytes 655360 | tf_op jit(solution)/shard_map/all_to_all | solution.py:279
  23.5 35.1 %copy-start.1 = (bf16[2,5,4,32,1024]{4,3,2,1,0:T(8,128)(2,1)S(1)}, bf16[2,5,4,32,1024]{4,3,2,1,0:T(8,128)(2,1)}, u32[]{:S(2)}) copy-start(bf16[2,5,4,32,1024]{4,3,2,1,0:T(8,128)(2,1)} %param.4) | copy-start | bytes 7864324
  27.0 37.6 %collective-permute-start.7 = (bf16[3,128,1024]{2,1,0:T(8,128)(2,1)}, bf16[3,128,1024]{2,1,0:T(8,128)(2,1)}, u32[]{:S(2)}, u32[]{:S(2)}) collective-permute-start(bf16[3,128,1024]{2,1,0:T(8,128)(2,1)} %get-tuple-element.83), channel_id=1, source_target_pairs={{0,3},{1,0},{2,1},{3,2},{4,7},{5,4},{6,5},{7,6},{8,11},{9,8},{10,9... | collective-permute-start | bytes 2359304 | tf_op jit(solution)/shard_map/ppermute | solution.py:270
  37.4 0.7 copy-start.4
  38.1 15.3 %all-to-all-start.1 = ((bf16[32,8,512]{2,1,0:T(8,128)(2,1)}), bf16[32,8,512]{2,1,0:T(8,128)(2,1)}, u32[]{:S(2)}, u32[]{:S(2)}) async-start(bf16[32,8,512]{2,1,0:T(8,128)(2,1)} %bitcast.35), calls=%async_computation.1 | async-start | bytes 524288 | tf_op jit(solution)/shard_map/all_to_all | solution.py:279
  43.0 23.0 %collective-permute-start.6 = (bf16[3,128,1024]{2,1,0:T(8,128)(2,1)}, bf16[3,128,1024]{2,1,0:T(8,128)(2,1)}, u32[]{:S(2)}, u32[]{:S(2)}) collective-permute-start(bf16[3,128,1024]{2,1,0:T(8,128)(2,1)} %get-tuple-element.84), channel_id=1, source_target_pairs={{0,2},{1,3},{2,0},{3,1},{4,6},{5,7},{6,4},{7,5},{8,10},{9,11},{10,... | collective-permute-start | bytes 2359304 | tf_op jit(solution)/shard_map/ppermute | solution.py:270
  45.8 36.1 %collective-permute-start.5 = (bf16[3,128,1024]{2,1,0:T(8,128)(2,1)}, bf16[3,128,1024]{2,1,0:T(8,128)(2,1)}, u32[]{:S(2)}, u32[]{:S(2)}) collective-permute-start(bf16[3,128,1024]{2,1,0:T(8,128)(2,1)} %get-tuple-element.85), channel_id=1, source_target_pairs={{0,1},{1,2},{2,3},{3,0},{4,5},{5,6},{6,7},{7,4},{8,9},{9,10},{10,1... | collective-permute-start | bytes 2359304 | tf_op jit(solution)/shard_map/ppermute | solution.py:270
  53.3 5.3 %collective-permute-start.1 = (bf16[256,512]{1,0:T(8,128)(2,1)}, bf16[256,512]{1,0:T(8,128)(2,1)}, u32[]{:S(2)}, u32[]{:S(2)}) collective-permute-start(bf16[256,512]{1,0:T(8,128)(2,1)} %bitcast.9.mine), channel_id=1, source_target_pairs={{0,4},{4,0},{1,5},{5,1},{2,6},{6,2},{3,7},{7,3},{8,12},{12,8},{9,1... | collective-permute-start | bytes 786440 | tf_op jit(solution)/shard_map/ppermute | solution.py:274
  60.9 22.3 %collective-permute-start.2 = (bf16[4,64,128]{2,1,0:T(8,128)(2,1)S(1)}, bf16[4,64,128]{2,1,0:T(8,128)(2,1)S(1)}, u32[]{:S(2)}, u32[]{:S(2)}) collective-permute-start(bf16[4,64,128]{2,1,0:T(8,128)(2,1)S(1)} %get-tuple-element.48), channel_id=1, source_target_pairs={{0,1},{1,2},{2,3},{3,0},{4,5},{5,6},{6,7},{7,4},{8,9},{9,10},{10,1... | collective-permute-start | bytes 196616 | tf_op jit(solution)/shard_map/ppermute | solution.py:270
  62.2 21.0 %collective-permute-start.3 = (bf16[4,64,128]{2,1,0:T(8,128)(2,1)S(1)}, bf16[4,64,128]{2,1,0:T(8,128)(2,1)S(1)}, u32[]{:S(2)}, u32[]{:S(2)}) collective-permute-start(bf16[4,64,128]{2,1,0:T(8,128)(2,1)S(1)} %get-tuple-element.49), channel_id=1, source_target_pairs={{0,2},{1,3},{2,0},{3,1},{4,6},{5,7},{6,4},{7,5},{8,10},{9,11},{10,... | collective-permute-start | bytes 196616 | tf_op jit(solution)/shard_map/ppermute | solution.py:270
  64.6 18.6 %collective-permute-start.4 = (bf16[4,64,128]{2,1,0:T(8,128)(2,1)S(1)}, bf16[4,64,128]{2,1,0:T(8,128)(2,1)S(1)}, u32[]{:S(2)}, u32[]{:S(2)}) collective-permute-start(bf16[4,64,128]{2,1,0:T(8,128)(2,1)S(1)} %get-tuple-element.50), channel_id=1, source_target_pairs={{0,3},{1,0},{2,1},{3,2},{4,7},{5,4},{6,5},{7,6},{8,11},{9,8},{10,9... | collective-permute-start | bytes 196616 | tf_op jit(solution)/shard_map/ppermute | solution.py:270
  86.5 3.2 %collective-permute-start.8 = (bf16[4,64,128]{2,1,0:T(8,128)(2,1)S(1)}, bf16[4,64,128]{2,1,0:T(8,128)(2,1)S(1)}, u32[]{:S(2)}, u32[]{:S(2)}) collective-permute-start(bf16[4,64,128]{2,1,0:T(8,128)(2,1)S(1)} %get-tuple-element.52), channel_id=1, source_target_pairs={{0,3},{1,0},{2,1},{3,2},{4,7},{5,4},{6,5},{7,6},{8,11},{9,8},{10,9... | collective-permute-start | bytes 196616 | tf_op jit(solution)/shard_map/ppermute | solution.py:270
  86.6 4.7 %collective-permute-start.9 = (bf16[4,64,128]{2,1,0:T(8,128)(2,1)S(1)}, bf16[4,64,128]{2,1,0:T(8,128)(2,1)S(1)}, u32[]{:S(2)}, u32[]{:S(2)}) collective-permute-start(bf16[4,64,128]{2,1,0:T(8,128)(2,1)S(1)} %get-tuple-element.53), channel_id=1, source_target_pairs={{0,2},{1,3},{2,0},{3,1},{4,6},{5,7},{6,4},{7,5},{8,10},{9,11},{10,... | collective-permute-start | bytes 196616 | tf_op jit(solution)/shard_map/ppermute | solution.py:270
  87.6 4.4 %collective-permute-start.10 = (bf16[4,64,128]{2,1,0:T(8,128)(2,1)S(1)}, bf16[4,64,128]{2,1,0:T(8,128)(2,1)S(1)}, u32[]{:S(2)}, u32[]{:S(2)}) collective-permute-start(bf16[4,64,128]{2,1,0:T(8,128)(2,1)S(1)} %get-tuple-element.54), channel_id=1, source_target_pairs={{0,1},{1,2},{2,3},{3,0},{4,5},{5,6},{6,7},{7,4},{8,9},{9,10},{10,1... | collective-permute-start | bytes 196616 | tf_op jit(solution)/shard_map/ppermute | solution.py:270
  93.5 5.7 %collective-permute-start.11 = (bf16[256,640]{1,0:T(8,128)(2,1)S(1)}, bf16[256,640]{1,0:T(8,128)(2,1)S(1)}, u32[]{:S(2)}, u32[]{:S(2)}) collective-permute-start(bf16[256,640]{1,0:T(8,128)(2,1)S(1)} %get-tuple-element.56), channel_id=1, source_target_pairs={{0,4},{4,0},{1,5},{5,1},{2,6},{6,2},{3,7},{7,3},{8,12},{12,8},{9,1... | collective-permute-start | bytes 983048 | tf_op jit(solution)/shard_map/ppermute | solution.py:274
  137.2 4.7 %collective-permute-start.12 = (bf16[256,512]{1,0:T(8,128)(2,1)S(1)}, bf16[256,512]{1,0:T(8,128)(2,1)S(1)}, u32[]{:S(2)}, u32[]{:S(2)}) collective-permute-start(bf16[256,512]{1,0:T(8,128)(2,1)S(1)} %bitcast.33), channel_id=1, source_target_pairs={{0,4},{4,0},{1,5},{5,1},{2,6},{6,2},{3,7},{7,3},{8,12},{12,8},{9,1... | collective-permute-start | bytes 786440 | tf_op jit(solution)/shard_map/ppermute | solution.py:274
  143.7 6.3 %collective-permute-start.13 = (bf16[4,64,128]{2,1,0:T(8,128)(2,1)S(1)}, bf16[4,64,128]{2,1,0:T(8,128)(2,1)S(1)}, u32[]{:S(2)}, u32[]{:S(2)}) collective-permute-start(bf16[4,64,128]{2,1,0:T(8,128)(2,1)S(1)} %get-tuple-element.62), channel_id=1, source_target_pairs={{0,1},{1,2},{2,3},{3,0},{4,5},{5,6},{6,7},{7,4},{8,9},{9,10},{10,1... | collective-permute-start | bytes 196616 | tf_op jit(solution)/shard_map/ppermute | solution.py:270
  143.8 6.2 %collective-permute-start.14 = (bf16[4,64,128]{2,1,0:T(8,128)(2,1)S(1)}, bf16[4,64,128]{2,1,0:T(8,128)(2,1)S(1)}, u32[]{:S(2)}, u32[]{:S(2)}) collective-permute-start(bf16[4,64,128]{2,1,0:T(8,128)(2,1)S(1)} %get-tuple-element.63), channel_id=1, source_target_pairs={{0,2},{1,3},{2,0},{3,1},{4,6},{5,7},{6,4},{7,5},{8,10},{9,11},{10,... | collective-permute-start | bytes 196616 | tf_op jit(solution)/shard_map/ppermute | solution.py:270
  145.4 4.6 %collective-permute-start.15 = (bf16[4,64,128]{2,1,0:T(8,128)(2,1)S(1)}, bf16[4,64,128]{2,1,0:T(8,128)(2,1)S(1)}, u32[]{:S(2)}, u32[]{:S(2)}) collective-permute-start(bf16[4,64,128]{2,1,0:T(8,128)(2,1)S(1)} %get-tuple-element.64), channel_id=1, source_target_pairs={{0,3},{1,0},{2,1},{3,2},{4,7},{5,4},{6,5},{7,6},{8,11},{9,8},{10,9... | collective-permute-start | bytes 196616 | tf_op jit(solution)/shard_map/ppermute | solution.py:270
  153.3 3.2 %collective-permute-start.16 = (bf16[4,64,128]{2,1,0:T(8,128)(2,1)S(1)}, bf16[4,64,128]{2,1,0:T(8,128)(2,1)S(1)}, u32[]{:S(2)}, u32[]{:S(2)}) collective-permute-start(bf16[4,64,128]{2,1,0:T(8,128)(2,1)S(1)} %get-tuple-element.67), channel_id=1, source_target_pairs={{0,3},{1,0},{2,1},{3,2},{4,7},{5,4},{6,5},{7,6},{8,11},{9,8},{10,9... | collective-permute-start | bytes 196616 | tf_op jit(solution)/shard_map/ppermute | solution.py:270
  154.8 4.6 %collective-permute-start.17 = (bf16[4,64,128]{2,1,0:T(8,128)(2,1)S(1)}, bf16[4,64,128]{2,1,0:T(8,128)(2,1)S(1)}, u32[]{:S(2)}, u32[]{:S(2)}) collective-permute-start(bf16[4,64,128]{2,1,0:T(8,128)(2,1)S(1)} %get-tuple-element.68), channel_id=1, source_target_pairs={{0,2},{1,3},{2,0},{3,1},{4,6},{5,7},{6,4},{7,5},{8,10},{9,11},{10,... | collective-permute-start | bytes 196616 | tf_op jit(solution)/shard_map/ppermute | solution.py:270
  155.8 4.4 %collective-permute-start.18 = (bf16[4,64,128]{2,1,0:T(8,128)(2,1)S(1)}, bf16[4,64,128]{2,1,0:T(8,128)(2,1)S(1)}, u32[]{:S(2)}, u32[]{:S(2)}) collective-permute-start(bf16[4,64,128]{2,1,0:T(8,128)(2,1)S(1)} %get-tuple-element.69), channel_id=1, source_target_pairs={{0,1},{1,2},{2,3},{3,0},{4,5},{5,6},{6,7},{7,4},{8,9},{9,10},{10,1... | collective-permute-start | bytes 196616 | tf_op jit(solution)/shard_map/ppermute | solution.py:270
  161.6 4.9 %collective-permute-start.19 = (bf16[256,640]{1,0:T(8,128)(2,1)S(1)}, bf16[256,640]{1,0:T(8,128)(2,1)S(1)}, u32[]{:S(2)}, u32[]{:S(2)}) collective-permute-start(bf16[256,640]{1,0:T(8,128)(2,1)S(1)} %get-tuple-element.71), channel_id=1, source_target_pairs={{0,4},{4,0},{1,5},{5,1},{2,6},{6,2},{3,7},{7,3},{8,12},{12,8},{9,1... | collective-permute-start | bytes 983048 | tf_op jit(solution)/shard_map/ppermute | solution.py:274
  199.4 5.5 %collective-permute-start.20 = (bf16[256,512]{1,0:T(8,128)(2,1)S(1)}, bf16[256,512]{1,0:T(8,128)(2,1)S(1)}, u32[]{:S(2)}, u32[]{:S(2)}) collective-permute-start(bf16[256,512]{1,0:T(8,128)(2,1)S(1)} %bitcast.31), channel_id=1, source_target_pairs={{0,4},{4,0},{1,5},{5,1},{2,6},{6,2},{3,7},{7,3},{8,12},{12,8},{9,1... | collective-permute-start | bytes 786440 | tf_op jit(solution)/shard_map/ppermute | solution.py:274
  205.8 2.8 %collective-permute-start.23 = (f32[64,128]{1,0:T(8,128)S(1)}, f32[64,128]{1,0:T(8,128)S(1)}, u32[]{:S(2)}, u32[]{:S(2)}) collective-permute-start(f32[64,128]{1,0:T(8,128)S(1)} %get-tuple-element.79.refs_5_), channel_id=1, source_target_pairs={{0,3},{1,0},{2,1},{3,2},{4,7},{5,4},{6,5},{7,6},{8,11},{9,8},{10,9... | collective-permute-start | bytes 98312 | tf_op jit(solution)/shard_map/ppermute | solution.py:270
  206.1 4.3 %collective-permute-start.22 = (f32[64,128]{1,0:T(8,128)S(1)}, f32[64,128]{1,0:T(8,128)S(1)}, u32[]{:S(2)}, u32[]{:S(2)}) collective-permute-start(f32[64,128]{1,0:T(8,128)S(1)} %get-tuple-element.79.refs_5_), channel_id=1, source_target_pairs={{0,2},{1,3},{2,0},{3,1},{4,6},{5,7},{6,4},{7,5},{8,10},{9,11},{10,... | collective-permute-start | bytes 98312 | tf_op jit(solution)/shard_map/ppermute | solution.py:270
  207.0 4.4 %collective-permute-start.21 = (f32[64,128]{1,0:T(8,128)S(1)}, f32[64,128]{1,0:T(8,128)S(1)}, u32[]{:S(2)}, u32[]{:S(2)}) collective-permute-start(f32[64,128]{1,0:T(8,128)S(1)} %get-tuple-element.79.refs_5_), channel_id=1, source_target_pairs={{0,1},{1,2},{2,3},{3,0},{4,5},{5,6},{6,7},{7,4},{8,9},{9,10},{10,1... | collective-permute-start | bytes 98312 | tf_op jit(solution)/shard_map/ppermute | solution.py:270

commit v2 on v1

--- a/solution.py
+++ b/solution.py
@@ -10,24 +10,39 @@
 
 ITERS = 2
 EPSILON = 1e-06
-ORDER = (2, 1, 0, 5, 4, 3, 8, 7, 6, 9)
 BF = jnp.bfloat16
 F32 = jnp.float32
 VMEM_LIMIT = 40 * 1024 * 1024
-
-
-def call(kernel, outs, scratch=(), name=None):
+START_LIMIT = 60 * 1024 * 1024
+
+
+def call(kernel, outs, scratch=(), name=None, limit=VMEM_LIMIT, anywhere=False, after=()):
+    space = pl.ANY if anywhere else pltpu.VMEM
+    given = kernel
+
     def run(places, *operands):
+        count = 1 + len(operands)
+
+        def kernel(*refs):
+            given(*refs[:count], *refs[count + len(after) :])
+
         return pl.pallas_call(
             kernel,
-            out_shape=[jax.ShapeDtypeStruct(shape, dtype) for shape, dtype in outs],
+            out_shape=[jax.ShapeDtypeStruct(out[0], out[1]) for out in outs],
             in_specs=[pl.BlockSpec(memory_space=pltpu.SMEM)]
-            + [pl.BlockSpec(memory_space=pltpu.VMEM)] * len(operands),
-            out_specs=[pl.BlockSpec(memory_space=pltpu.VMEM)] * len(outs),
-            scratch_shapes=[pltpu.VMEM(shape, dtype) for shape, dtype in scratch],
-            compiler_params=pltpu.CompilerParams(vmem_limit_bytes=VMEM_LIMIT),
+            + [pl.BlockSpec(memory_space=space)] * len(operands)
+            + [pl.BlockSpec(memory_space=pl.ANY)] * len(after),
+            out_specs=[
+                pl.BlockSpec(memory_space=pl.ANY if len(out) > 2 else pltpu.VMEM)
+                for out in outs
+            ],
+            scratch_shapes=[
+                pltpu.VMEM(*entry) if isinstance(entry, tuple) else entry
+                for entry in scratch
+            ],
+            compiler_params=pltpu.CompilerParams(vmem_limit_bytes=limit),
             name=name,
-        )(places, *operands)
+        )(places, *operands, *after)
 
     return run
 
@@ -85,7 +100,7 @@
 
 def write_partial(places, coeffs, right, squares, keep, send, field):
     for t in range(4):
-        factors = jnp.concatenate([right[pair, t] for pair in ORDER], axis=0)
+        factors = jnp.concatenate([right[pair, t] for pair in range(10)], axis=0)
         value = dot(coeffs(t), factors)
         for i in range(8):
             field[i % 4, pl.ds(2 * t + i // 4, 64, stride=8), :] = value[
@@ -102,32 +117,88 @@
     send[:, 512:640] = tail.astype(BF)
 
 
-def start_kernel(places, left, right, observations, keep, send, field, slots):
+def in_slots(slots):
+    return lambda t: jnp.concatenate(
+        [slots[j][:, 32 * t : 32 * t + 32] for j in range(10)], axis=1
+    )
+
+
+def start_kernel(
+    places, left, right, observations, keep, send, one, two, three, own, own_field,
+    field, slots, left_here, right_here, values_here, in_sems, out_sems,
+):
+    here = places[0]
+    loads = []
+    for pair in range(10):
+        loads.append(
+            (
+                pltpu.make_async_copy(
+                    observations.at[pair], values_here.at[pair], in_sems.at[2 * pair]
+                ),
+                pltpu.make_async_copy(
+                    left.at[pair], left_here.at[pair], in_sems.at[2 * pair + 1]
+                ),
+            )
+        )
+    right_loads = [
+        pltpu.make_async_copy(right.at[:, t], right_here.at[:, t], in_sems.at[20 + t])
+        for t in range(4)
+    ]
+    for first, second in loads:
+        first.start()
+        second.start()
+    for load in right_loads:
+        load.start()
     total = jnp.zeros((64, 128), F32)
-    for j, pair in enumerate(ORDER):
-        values = observations[pair]
+    for pair, (first, second) in enumerate(loads):
+        first.wait()
+        values = values_here[pair]
         wide = values.astype(F32)
         wide = wide * wide
         total = total + sum(wide[:, 128 * i : 128 * i + 128] for i in range(8))
-        slots[j] = dot_nt(values, left[pair]).astype(BF)
-    coeffs = lambda t: jnp.concatenate(
-        [slots[j][:, 32 * t : 32 * t + 32] for j in range(10)], axis=1
-    )
-    write_partial(places, coeffs, right, lane_sum(total), keep, send, field)
-
-
-def back_kernel(places, right, own, one, two, three, keep, send, field, slots):
+        second.wait()
+        slots[pair] = dot_nt(values, left_here[pair]).astype(BF)
+    stores = []
+    for step, out in enumerate((own, one, two, three)):
+        peer = lax.rem(here + step, 4)
+        half = pl.ds(pl.multiple_of(512 * lax.rem(peer, 2), 512), 512)
+        at = 5 * step
+        for unit in range(4):
+            source = left_here.at[2 * peer + unit // 2, :, pl.ds(512 * (unit % 2), 512)]
+            stores.append(
+                pltpu.make_async_copy(source, out.at[unit], out_sems.at[at + unit])
+            )
+        source = left_here.at[8 + peer // 2, :, half]
+        stores.append(pltpu.make_async_copy(source, out.at[4], out_sems.at[at + 4]))
+    half = pl.ds(pl.multiple_of(512 * lax.rem(here, 2), 512), 512)
+    for unit in range(4):
+        source = values_here.at[2 * here + unit // 2, :, pl.ds(512 * (unit % 2), 512)]
+        stores.append(
+            pltpu.make_async_copy(source, own_field.at[unit], out_sems.at[20 + unit])
+        )
+    source = values_here.at[8 + here // 2, :, half]
+    stores.append(pltpu.make_async_copy(source, own_field.at[4], out_sems.at[24]))
+    for store in stores:
+        store.start()
+    for load in right_loads:
+        load.wait()
+    write_partial(places, in_slots(slots), right_here, lane_sum(total), keep, send, field)
+    for store in stores:
+        store.wait()
+
+
+def back_kernel(places, right, own, one, two, three, keep, send, field, slots, shared):
     here = places[0]
     squares = jnp.zeros((64, 1), F32)
     for step, chunk in enumerate((own, one, two, three)):
-        at = 3 * lax.rem(here + step, 4)
-        for i in range(3):
-            slots[at + i] = chunk[i]
+        peer = lax.rem(here + step, 4)
+        slots[2 * peer] = chunk[0]
+        slots[2 * peer + 1] = chunk[1]
+        shared[peer] = chunk[2].astype(F32)
         squares = squares + lane_sum(chunk[3].astype(F32))
-    coeffs = lambda t: jnp.concatenate(
-        [slots[j][:, 32 * t : 32 * t + 32] for j in range(10)], axis=1
-    )
-    write_partial(places, coeffs, right, squares, keep, send, field)
+    slots[8] = (shared[0] + shared[1]).astype(BF)
+    slots[9] = (shared[2] + shared[3]).astype(BF)
+    write_partial(places, in_slots(slots), right, squares, keep, send, field)
 
 
 def core_kernel(places, keep, got, out):
@@ -172,18 +243,17 @@
 def forward_kernel(places, mine, other, right, model, own, one, two, three, field, slots):
     squares = read_model(places, mine, other, model, field)
     for t in range(4):
-        factors = jnp.concatenate([right[pair, t] for pair in ORDER], axis=0)
+        factors = jnp.concatenate([right[pair, t] for pair in range(10)], axis=0)
         value = dot_nt(model[:, 1024 * t : 1024 * t + 1024], factors).astype(BF)
         for j in range(10):
             slots[j, :, 32 * t : 32 * t + 32] = value[:, 32 * j : 32 * j + 32]
-    for j in (10, 11):
-        slots[j] = jnp.zeros((64, 128), BF)
     tail = pieces_in_lanes(squares).astype(BF)
     here = places[0]
     for step, chunk in enumerate((own, one, two, three)):
-        at = 3 * lax.rem(here + step, 4)
-        for i in range(3):
-            chunk[i] = slots[at + i]
+        peer = lax.rem(here + step, 4)
+        chunk[0] = slots[2 * peer]
+        chunk[1] = slots[2 * peer + 1]
+        chunk[2] = slots[8 + peer // 2]
         chunk[3] = tail
 
 
@@ -197,16 +267,20 @@
     ratio = length / data_len[:, 0:1]
     total = jnp.zeros((64, 128), F32)
     for i in range(3):
-        factors = jnp.concatenate([block[2 - i] for block in left], axis=0)
-        value = dot(jnp.concatenate([chunk[i] for chunk in coeffs], axis=1), factors)
-        value = value * inverse - ratio * field[i]
-        if not last:
-            refs[5][i] = value
-        back = dot_nt(value.astype(BF), factors).astype(BF)
+        given = jnp.concatenate([chunk[i] for chunk in coeffs], axis=1)
+        back = None
+        for unit in range(2 * i, min(2 * i + 2, 5)):
+            factors = jnp.concatenate([block[unit] for block in left], axis=0)
+            value = dot(given, factors) * inverse - ratio * field[unit].astype(F32)
+            if not last:
+                refs[5][unit] = value
+            term = dot_nt(value.astype(BF), factors)
+            back = term if back is None else back + term
+            value = value * value
+            total = total + sum(value[:, 128 * k : 128 * k + 128] for k in range(4))
+        back = back.astype(BF)
         for step in range(4):
             outs[step][i] = back[:, 128 * step : 128 * step + 128]
-        value = value * value
-        total = total + sum(value[:, 128 * k : 128 * k + 128] for k in range(8))
     tail = pieces_in_lanes(lane_sum(total)).astype(BF)
     for step in range(4):
         outs[step][3] = tail
@@ -283,7 +357,7 @@
 
 
 PARTIAL = [((256, 640), F32), ((256, 640), BF)]
-PARTIAL_SCRATCH = [((4, 512, 128), F32), ((12, 64, 128), BF)]
+PARTIAL_SCRATCH = [((4, 512, 128), F32), ((10, 64, 128), BF)]
 CHUNKS = [((4, 64, 128), BF)] * 4
 COLUMN = ((64, 128), F32)
 MODEL = ((64, 4096), BF)
@@ -297,64 +371,74 @@
     left = left.reshape(10, 128, 1024)
     right = right.reshape(10, 4, 32, 1024)
     observations = observations.reshape(10, 64, 1024)
-    own_first = lambda device: jnp.minimum(3 * device, 7)
-    owned = []
-    for step in range(4):
-        block = lax.dynamic_slice_in_dim(left, own_first((here + step) % 4), 3, 0)
-        owned.append(block if step == 0 else shift(block, step))
-    field = lax.dynamic_slice_in_dim(observations, own_first(here), 3, 0)[::-1]
-    valid = (here < 3) | (jnp.arange(3) == 0)
-    field = jnp.where(valid[:, None, None], field.astype(F32), 0.0)
-
-    def sum_dp(keep, send, first, *extra):
+
+    def sum_dp(keep, send, extra, before_shard=()):
         whole = call(core_kernel, [((256, 640), BF)], name="core_sum")(
             places, keep, swap_core(send)
         )[0]
         raw, data_len, send = call(
-            functools.partial(shard_kernel, first),
+            functools.partial(shard_kernel, not extra),
             [((8, 512), F32), COLUMN, ((256, 512), BF)],
             name="shard",
+            after=before_shard,
         )(places, exchange(whole), *extra)
         mine = exchange(send)
         return raw, data_len, mine, swap_core(mine)
 
-    keep, send = call(start_kernel, PARTIAL, PARTIAL_SCRATCH, name="start")(
-        places, left, right, observations
-    )
-    raw, data_len, mine, other = sum_dp(keep, send, True)
+    keep, send, one, two, three, own, field = call(
+        start_kernel,
+        PARTIAL + [((5, 128, 512), BF, True)] * 4 + [((5, 64, 512), BF, True)],
+        PARTIAL_SCRATCH
+        + [
+            ((10, 128, 1024), BF),
+            ((10, 4, 32, 1024), BF),
+            ((10, 64, 1024), BF),
+            pltpu.SemaphoreType.DMA((24,)),
+            pltpu.SemaphoreType.DMA((25,)),
+        ],
+        name="start",
+        limit=START_LIMIT,
+        anywhere=True,
+    )(places, left, right, observations)
+    one, two, three = shift(one, 1), shift(two, 2), shift(three, 3)
+    owned = [own, one, two, three]
+    raw, data_len, mine, other = sum_dp(keep, send, (), (one, three))
     models, model_lens, data_lens = [], [], [data_len]
     for sweep in range(ITERS):
         model, *chunks = call(
             forward_kernel,
             [MODEL] + CHUNKS,
-            [((4, 512, 128), F32), ((12, 64, 128), BF)],
+            [((4, 512, 128), F32), ((10, 64, 128), BF)],
             name="forward",
+            after=(two,) if sweep == 0 else (),
         )(places, mine, other, right)
         models.append(model)
         chunks = [chunks[0]] + [shift(chunks[step], step) for step in (1, 2, 3)]
         last = sweep == ITERS - 1
         outs = call(
             functools.partial(data_kernel, last),
-            [COLUMN] + CHUNKS + ([] if last else [((3, 64, 1024), F32)]),
+            [COLUMN] + CHUNKS + ([] if last else [((5, 64, 512), F32)]),
             name="data",
         )(places, *chunks, *owned, field, data_lens[-1])
         model_lens.append(outs[0])
         field = None if last else outs[5]
         chunks = [outs[1]] + [shift(outs[1 + step], -step) for step in (1, 2, 3)]
-        keep, send = call(back_kernel, PARTIAL, PARTIAL_SCRATCH, name="back")(
-            places, right, *chunks
-        )
-        raw, data_len, mine, other = sum_dp(keep, send, False, raw, model_lens[-1])
+        keep, send = call(
+            back_kernel, PARTIAL, PARTIAL_SCRATCH + [((4, 64, 128), F32)], name="back"
+        )(places, right, *chunks)
+        raw, data_len, mine, other = sum_dp(keep, send, (raw, model_lens[-1]))
         data_lens.append(data_len)
 
     model, squares = call(
         last_model_kernel, [MODEL, COLUMN], [((4, 512, 128), F32)], name="last_model"
     )(places, mine, other)
+    solve_after = (squares,)
     squares = [squares] + [shift(squares, step) for step in (1, 2, 3)]
     solved, residual, last_direction = call(
         solution_kernel,
         [((4, 64, 1024), F32), COLUMN, ((4, 64, 1024), F32)],
         name="solve",
+        after=solve_after,
     )(places, *data_lens, *model_lens, *models)
     direction = call(direction_kernel, [((4, 64, 1024), F32)], name="direct")(
         places, *data_lens, *model_lens, *squares, model, last_direction

time: 214 us -> 204 us (0.953)
  waiting for transfers between devices: 51.3 us -> 43.6 us
  local copies, waits for them, and re-layouts: 10.6 us -> 4.37 us
  Pallas kernels: 26.2 us -> 29.2 us
    ppermute x18, waiting for transfers between devices: 31.9 us -> 20.5 us  [shift(): return lax.ppermute(value, 'x', [(i, (i + step) % 4) for i in range(4)])]
    dynamic_slice x2 -> x0, local copies, waits for them, and re-layouts: 4.52 us -> none  [the longest x1 3.5 us: on_device(): block = lax.dynamic_slice_in_dim(left, own_first((here + step) % 4), 3, 0)]
    all_to_all x2, waiting for transfers between devices: 13.9 us -> 18.3 us  [exchange(): lax.all_to_all(value.reshape(32, 8, width), ('z', 'y'), split_axis=0, con...]
    pallas_call x16, Pallas kernels: 26.2 us -> 29.2 us  [run(): pl.pallas_call(kernel, out_shape=[jax.ShapeDtypeStruct(out[0], out[1]) fo...]
    unnamed x10 -> x22, local copies, waits for them, and re-layouts: 5.49 us -> 3.74 us
  transfers between devices with their start and end apart: 26 -> 26, of which waited for: 19 -> 19; matrix products, arithmetic and copies ran while one was open for 2% -> 0% of each run, Pallas kernels for 3% -> 1%
where the time goes in v2:
time: 204 us; the launch traced here: 203 us
  blocking collectives  67.8 us (33%)
  starting transfers between devices  57 us (28%)
  waiting for transfers between devices  43.6 us (21%)
  Pallas kernels  29.2 us (14%)
  local copies, waits for them, and re-layouts  4.37 us (2%)
    all_to_all x4, blocking collectives, exchange(): lax.all_to_all(value.reshape(32, 8, width), ('z', 'y'), split_axis=0, con...  67.8 us
    pallas_call x16, Pallas kernels, run(): pl.pallas_call(kernel, out_shape=[jax.ShapeDtypeStruct(out[0], out[1]) fo...  29.2 us
    ppermute x6, starting transfers between devices, swap_core(): return lax.ppermute(value, 'c', [(0, 1), (1, 0)])  22.7 us
    ppermute x18, waiting for transfers between devices, shift(): return lax.ppermute(value, 'x', [(i, (i + step) % 4) for i in range(4)])  20.5 us
    ppermute x18, starting transfers between devices, shift(): return lax.ppermute(value, 'x', [(i, (i + step) % 4) for i in range(4)])  19.7 us
    all_to_all x2, waiting for transfers between devices, exchange(): lax.all_to_all(value.reshape(32, 8, width), ('z', 'y'), split_axis=0, con...  18.3 us
    all_to_all x2, starting transfers between devices, exchange(): lax.all_to_all(value.reshape(32, 8, width), ('z', 'y'), split_axis=0, con...  14.6 us
    ppermute x6, waiting for transfers between devices, swap_core(): return lax.ppermute(value, 'c', [(0, 1), (1, 0)])  4.84 us
  transfers between devices with their start and end apart: 26, of which 19 were waited for; matrix products, arithmetic and copies ran while one was open for 0% of the time, Pallas kernels for 1%

profile of v2, /device:TPU:1, one launch (start us, length us, event | category | flops | bytes accessed | tf_op | source)
XLA Modules:
  0.0 203.4 jit_solution(4444966970570701805)
XLA Ops:
  0.6 0.6 pad_add_fusion.refs_0_
  1.3 7.5 %start.1 = (f32[256,640]{1,0:T(8,128)}, bf16[256,640]{1,0:T(8,128)(2,1)}, bf16[5,128,512]{2,1,0:T(8,128)(2,1)}, bf16[5,128,512]{2,1,0:T(8,128)(2,1)}, bf16[5,128...) custom-call(s32[3]{0:T(128)} %pad_add_fusion.refs_0_, ...), custom_call_target="tpu_custom_call" | custom-call | tf_op jit(solution)/shard_map/start/pallas_call | solution.py:29
  8.7 3.3 %collective-permute-start = (bf16[256,640]{1,0:T(8,128)(2,1)}, bf16[256,640]{1,0:T(8,128)(2,1)S(1)}, u32[]{:S(2)}, u32[]{:S(2)}) collective-permute-start(bf16[256,640]{1,0:T(8,128)(2,1)} %get-tuple-element.49), channel_id=1, source_target_pairs={{0,4},{4,0},{1,5},{5,1},{2,6},{6,2},{3,7},{7,3},{8,12},{12,8},{9,1... | collective-permute-start | bytes 983048 | tf_op jit(solution)/shard_map/ppermute | solution.py:348
  12.1 2.7 %collective-permute-start.2 = (bf16[5,128,512]{2,1,0:T(8,128)(2,1)}, bf16[5,128,512]{2,1,0:T(8,128)(2,1)}, u32[]{:S(2)}, u32[]{:S(2)}) collective-permute-start(bf16[5,128,512]{2,1,0:T(8,128)(2,1)} %get-tuple-element.51), channel_id=1, source_target_pairs={{0,3},{1,0},{2,1},{3,2},{4,7},{5,4},{6,5},{7,6},{8,11},{9,8},{10,9... | collective-permute-start | bytes 1966088 | tf_op jit(solution)/shard_map/ppermute | solution.py:344
  14.8 1.1 copy-done.3
  15.9 0.6 core_sum.3
  16.5 0.7 copy-done.2
  17.2 9.6 %all-to-all-start = ((bf16[32,8,640]{2,1,0:T(8,128)(2,1)}), bf16[32,8,640]{2,1,0:T(8,128)(2,1)}, u32[]{:S(2)}, u32[]{:S(2)}) async-start(bf16[32,8,640]{2,1,0:T(8,128)(2,1)} %bitcast.25), calls=%async_computation | async-start | bytes 655360 | tf_op jit(solution)/shard_map/all_to_all | solution.py:353
  26.8 3.0 %collective-permute-done.1.refs_2_.refs_6_ = bf16[5,128,512]{2,1,0:T(8,128)(2,1)S(1)} collective-permute-done((bf16[5,128,512]{2,1,0:T(8,128)(2,1)}, bf16[5,128,512]{2,1,0:T(8,128)(2,1)S(1)}, u32[]{:S(2)}, u32[]{:S(2)}) %collective-permute-start.1) | collective-permute-done | bytes 655392 | tf_op jit(solution)/shard_map/ppermute | solution.py:344
  29.8 9.5 %all-to-all-done = bf16[32,8,640]{2,1,0:T(8,128)(2,1)} async-done(((bf16[32,8,640]{2,1,0:T(8,128)(2,1)}), bf16[32,8,640]{2,1,0:T(8,128)(2,1)}, u32[]{:S(2)}, u32[]{:S(2)}) %all-to-all-start) | async-done | bytes 327712 | tf_op jit(solution)/shard_map/all_to_all | solution.py:353
  39.3 1.2 shard.3
  40.5 0.6 copy-done.5
  41.1 0.6 copy-done.9
  41.7 0.7 copy-done.7
  42.4 5.0 %all-to-all-start.1 = ((bf16[32,8,512]{2,1,0:T(8,128)(2,1)}), bf16[32,8,512]{2,1,0:T(8,128)(2,1)S(1)}, u32[]{:S(2)}, u32[]{:S(2)}) async-start(bf16[32,8,512]{2,1,0:T(8,128)(2,1)} %bitcast.34), calls=%async_computation.1 | async-start | bytes 524288 | tf_op jit(solution)/shard_map/all_to_all | solution.py:353
  47.4 1.6 collective-permute-start.4
  49.0 8.8 %all-to-all-done.1 = bf16[32,8,512]{2,1,0:T(8,128)(2,1)S(1)} async-done(((bf16[32,8,512]{2,1,0:T(8,128)(2,1)}), bf16[32,8,512]{2,1,0:T(8,128)(2,1)S(1)}, u32[]{:S(2)}, u32[]{:S(2)}) %all-to-all-start.1) | async-done | bytes 262176 | tf_op jit(solution)/shard_map/all_to_all | solution.py:353
  57.9 3.5 %collective-permute-start.3 = (bf16[256,512]{1,0:T(8,128)(2,1)S(1)}, bf16[256,512]{1,0:T(8,128)(2,1)S(1)}, u32[]{:S(2)}, u32[]{:S(2)}) collective-permute-start(bf16[256,512]{1,0:T(8,128)(2,1)S(1)} %bitcast.28), channel_id=1, source_target_pairs={{0,4},{4,0},{1,5},{5,1},{2,6},{6,2},{3,7},{7,3},{8,12},{12,8},{9,1... | collective-permute-start | bytes 786440 | tf_op jit(solution)/shard_map/ppermute | solution.py:348
  61.4 2.5 %collective-permute-done.4.refs_4_.refs_7_ = bf16[5,128,512]{2,1,0:T(8,128)(2,1)} collective-permute-done((bf16[5,128,512]{2,1,0:T(8,128)(2,1)}, bf16[5,128,512]{2,1,0:T(8,128)(2,1)}, u32[]{:S(2)}, u32[]{:S(2)}) %collective-permute-start.4) | collective-permute-done | bytes 655392 | tf_op jit(solution)/shard_map/ppermute | solution.py:344
  63.9 1.7 forward.2
  65.8 2.4 %collective-permute-start.6 = (bf16[4,64,128]{2,1,0:T(8,128)(2,1)S(1)}, bf16[4,64,128]{2,1,0:T(8,128)(2,1)S(1)}, u32[]{:S(2)}, u32[]{:S(2)}) collective-permute-start(bf16[4,64,128]{2,1,0:T(8,128)(2,1)S(1)} %get-tuple-element.57), channel_id=1, source_target_pairs={{0,2},{1,3},{2,0},{3,1},{4,6},{5,7},{6,4},{7,5},{8,10},{9,11},{10,... | collective-permute-start | bytes 196616 | tf_op jit(solution)/shard_map/ppermute | solution.py:344
  68.2 1.2 collective-permute-start.7
  69.4 1.4 collective-permute-done.5.refs_2_
  70.8 0.6 collective-permute-done.7.refs_4_
  71.4 2.9 %data.2 = (f32[64,128]{1,0:T(8,128)S(1)}, bf16[4,64,128]{2,1,0:T(8,128)(2,1)S(1)}, bf16[4,64,128]{2,1,0:T(8,128)(2,1)S(1)}, bf16[4,64,128]{2,1,0:T(8,128)(2,1)S(...) custom-call(s32[3]{0:T(128)S(1)} %copy-done.8, bf16[4,64,128]{2,1,0:T(8,128)(2,1)S(1)} %get-tuple-element.55.refs_1_, ...), custom_call_target="tpu_custom_call" | custom-call | tf_op jit(solution)/shard_map/data/pallas_call | solution.py:29
  74.3 2.5 %collective-permute-start.8 = (bf16[4,64,128]{2,1,0:T(8,128)(2,1)S(1)}, bf16[4,64,128]{2,1,0:T(8,128)(2,1)S(1)}, u32[]{:S(2)}, u32[]{:S(2)}) collective-permute-start(bf16[4,64,128]{2,1,0:T(8,128)(2,1)S(1)} %get-tuple-element.62), channel_id=1, source_target_pairs={{0,3},{1,0},{2,1},{3,2},{4,7},{5,4},{6,5},{7,6},{8,11},{9,8},{10,9... | collective-permute-start | bytes 196616 | tf_op jit(solution)/shard_map/ppermute | solution.py:344
  77.4 0.7 collective-permute-done.8.refs_3_
  78.1 3.4 %collective-permute-done.9.refs_4_ = bf16[4,64,128]{2,1,0:T(8,128)(2,1)S(1)} collective-permute-done((bf16[4,64,128]{2,1,0:T(8,128)(2,1)S(1)}, bf16[4,64,128]{2,1,0:T(8,128)(2,1)S(1)}, u32[]{:S(2)}, u32[]{:S(2)}) %collective-permute-start.9) | collective-permute-done | bytes 65568 | tf_op jit(solution)/shard_map/ppermute | solution.py:344
  81.4 0.6 collective-permute-done.10.refs_5_
  82.0 1.4 back.2
  83.5 5.7 %collective-permute-start.11 = (bf16[256,640]{1,0:T(8,128)(2,1)S(1)}, bf16[256,640]{1,0:T(8,128)(2,1)S(1)}, u32[]{:S(2)}, u32[]{:S(2)}) collective-permute-start(bf16[256,640]{1,0:T(8,128)(2,1)S(1)} %get-tuple-element.66), channel_id=1, source_target_pairs={{0,4},{4,0},{1,5},{5,1},{2,6},{6,2},{3,7},{7,3},{8,12},{12,8},{9,1... | collective-permute-start | bytes 983048 | tf_op jit(solution)/shard_map/ppermute | solution.py:348
  89.2 1.3 collective-permute-done.11.refs_2_
  90.4 0.6 core_sum.4
  91.1 21.8 %all_to_all.30 = bf16[32,8,640]{2,1,0:T(8,128)(2,1)S(1)} all-to-all(bf16[32,8,640]{2,1,0:T(8,128)(2,1)S(1)} %bitcast.26), channel_id=1, replica_groups=mesh['z'=8,'y'=4,'c'=2,'x'=4] {'z','y'}, dimensions={0} | all-to-all | bytes 655360 | tf_op jit(solution)/shard_map/all_to_all | solution.py:353
  112.8 0.7 shard.4
  113.6 15.0 %all_to_all.31 = bf16[32,8,512]{2,1,0:T(8,128)(2,1)S(1)} all-to-all(bf16[32,8,512]{2,1,0:T(8,128)(2,1)S(1)} %bitcast.35), channel_id=1, replica_groups=mesh['z'=8,'y'=4,'c'=2,'x'=4] {'z','y'}, dimensions={0} | all-to-all | bytes 524288 | tf_op jit(solution)/shard_map/all_to_all | solution.py:353
  128.5 3.5 %collective-permute-start.12 = (bf16[256,512]{1,0:T(8,128)(2,1)S(1)}, bf16[256,512]{1,0:T(8,128)(2,1)S(1)}, u32[]{:S(2)}, u32[]{:S(2)}) collective-permute-start(bf16[256,512]{1,0:T(8,128)(2,1)S(1)} %bitcast.32), channel_id=1, source_target_pairs={{0,4},{4,0},{1,5},{5,1},{2,6},{6,2},{3,7},{7,3},{8,12},{12,8},{9,1... | collective-permute-start | bytes 786440 | tf_op jit(solution)/shard_map/ppermute | solution.py:348
  132.1 1.2 collective-permute-done.12.refs_2_
  133.3 1.7 forward.3
  135.1 1.4 collective-permute-start.14
  136.6 1.7 collective-permute-start.15
  138.2 3.1 %collective-permute-done.13.refs_2_ = bf16[4,64,128]{2,1,0:T(8,128)(2,1)S(1)} collective-permute-done((bf16[4,64,128]{2,1,0:T(8,128)(2,1)S(1)}, bf16[4,64,128]{2,1,0:T(8,128)(2,1)S(1)}, u32[]{:S(2)}, u32[]{:S(2)}) %collective-permute-start.13) | collective-permute-done | bytes 65568 | tf_op jit(solution)/shard_map/ppermute | solution.py:344
  141.4 2.8 %data.3 = (f32[64,128]{1,0:T(8,128)S(1)}, bf16[4,64,128]{2,1,0:T(8,128)(2,1)S(1)}, bf16[4,64,128]{2,1,0:T(8,128)(2,1)S(1)}, bf16[4,64,128]{2,1,0:T(8,128)(2,1)S(1)}, bf16[4,64,128]{2,1,0:T(8,128)(2,1)S(1)}) custom-call(s32[3]{0:T(128)S(1)} %copy-done.8, bf16[4,64,128]{2,1,0:T(8,128)(2,1)S(1)} %get-tuple-element.71.refs_1_, ...), custom_call_target="tpu_custom_call" | custom-call | tf_op jit(solution)/shard_map/data/pallas_call | solution.py:29
  144.2 2.5 %collective-permute-start.16 = (bf16[4,64,128]{2,1,0:T(8,128)(2,1)S(1)}, bf16[4,64,128]{2,1,0:T(8,128)(2,1)S(1)}, u32[]{:S(2)}, u32[]{:S(2)}) collective-permute-start(bf16[4,64,128]{2,1,0:T(8,128)(2,1)S(1)} %get-tuple-element.77), channel_id=1, source_target_pairs={{0,3},{1,0},{2,1},{3,2},{4,7},{5,4},{6,5},{7,6},{8,11},{9,8},{10,9... | collective-permute-start | bytes 196616 | tf_op jit(solution)/shard_map/ppermute | solution.py:344
  146.9 0.6 collective-permute-start.18
  147.4 0.7 collective-permute-done.16.refs_3_
  148.1 3.4 %collective-permute-done.17.refs_4_ = bf16[4,64,128]{2,1,0:T(8,128)(2,1)S(1)} collective-permute-done((bf16[4,64,128]{2,1,0:T(8,128)(2,1)S(1)}, bf16[4,64,128]{2,1,0:T(8,128)(2,1)S(1)}, u32[]{:S(2)}, u32[]{:S(2)}) %collective-permute-start.17) | collective-permute-done | bytes 65568 | tf_op jit(solution)/shard_map/ppermute | solution.py:344
  151.9 1.4 back.3
  153.3 3.0 %collective-permute-start.19 = (bf16[256,640]{1,0:T(8,128)(2,1)S(1)}, bf16[256,640]{1,0:T(8,128)(2,1)S(1)}, u32[]{:S(2)}, u32[]{:S(2)}) collective-permute-start(bf16[256,640]{1,0:T(8,128)(2,1)S(1)} %get-tuple-element.81), channel_id=1, source_target_pairs={{0,4},{4,0},{1,5},{5,1},{2,6},{6,2},{3,7},{7,3},{8,12},{12,8},{9,1... | collective-permute-start | bytes 983048 | tf_op jit(solution)/shard_map/ppermute | solution.py:348
  156.4 1.3 collective-permute-done.19.refs_2_
  157.6 0.6 core_sum.5
  158.2 16.0 %all_to_all.32 = bf16[32,8,640]{2,1,0:T(8,128)(2,1)S(1)} all-to-all(bf16[32,8,640]{2,1,0:T(8,128)(2,1)S(1)} %bitcast.27), channel_id=1, replica_groups=mesh['z'=8,'y'=4,'c'=2,'x'=4] {'z','y'}, dimensions={0} | all-to-all | bytes 655360 | tf_op jit(solution)/shard_map/all_to_all | solution.py:353
  174.3 1.3 shard.5
  175.6 15.0 %all_to_all.33 = bf16[32,8,512]{2,1,0:T(8,128)(2,1)S(1)} all-to-all(bf16[32,8,512]{2,1,0:T(8,128)(2,1)S(1)} %bitcast.36), channel_id=1, replica_groups=mesh['z'=8,'y'=4,'c'=2,'x'=4] {'z','y'}, dimensions={0} | all-to-all | bytes 524288 | tf_op jit(solution)/shard_map/all_to_all | solution.py:353
  190.6 3.5 %collective-permute-start.20 = (bf16[256,512]{1,0:T(8,128)(2,1)S(1)}, bf16[256,512]{1,0:T(8,128)(2,1)S(1)}, u32[]{:S(2)}, u32[]{:S(2)}) collective-permute-start(bf16[256,512]{1,0:T(8,128)(2,1)S(1)} %bitcast.30), channel_id=1, source_target_pairs={{0,4},{4,0},{1,5},{5,1},{2,6},{6,2},{3,7},{7,3},{8,12},{12,8},{9,1... | collective-permute-start | bytes 786440 | tf_op jit(solution)/shard_map/ppermute | solution.py:348
  194.1 1.2 collective-permute-done.20.refs_2_
  195.3 0.9 last_model.1
  196.2 0.6 collective-permute-start.23
  196.7 0.9 collective-permute-start.22
  197.6 0.8 collective-permute-start.21
  198.4 2.0 solve.1
  200.3 0.6 slice_reduce_fusion
  201.0 0.6 collective-permute-done.21.refs_7_
  201.6 1.8 direct.1
  (32 shorter events, 1.5 us)
Async XLA Ops:
  1.3 13.5 %copy-start.8 = (s32[3]{0:T(128)S(1)}, s32[3]{0:T(128)}, u32[]{:S(2)}) copy-start(s32[3]{0:T(128)} %pad_add_fusion.refs_0_) | copy-start | bytes 40
  8.7 55.2 %copy-start = (bf16[2,5,4,32,1024]{4,3,2,1,0:T(8,128)(2,1)S(1)}, bf16[2,5,4,32,1024]{4,3,2,1,0:T(8,128)(2,1)}, u32[]{:S(2)}) copy-start(bf16[2,5,4,32,1024]{4,3,2,1,0:T(8,128)(2,1)} %param.4) | copy-start | bytes 7864324
  8.7 6.0 %collective-permute-start = (bf16[256,640]{1,0:T(8,128)(2,1)}, bf16[256,640]{1,0:T(8,128)(2,1)S(1)}, u32[]{:S(2)}, u32[]{:S(2)}) collective-permute-start(bf16[256,640]{1,0:T(8,128)(2,1)} %get-tuple-element.49), channel_id=1, source_target_pairs={{0,4},{4,0},{1,5},{5,1},{2,6},{6,2},{3,7},{7,3},{8,12},{12,8},{9,1... | collective-permute-start | bytes 983048 | tf_op jit(solution)/shard_map/ppermute | solution.py:348
  12.1 17.7 %collective-permute-start.1 = (bf16[5,128,512]{2,1,0:T(8,128)(2,1)}, bf16[5,128,512]{2,1,0:T(8,128)(2,1)S(1)}, u32[]{:S(2)}, u32[]{:S(2)}) collective-permute-start(bf16[5,128,512]{2,1,0:T(8,128)(2,1)} %get-tuple-element.50), channel_id=1, source_target_pairs={{0,1},{1,2},{2,3},{3,0},{4,5},{5,6},{6,7},{7,4},{8,9},{9,10},{10,1... | collective-permute-start | bytes 1966088 | tf_op jit(solution)/shard_map/ppermute | solution.py:344
  12.1 17.7 %collective-permute-start.2 = (bf16[5,128,512]{2,1,0:T(8,128)(2,1)}, bf16[5,128,512]{2,1,0:T(8,128)(2,1)}, u32[]{:S(2)}, u32[]{:S(2)}) collective-permute-start(bf16[5,128,512]{2,1,0:T(8,128)(2,1)} %get-tuple-element.51), channel_id=1, source_target_pairs={{0,3},{1,0},{2,1},{3,2},{4,7},{5,4},{6,5},{7,6},{8,11},{9,8},{10,9... | collective-permute-start | bytes 1966088 | tf_op jit(solution)/shard_map/ppermute | solution.py:344
  14.8 1.1 copy-start.3
  16.5 0.7 copy-start.2
  17.2 22.1 %all-to-all-start = ((bf16[32,8,640]{2,1,0:T(8,128)(2,1)}), bf16[32,8,640]{2,1,0:T(8,128)(2,1)}, u32[]{:S(2)}, u32[]{:S(2)}) async-start(bf16[32,8,640]{2,1,0:T(8,128)(2,1)} %bitcast.25), calls=%async_computation | async-start | bytes 655360 | tf_op jit(solution)/shard_map/all_to_all | solution.py:353
  40.5 0.6 copy-start.5
  41.1 0.6 copy-start.9
  41.7 0.7 copy-start.7
  42.4 15.4 %all-to-all-start.1 = ((bf16[32,8,512]{2,1,0:T(8,128)(2,1)}), bf16[32,8,512]{2,1,0:T(8,128)(2,1)S(1)}, u32[]{:S(2)}, u32[]{:S(2)}) async-start(bf16[32,8,512]{2,1,0:T(8,128)(2,1)} %bitcast.34), calls=%async_computation.1 | async-start | bytes 524288 | tf_op jit(solution)/shard_map/all_to_all | solution.py:353
  47.4 16.5 %collective-permute-start.4 = (bf16[5,128,512]{2,1,0:T(8,128)(2,1)}, bf16[5,128,512]{2,1,0:T(8,128)(2,1)}, u32[]{:S(2)}, u32[]{:S(2)}) collective-permute-start(bf16[5,128,512]{2,1,0:T(8,128)(2,1)} %get-tuple-element.54), channel_id=1, source_target_pairs={{0,2},{1,3},{2,0},{3,1},{4,6},{5,7},{6,4},{7,5},{8,10},{9,11},{10,... | collective-permute-start | bytes 1966088 | tf_op jit(solution)/shard_map/ppermute | solution.py:344
  57.8 13.5 %copy-start.1 = (bf16[5,128,512]{2,1,0:T(8,128)(2,1)S(1)}, bf16[5,128,512]{2,1,0:T(8,128)(2,1)}, u32[]{:S(2)}) copy-start(bf16[5,128,512]{2,1,0:T(8,128)(2,1)} %get-tuple-element.59.refs_5_) | copy-start | bytes 1966084
  57.8 13.5 %copy-start.4 = (bf16[5,64,512]{2,1,0:T(8,128)(2,1)S(1)}, bf16[5,64,512]{2,1,0:T(8,128)(2,1)}, u32[]{:S(2)}) copy-start(bf16[5,64,512]{2,1,0:T(8,128)(2,1)} %get-tuple-element.60.refs_9_) | copy-start | bytes 983044
  57.9 13.5 %copy-start.6 = (f32[64,128]{1,0:T(8,128)S(1)}, f32[64,128]{1,0:T(8,128)}, u32[]{:S(2)}) copy-start(f32[64,128]{1,0:T(8,128)} %copy-done.5) | copy-start | bytes 98308
  57.9 6.1 %collective-permute-start.3 = (bf16[256,512]{1,0:T(8,128)(2,1)S(1)}, bf16[256,512]{1,0:T(8,128)(2,1)S(1)}, u32[]{:S(2)}, u32[]{:S(2)}) collective-permute-start(bf16[256,512]{1,0:T(8,128)(2,1)S(1)} %bitcast.28), channel_id=1, source_target_pairs={{0,4},{4,0},{1,5},{5,1},{2,6},{6,2},{3,7},{7,3},{8,12},{12,8},{9,1... | collective-permute-start | bytes 786440 | tf_op jit(solution)/shard_map/ppermute | solution.py:348
  65.7 5.1 %collective-permute-start.5 = (bf16[4,64,128]{2,1,0:T(8,128)(2,1)S(1)}, bf16[4,64,128]{2,1,0:T(8,128)(2,1)S(1)}, u32[]{:S(2)}, u32[]{:S(2)}) collective-permute-start(bf16[4,64,128]{2,1,0:T(8,128)(2,1)S(1)} %get-tuple-element.56), channel_id=1, source_target_pairs={{0,1},{1,2},{2,3},{3,0},{4,5},{5,6},{6,7},{7,4},{8,9},{9,10},{10,1... | collective-permute-start | bytes 196616 | tf_op jit(solution)/shard_map/ppermute | solution.py:344
  65.8 5.0 %collective-permute-start.6 = (bf16[4,64,128]{2,1,0:T(8,128)(2,1)S(1)}, bf16[4,64,128]{2,1,0:T(8,128)(2,1)S(1)}, u32[]{:S(2)}, u32[]{:S(2)}) collective-permute-start(bf16[4,64,128]{2,1,0:T(8,128)(2,1)S(1)} %get-tuple-element.57), channel_id=1, source_target_pairs={{0,2},{1,3},{2,0},{3,1},{4,6},{5,7},{6,4},{7,5},{8,10},{9,11},{10,... | collective-permute-start | bytes 196616 | tf_op jit(solution)/shard_map/ppermute | solution.py:344
  68.2 3.2 %collective-permute-start.7 = (bf16[4,64,128]{2,1,0:T(8,128)(2,1)S(1)}, bf16[4,64,128]{2,1,0:T(8,128)(2,1)S(1)}, u32[]{:S(2)}, u32[]{:S(2)}) collective-permute-start(bf16[4,64,128]{2,1,0:T(8,128)(2,1)S(1)} %get-tuple-element.58), channel_id=1, source_target_pairs={{0,3},{1,0},{2,1},{3,2},{4,7},{5,4},{6,5},{7,6},{8,11},{9,8},{10,9... | collective-permute-start | bytes 196616 | tf_op jit(solution)/shard_map/ppermute | solution.py:344
  74.2 38.6 %copy-start.10 = (f32[8,512]{1,0:T(8,128)S(1)}, f32[8,512]{1,0:T(8,128)}, u32[]{:S(2)}) copy-start(f32[8,512]{1,0:T(8,128)} %copy-done.9) | copy-start | bytes 49156
  74.3 3.8 %collective-permute-start.8 = (bf16[4,64,128]{2,1,0:T(8,128)(2,1)S(1)}, bf16[4,64,128]{2,1,0:T(8,128)(2,1)S(1)}, u32[]{:S(2)}, u32[]{:S(2)}) collective-permute-start(bf16[4,64,128]{2,1,0:T(8,128)(2,1)S(1)} %get-tuple-element.62), channel_id=1, source_target_pairs={{0,3},{1,0},{2,1},{3,2},{4,7},{5,4},{6,5},{7,6},{8,11},{9,8},{10,9... | collective-permute-start | bytes 196616 | tf_op jit(solution)/shard_map/ppermute | solution.py:344
  76.7 4.7 %collective-permute-start.9 = (bf16[4,64,128]{2,1,0:T(8,128)(2,1)S(1)}, bf16[4,64,128]{2,1,0:T(8,128)(2,1)S(1)}, u32[]{:S(2)}, u32[]{:S(2)}) collective-permute-start(bf16[4,64,128]{2,1,0:T(8,128)(2,1)S(1)} %get-tuple-element.63), channel_id=1, source_target_pairs={{0,2},{1,3},{2,0},{3,1},{4,6},{5,7},{6,4},{7,5},{8,10},{9,11},{10,... | collective-permute-start | bytes 196616 | tf_op jit(solution)/shard_map/ppermute | solution.py:344
  77.1 5.0 %collective-permute-start.10 = (bf16[4,64,128]{2,1,0:T(8,128)(2,1)S(1)}, bf16[4,64,128]{2,1,0:T(8,128)(2,1)S(1)}, u32[]{:S(2)}, u32[]{:S(2)}) collective-permute-start(bf16[4,64,128]{2,1,0:T(8,128)(2,1)S(1)} %get-tuple-element.64), channel_id=1, source_target_pairs={{0,1},{1,2},{2,3},{3,0},{4,5},{5,6},{6,7},{7,4},{8,9},{9,10},{10,1... | collective-permute-start | bytes 196616 | tf_op jit(solution)/shard_map/ppermute | solution.py:344
  83.5 7.0 %collective-permute-start.11 = (bf16[256,640]{1,0:T(8,128)(2,1)S(1)}, bf16[256,640]{1,0:T(8,128)(2,1)S(1)}, u32[]{:S(2)}, u32[]{:S(2)}) collective-permute-start(bf16[256,640]{1,0:T(8,128)(2,1)S(1)} %get-tuple-element.66), channel_id=1, source_target_pairs={{0,4},{4,0},{1,5},{5,1},{2,6},{6,2},{3,7},{7,3},{8,12},{12,8},{9,1... | collective-permute-start | bytes 983048 | tf_op jit(solution)/shard_map/ppermute | solution.py:348
  128.5 4.7 %collective-permute-start.12 = (bf16[256,512]{1,0:T(8,128)(2,1)S(1)}, bf16[256,512]{1,0:T(8,128)(2,1)S(1)}, u32[]{:S(2)}, u32[]{:S(2)}) collective-permute-start(bf16[256,512]{1,0:T(8,128)(2,1)S(1)} %bitcast.32), channel_id=1, source_target_pairs={{0,4},{4,0},{1,5},{5,1},{2,6},{6,2},{3,7},{7,3},{8,12},{12,8},{9,1... | collective-permute-start | bytes 786440 | tf_op jit(solution)/shard_map/ppermute | solution.py:348
  135.0 6.3 %collective-permute-start.13 = (bf16[4,64,128]{2,1,0:T(8,128)(2,1)S(1)}, bf16[4,64,128]{2,1,0:T(8,128)(2,1)S(1)}, u32[]{:S(2)}, u32[]{:S(2)}) collective-permute-start(bf16[4,64,128]{2,1,0:T(8,128)(2,1)S(1)} %get-tuple-element.72), channel_id=1, source_target_pairs={{0,1},{1,2},{2,3},{3,0},{4,5},{5,6},{6,7},{7,4},{8,9},{9,10},{10,1... | collective-permute-start | bytes 196616 | tf_op jit(solution)/shard_map/ppermute | solution.py:344
  135.1 6.3 %collective-permute-start.14 = (bf16[4,64,128]{2,1,0:T(8,128)(2,1)S(1)}, bf16[4,64,128]{2,1,0:T(8,128)(2,1)S(1)}, u32[]{:S(2)}, u32[]{:S(2)}) collective-permute-start(bf16[4,64,128]{2,1,0:T(8,128)(2,1)S(1)} %get-tuple-element.73), channel_id=1, source_target_pairs={{0,2},{1,3},{2,0},{3,1},{4,6},{5,7},{6,4},{7,5},{8,10},{9,11},{10,... | collective-permute-start | bytes 196616 | tf_op jit(solution)/shard_map/ppermute | solution.py:344
  136.6 4.8 %collective-permute-start.15 = (bf16[4,64,128]{2,1,0:T(8,128)(2,1)S(1)}, bf16[4,64,128]{2,1,0:T(8,128)(2,1)S(1)}, u32[]{:S(2)}, u32[]{:S(2)}) collective-permute-start(bf16[4,64,128]{2,1,0:T(8,128)(2,1)S(1)} %get-tuple-element.74), channel_id=1, source_target_pairs={{0,3},{1,0},{2,1},{3,2},{4,7},{5,4},{6,5},{7,6},{8,11},{9,8},{10,9... | collective-permute-start | bytes 196616 | tf_op jit(solution)/shard_map/ppermute | solution.py:344
  144.2 3.9 %collective-permute-start.16 = (bf16[4,64,128]{2,1,0:T(8,128)(2,1)S(1)}, bf16[4,64,128]{2,1,0:T(8,128)(2,1)S(1)}, u32[]{:S(2)}, u32[]{:S(2)}) collective-permute-start(bf16[4,64,128]{2,1,0:T(8,128)(2,1)S(1)} %get-tuple-element.77), channel_id=1, source_target_pairs={{0,3},{1,0},{2,1},{3,2},{4,7},{5,4},{6,5},{7,6},{8,11},{9,8},{10,9... | collective-permute-start | bytes 196616 | tf_op jit(solution)/shard_map/ppermute | solution.py:344
  146.7 4.7 %collective-permute-start.17 = (bf16[4,64,128]{2,1,0:T(8,128)(2,1)S(1)}, bf16[4,64,128]{2,1,0:T(8,128)(2,1)S(1)}, u32[]{:S(2)}, u32[]{:S(2)}) collective-permute-start(bf16[4,64,128]{2,1,0:T(8,128)(2,1)S(1)} %get-tuple-element.78), channel_id=1, source_target_pairs={{0,2},{1,3},{2,0},{3,1},{4,6},{5,7},{6,4},{7,5},{8,10},{9,11},{10,... | collective-permute-start | bytes 196616 | tf_op jit(solution)/shard_map/ppermute | solution.py:344
  146.9 5.0 %collective-permute-start.18 = (bf16[4,64,128]{2,1,0:T(8,128)(2,1)S(1)}, bf16[4,64,128]{2,1,0:T(8,128)(2,1)S(1)}, u32[]{:S(2)}, u32[]{:S(2)}) collective-permute-start(bf16[4,64,128]{2,1,0:T(8,128)(2,1)S(1)} %get-tuple-element.79), channel_id=1, source_target_pairs={{0,1},{1,2},{2,3},{3,0},{4,5},{5,6},{6,7},{7,4},{8,9},{9,10},{10,1... | collective-permute-start | bytes 196616 | tf_op jit(solution)/shard_map/ppermute | solution.py:344
  153.3 4.3 %collective-permute-start.19 = (bf16[256,640]{1,0:T(8,128)(2,1)S(1)}, bf16[256,640]{1,0:T(8,128)(2,1)S(1)}, u32[]{:S(2)}, u32[]{:S(2)}) collective-permute-start(bf16[256,640]{1,0:T(8,128)(2,1)S(1)} %get-tuple-element.81), channel_id=1, source_target_pairs={{0,4},{4,0},{1,5},{5,1},{2,6},{6,2},{3,7},{7,3},{8,12},{12,8},{9,1... | collective-permute-start | bytes 983048 | tf_op jit(solution)/shard_map/ppermute | solution.py:348
  190.6 4.7 %collective-permute-start.20 = (bf16[256,512]{1,0:T(8,128)(2,1)S(1)}, bf16[256,512]{1,0:T(8,128)(2,1)S(1)}, u32[]{:S(2)}, u32[]{:S(2)}) collective-permute-start(bf16[256,512]{1,0:T(8,128)(2,1)S(1)} %bitcast.30), channel_id=1, source_target_pairs={{0,4},{4,0},{1,5},{5,1},{2,6},{6,2},{3,7},{7,3},{8,12},{12,8},{9,1... | collective-permute-start | bytes 786440 | tf_op jit(solution)/shard_map/ppermute | solution.py:348
  196.2 4.8 %collective-permute-start.23 = (f32[64,128]{1,0:T(8,128)S(1)}, f32[64,128]{1,0:T(8,128)S(1)}, u32[]{:S(2)}, u32[]{:S(2)}) collective-permute-start(f32[64,128]{1,0:T(8,128)S(1)} %get-tuple-element.88.refs_8_.refs_6_), channel_id=1, source_target_pairs={{0,3},{1,0},{2,1},{3,2},{4,7},{5,4},{6,5},{7,6},{8,11},{9,8},{10,9... | collective-permute-start | bytes 98312 | tf_op jit(solution)/shard_map/ppermute | solution.py:344
  196.7 4.3 %collective-permute-start.22 = (f32[64,128]{1,0:T(8,128)S(1)}, f32[64,128]{1,0:T(8,128)S(1)}, u32[]{:S(2)}, u32[]{:S(2)}) collective-permute-start(f32[64,128]{1,0:T(8,128)S(1)} %get-tuple-element.88.refs_8_.refs_6_), channel_id=1, source_target_pairs={{0,2},{1,3},{2,0},{3,1},{4,6},{5,7},{6,4},{7,5},{8,10},{9,11},{10,... | collective-permute-start | bytes 98312 | tf_op jit(solution)/shard_map/ppermute | solution.py:344
  197.6 4.0 %collective-permute-start.21 = (f32[64,128]{1,0:T(8,128)S(1)}, f32[64,128]{1,0:T(8,128)S(1)}, u32[]{:S(2)}, u32[]{:S(2)}) collective-permute-start(f32[64,128]{1,0:T(8,128)S(1)} %get-tuple-element.88.refs_8_.refs_6_), channel_id=1, source_target_pairs={{0,1},{1,2},{2,3},{3,0},{4,5},{5,6},{6,7},{7,4},{8,9},{9,10},{10,1... | collective-permute-start | bytes 98312 | tf_op jit(solution)/shard_map/ppermute | solution.py:344

commit v3 on v2

--- a/solution.py
+++ b/solution.py
@@ -12,37 +12,35 @@
 EPSILON = 1e-06
 BF = jnp.bfloat16
 F32 = jnp.float32
-VMEM_LIMIT = 40 * 1024 * 1024
-START_LIMIT = 60 * 1024 * 1024
-
-
-def call(kernel, outs, scratch=(), name=None, limit=VMEM_LIMIT, anywhere=False, after=()):
-    space = pl.ANY if anywhere else pltpu.VMEM
+VMEM_LIMIT = 24 * 1024 * 1024
+LOADING_LIMIT = 52 * 1024 * 1024
+
+
+def call(kernel, outs, scratch=(), name=None, space=pltpu.VMEM, after=(), limit=VMEM_LIMIT):
     given = kernel
 
-    def run(places, *operands):
-        count = 1 + len(operands)
+    def run(*operands):
+        count = len(operands)
 
         def kernel(*refs):
-            given(*refs[:count], *refs[count + len(after) :])
+            core = lax.axis_index("c")
+            row = 32 * core + 4 * lax.axis_index("z") + lax.axis_index("y")
+            places = (lax.axis_index("x"), core, row)
+            given(places, *refs[:count], *refs[count + len(after) :])
 
         return pl.pallas_call(
             kernel,
             out_shape=[jax.ShapeDtypeStruct(out[0], out[1]) for out in outs],
-            in_specs=[pl.BlockSpec(memory_space=pltpu.SMEM)]
-            + [pl.BlockSpec(memory_space=space)] * len(operands)
+            in_specs=[pl.BlockSpec(memory_space=space)] * len(operands)
             + [pl.BlockSpec(memory_space=pl.ANY)] * len(after),
-            out_specs=[
-                pl.BlockSpec(memory_space=pl.ANY if len(out) > 2 else pltpu.VMEM)
-                for out in outs
-            ],
+            out_specs=[pl.BlockSpec(memory_space=pltpu.VMEM)] * len(outs),
             scratch_shapes=[
                 pltpu.VMEM(*entry) if isinstance(entry, tuple) else entry
                 for entry in scratch
             ],
             compiler_params=pltpu.CompilerParams(vmem_limit_bytes=limit),
             name=name,
-        )(places, *operands, *after)
+        )(*operands, *after)
 
     return run
 
@@ -98,8 +96,10 @@
     return lane_sum(jnp.where(diagonal(), row, 0.0))
 
 
-def write_partial(places, coeffs, right, squares, keep, send, field):
+def write_partial(places, coeffs, right, squares, keep, send, field, loads=None):
     for t in range(4):
+        if loads:
+            loads[t].wait()
         factors = jnp.concatenate([right[pair, t] for pair in range(10)], axis=0)
         value = dot(coeffs(t), factors)
         for i in range(8):
@@ -124,24 +124,23 @@
 
 
 def start_kernel(
-    places, left, right, observations, keep, send, one, two, three, own, own_field,
-    field, slots, left_here, right_here, values_here, in_sems, out_sems,
+    places, left, right, observations, keep, send, field, slots, left_here, right_here,
+    values_here, sems,
 ):
-    here = places[0]
     loads = []
     for pair in range(10):
         loads.append(
             (
                 pltpu.make_async_copy(
-                    observations.at[pair], values_here.at[pair], in_sems.at[2 * pair]
+                    observations.at[pair], values_here.at[pair], sems.at[2 * pair]
                 ),
                 pltpu.make_async_copy(
-                    left.at[pair], left_here.at[pair], in_sems.at[2 * pair + 1]
+                    left.at[pair], left_here.at[pair], sems.at[2 * pair + 1]
                 ),
             )
         )
     right_loads = [
-        pltpu.make_async_copy(right.at[:, t], right_here.at[:, t], in_sems.at[20 + t])
+        pltpu.make_async_copy(right.at[:, t], right_here.at[:, t], sems.at[20 + t])
         for t in range(4)
     ]
     for first, second in loads:
@@ -158,33 +157,36 @@
         total = total + sum(wide[:, 128 * i : 128 * i + 128] for i in range(8))
         second.wait()
         slots[pair] = dot_nt(values, left_here[pair]).astype(BF)
-    stores = []
+    squares = lane_sum(total)
+    write_partial(
+        places, in_slots(slots), right_here, squares, keep, send, field, right_loads
+    )
+
+
+def pack_kernel(places, left, values, own, one, two, three, own_field, sems):
+    here = places[0]
+    copies = []
+
+    def copy(source, target):
+        copies.append(pltpu.make_async_copy(source, target, sems.at[len(copies)]))
+        copies[-1].start()
+
     for step, out in enumerate((own, one, two, three)):
         peer = lax.rem(here + step, 4)
         half = pl.ds(pl.multiple_of(512 * lax.rem(peer, 2), 512), 512)
-        at = 5 * step
-        for unit in range(4):
-            source = left_here.at[2 * peer + unit // 2, :, pl.ds(512 * (unit % 2), 512)]
-            stores.append(
-                pltpu.make_async_copy(source, out.at[unit], out_sems.at[at + unit])
-            )
-        source = left_here.at[8 + peer // 2, :, half]
-        stores.append(pltpu.make_async_copy(source, out.at[4], out_sems.at[at + 4]))
+        for pair in range(2):
+            for part in range(2):
+                source = left.at[2 * peer + pair, :, pl.ds(512 * part, 512)]
+                copy(source, out.at[2 * pair + part])
+        copy(left.at[8 + peer // 2, :, half], out.at[4])
     half = pl.ds(pl.multiple_of(512 * lax.rem(here, 2), 512), 512)
-    for unit in range(4):
-        source = values_here.at[2 * here + unit // 2, :, pl.ds(512 * (unit % 2), 512)]
-        stores.append(
-            pltpu.make_async_copy(source, own_field.at[unit], out_sems.at[20 + unit])
-        )
-    source = values_here.at[8 + here // 2, :, half]
-    stores.append(pltpu.make_async_copy(source, own_field.at[4], out_sems.at[24]))
-    for store in stores:
-        store.start()
-    for load in right_loads:
-        load.wait()
-    write_partial(places, in_slots(slots), right_here, lane_sum(total), keep, send, field)
-    for store in stores:
-        store.wait()
+    for pair in range(2):
+        for part in range(2):
+            source = values.at[2 * here + pair, :, pl.ds(512 * part, 512)]
+            copy(source, own_field.at[2 * pair + part])
+    copy(values.at[8 + here // 2, :, half], own_field.at[4])
+    for started in copies:
+        started.wait()
 
 
 def back_kernel(places, right, own, one, two, three, keep, send, field, slots, shared):
@@ -326,12 +328,8 @@
 
 
 def direction_kernel(places, *refs):
-    data_lens, model_lens, squares, (third, last_direction, out) = (
-        refs[:3],
-        refs[3:5],
-        refs[5:9],
-        refs[9:],
-    )
+    data_lens, model_lens, squares = refs[:3], refs[3:5], refs[5:9]
+    third, last_direction, out = refs[9:]
     length = jnp.sqrt(sum(ref[:, 0:1] for ref in squares) + EPSILON)
     model_lens = [ref[:, 0:1] for ref in model_lens] + [length]
     steps, residual = scalars([ref[:, 0:1] for ref in data_lens], model_lens)
@@ -364,45 +362,46 @@
 
 
 def on_device(left, right, observations):
-    here = lax.axis_index("x")
-    core = lax.axis_index("c")
-    row = 32 * core + 4 * lax.axis_index("z") + lax.axis_index("y")
-    places = jnp.stack([here, core, row]).astype(jnp.int32)
     left = left.reshape(10, 128, 1024)
     right = right.reshape(10, 4, 32, 1024)
     observations = observations.reshape(10, 64, 1024)
 
     def sum_dp(keep, send, extra, before_shard=()):
-        whole = call(core_kernel, [((256, 640), BF)], name="core_sum")(
-            places, keep, swap_core(send)
-        )[0]
+        whole = call(core_kernel, [((256, 640), BF)], name="core_sum")(keep, swap_core(send))[0]
         raw, data_len, send = call(
             functools.partial(shard_kernel, not extra),
             [((8, 512), F32), COLUMN, ((256, 512), BF)],
             name="shard",
             after=before_shard,
-        )(places, exchange(whole), *extra)
+        )(exchange(whole), *extra)
         mine = exchange(send)
         return raw, data_len, mine, swap_core(mine)
 
-    keep, send, one, two, three, own, field = call(
+    keep, send = call(
         start_kernel,
-        PARTIAL + [((5, 128, 512), BF, True)] * 4 + [((5, 64, 512), BF, True)],
+        PARTIAL,
         PARTIAL_SCRATCH
         + [
             ((10, 128, 1024), BF),
             ((10, 4, 32, 1024), BF),
             ((10, 64, 1024), BF),
             pltpu.SemaphoreType.DMA((24,)),
-            pltpu.SemaphoreType.DMA((25,)),
         ],
         name="start",
-        limit=START_LIMIT,
-        anywhere=True,
-    )(places, left, right, observations)
+        space=pltpu.HBM,
+        limit=LOADING_LIMIT,
+    )(left, right, observations)
+    own, one, two, three, field = call(
+        pack_kernel,
+        [((5, 128, 512), BF)] * 4 + [((5, 64, 512), BF)],
+        [pltpu.SemaphoreType.DMA((25,))],
+        name="pack",
+        space=pltpu.HBM,
+        after=(send,),
+        limit=LOADING_LIMIT,
+    )(left, observations)
     one, two, three = shift(one, 1), shift(two, 2), shift(three, 3)
-    owned = [own, one, two, three]
-    raw, data_len, mine, other = sum_dp(keep, send, (), (one, three))
+    raw, data_len, mine, other = sum_dp(keep, send, (), (one, two, three))
     models, model_lens, data_lens = [], [], [data_len]
     for sweep in range(ITERS):
         model, *chunks = call(
@@ -410,8 +409,7 @@
             [MODEL] + CHUNKS,
             [((4, 512, 128), F32), ((10, 64, 128), BF)],
             name="forward",
-            after=(two,) if sweep == 0 else (),
-        )(places, mine, other, right)
+        )(mine, other, right)
         models.append(model)
         chunks = [chunks[0]] + [shift(chunks[step], step) for step in (1, 2, 3)]
         last = sweep == ITERS - 1
@@ -419,19 +417,19 @@
             functools.partial(data_kernel, last),
             [COLUMN] + CHUNKS + ([] if last else [((5, 64, 512), F32)]),
             name="data",
-        )(places, *chunks, *owned, field, data_lens[-1])
+        )(*chunks, own, one, two, three, field, data_lens[-1])
         model_lens.append(outs[0])
         field = None if last else outs[5]
         chunks = [outs[1]] + [shift(outs[1 + step], -step) for step in (1, 2, 3)]
         keep, send = call(
             back_kernel, PARTIAL, PARTIAL_SCRATCH + [((4, 64, 128), F32)], name="back"
-        )(places, right, *chunks)
+        )(right, *chunks)
         raw, data_len, mine, other = sum_dp(keep, send, (raw, model_lens[-1]))
         data_lens.append(data_len)
 
     model, squares = call(
         last_model_kernel, [MODEL, COLUMN], [((4, 512, 128), F32)], name="last_model"
-    )(places, mine, other)
+    )(mine, other)
     solve_after = (squares,)
     squares = [squares] + [shift(squares, step) for step in (1, 2, 3)]
     solved, residual, last_direction = call(
@@ -439,9 +437,9 @@
         [((4, 64, 1024), F32), COLUMN, ((4, 64, 1024), F32)],
         name="solve",
         after=solve_after,
-    )(places, *data_lens, *model_lens, *models)
+    )(*data_lens, *model_lens, *models)
     direction = call(direction_kernel, [((4, 64, 1024), F32)], name="direct")(
-        places, *data_lens, *model_lens, *squares, model, last_direction
+        *data_lens, *model_lens, *squares, model, last_direction
     )[0]
     return solved, direction, residual[:, 0]
 

time: 204 us -> 199 us (0.975)
  blocking collectives: 67.8 us -> 83.3 us
  starting transfers between devices: 57 us -> 49.2 us
  Pallas kernels: 29.2 us -> 24.2 us
  waiting for transfers between devices: 43.6 us -> 39 us
  local copies, waits for them, and re-layouts: 4.37 us -> 2.18 us
    all_to_all x2 -> x1, waiting for transfers between devices: 18.3 us -> 0.01 us  [exchange(): lax.all_to_all(value.reshape(32, 8, width), ('z', 'y'), split_axis=0, con...]
    all_to_all x4 -> x5, blocking collectives: 67.8 us -> 83.3 us  [exchange(): lax.all_to_all(value.reshape(32, 8, width), ('z', 'y'), split_axis=0, con...]
    ppermute x18, waiting for transfers between devices: 20.5 us -> 33 us  [shift(): return lax.ppermute(value, 'x', [(i, (i + step) % 4) for i in range(4)])]
    pallas_call x16 -> x17, Pallas kernels: 29.2 us -> 24.2 us  [run(): pl.pallas_call(kernel, out_shape=[jax.ShapeDtypeStruct(out[0], out[1]) fo...]
    ppermute x6, starting transfers between devices: 22.7 us -> 19.3 us  [swap_core(): return lax.ppermute(value, 'c', [(0, 1), (1, 0)])]
    all_to_all x2 -> x1, starting transfers between devices: 14.6 us -> 11.3 us  [exchange(): lax.all_to_all(value.reshape(32, 8, width), ('z', 'y'), split_axis=0, con...]
    unnamed x22 -> x12, local copies, waits for them, and re-layouts: 3.74 us -> 1.56 us
  transfers between devices with their start and end apart: 26 -> 25, of which waited for: 19 -> 18; matrix products, arithmetic and copies ran while one was open for 0% -> 0% of each run, Pallas kernels for 1% -> 2%
where the time goes in v3:
time: 199 us
  blocking collectives  83.3 us (42%)
  starting transfers between devices  49.2 us (25%)
  waiting for transfers between devices  39 us (20%)
  Pallas kernels  24.2 us (12%)
  local copies, waits for them, and re-layouts  2.18 us (1%)
    all_to_all x5, blocking collectives, exchange(): lax.all_to_all(value.reshape(32, 8, width), ('z', 'y'), split_axis=0, con...  83.3 us
    ppermute x18, waiting for transfers between devices, shift(): return lax.ppermute(value, 'x', [(i, (i + step) % 4) for i in range(4)])  33 us
    pallas_call x17, Pallas kernels, run(): pl.pallas_call(kernel, out_shape=[jax.ShapeDtypeStruct(out[0], out[1]) fo...  24.2 us
    ppermute x6, starting transfers between devices, swap_core(): return lax.ppermute(value, 'c', [(0, 1), (1, 0)])  19.3 us
    ppermute x18, starting transfers between devices, shift(): return lax.ppermute(value, 'x', [(i, (i + step) % 4) for i in range(4)])  18.7 us
    all_to_all x1, starting transfers between devices, exchange(): lax.all_to_all(value.reshape(32, 8, width), ('z', 'y'), split_axis=0, con...  11.3 us
    ppermute x6, waiting for transfers between devices, swap_core(): return lax.ppermute(value, 'c', [(0, 1), (1, 0)])  6 us
  transfers between devices with their start and end apart: 25, of which 18 were waited for; matrix products, arithmetic and copies ran while one was open for 0% of the time, Pallas kernels for 2%

profile of v3, /device:TPU:1, one launch (start us, length us, event | category | flops | bytes accessed | tf_op | source)
XLA Modules:
  0.0 198.7 jit_solution(5734770403790456648)
XLA Ops:
  0.6 5.6 %start.1 = (f32[256,640]{1,0:T(8,128)S(1)}, bf16[256,640]{1,0:T(8,128)(2,1)S(1)}) custom-call(bf16[10,128,1024]{2,1,0:T(8,128)(2,1)} %bitcast.34, bf16[10,4,32,1024]{3,2,1,0:T(8,128)(2,1)} %bitcast.15, bf16[10,64,1024]{2,1,0:T(8,128)(2,1)} %bitcast.36), custom_call_target="tpu_custom_call" | custom-call | tf_op jit(solution)/shard_map/start/pallas_call | solution.py:31
  6.2 3.3 %collective-permute-start = (bf16[256,640]{1,0:T(8,128)(2,1)S(1)}, bf16[256,640]{1,0:T(8,128)(2,1)S(1)}, u32[]{:S(2)}, u32[]{:S(2)}) collective-permute-start(bf16[256,640]{1,0:T(8,128)(2,1)S(1)} %get-tuple-element.49.refs_2_), channel_id=1, source_target_pairs={{0,4},{4,0},{1,5},{5,1},{2,6},{6,2},{3,7},{7,3},{8,12},{12,8},{9,1... | collective-permute-start | bytes 983048 | tf_op jit(solution)/shard_map/ppermute | solution.py:346
  9.6 3.3 %pack.1 = (bf16[5,128,512]{2,1,0:T(8,128)(2,1)S(1)}, bf16[5,128,512]{2,1,0:T(8,128)(2,1)}, bf16[5,128,512]{2,1,0:T(8,128)(2,1)}, bf16[5,128,512]{2,1,0:T(8,128)(2,1)}, bf16[5,64,512]{2,1,0:T(8,128)(2,1)S(1)}) custom-call(bf16[10,128,1024]{2,1,0:T(8,128)(2,1)} %bitcast.35, bf16[10,64,1024]{2,1,0:T(8,128)(2,1)} %bitcast.37, ...), custom_call_target="tpu_custom_call" | custom-call | tf_op jit(solution)/shard_map/pack/pallas_call | solution.py:31
  12.9 0.8 copy-done.1
  13.7 1.9 collective-permute-start.2
  15.6 1.2 collective-permute-start.3
  16.9 0.7 copy-done.3
  17.6 11.3 %all-to-all-start = ((bf16[32,8,640]{2,1,0:T(8,128)(2,1)}), bf16[32,8,640]{2,1,0:T(8,128)(2,1)}, u32[]{:S(2)}, u32[]{:S(2)}) async-start(bf16[32,8,640]{2,1,0:T(8,128)(2,1)} %bitcast.20), calls=%async_computation | async-start | bytes 655360 | tf_op jit(solution)/shard_map/all_to_all | solution.py:351
  28.9 16.6 %collective-permute-done.1.refs_1_.refs_5_ = bf16[5,128,512]{2,1,0:T(8,128)(2,1)S(1)} collective-permute-done((bf16[5,128,512]{2,1,0:T(8,128)(2,1)}, bf16[5,128,512]{2,1,0:T(8,128)(2,1)S(1)}, u32[]{:S(2)}, u32[]{:S(2)}) %collective-permute-start.1) | collective-permute-done | bytes 655392 | tf_op jit(solution)/shard_map/ppermute | solution.py:342
  45.5 0.4 collective-permute-done.3.refs_3_.refs_7_
  45.9 1.2 shard.3
  47.2 21.2 %all_to_all.30 = bf16[32,8,512]{2,1,0:T(8,128)(2,1)S(1)} all-to-all(bf16[32,8,512]{2,1,0:T(8,128)(2,1)S(1)} %bitcast.33), channel_id=1, replica_groups=mesh['z'=8,'y'=4,'c'=2,'x'=4] {'z','y'}, dimensions={0} | all-to-all | bytes 524288 | tf_op jit(solution)/shard_map/all_to_all | solution.py:351
  68.3 2.5 %collective-permute-start.4 = (bf16[256,512]{1,0:T(8,128)(2,1)S(1)}, bf16[256,512]{1,0:T(8,128)(2,1)S(1)}, u32[]{:S(2)}, u32[]{:S(2)}) collective-permute-start(bf16[256,512]{1,0:T(8,128)(2,1)S(1)} %bitcast.25), channel_id=1, source_target_pairs={{0,4},{4,0},{1,5},{5,1},{2,6},{6,2},{3,7},{7,3},{8,12},{12,8},{9,1... | collective-permute-start | bytes 786440 | tf_op jit(solution)/shard_map/ppermute | solution.py:346
  70.8 1.2 collective-permute-done.4.refs_1_
  71.9 1.2 forward.2
  73.2 1.0 collective-permute-start.5
  74.2 2.7 %collective-permute-start.6 = (bf16[4,64,128]{2,1,0:T(8,128)(2,1)S(1)}, bf16[4,64,128]{2,1,0:T(8,128)(2,1)S(1)}, u32[]{:S(2)}, u32[]{:S(2)}) collective-permute-start(bf16[4,64,128]{2,1,0:T(8,128)(2,1)S(1)} %get-tuple-element.57), channel_id=1, source_target_pairs={{0,2},{1,3},{2,0},{3,1},{4,6},{5,7},{6,4},{7,5},{8,10},{9,11},{10,... | collective-permute-start | bytes 196616 | tf_op jit(solution)/shard_map/ppermute | solution.py:342
  76.9 0.7 collective-permute-start.7
  77.6 2.2 %collective-permute-done.6.refs_2_ = bf16[4,64,128]{2,1,0:T(8,128)(2,1)S(1)} collective-permute-done((bf16[4,64,128]{2,1,0:T(8,128)(2,1)S(1)}, bf16[4,64,128]{2,1,0:T(8,128)(2,1)S(1)}, u32[]{:S(2)}, u32[]{:S(2)}) %collective-permute-start.6) | collective-permute-done | bytes 65568 | tf_op jit(solution)/shard_map/ppermute | solution.py:342
  79.8 0.5 collective-permute-done.7.refs_3_
  80.3 2.8 %data.2 = (f32[64,128]{1,0:T(8,128)S(1)}, bf16[4,64,128]{2,1,0:T(8,128)(2,1)S(1)}, bf16[4,64,128]{2,1,0:T(8,128)(2,1)S(1)}, bf16[4,64,128]{2,1,0:T(8,128)(2,1)S(...) custom-call(bf16[4,64,128]{2,1,0:T(8,128)(2,1)S(1)} %get-tuple-element.55.refs_0_, ...), custom_call_target="tpu_custom_call" | custom-call | tf_op jit(solution)/shard_map/data/pallas_call | solution.py:31
  83.1 2.2 %collective-permute-start.8 = (bf16[4,64,128]{2,1,0:T(8,128)(2,1)S(1)}, bf16[4,64,128]{2,1,0:T(8,128)(2,1)S(1)}, u32[]{:S(2)}, u32[]{:S(2)}) collective-permute-start(bf16[4,64,128]{2,1,0:T(8,128)(2,1)S(1)} %get-tuple-element.62), channel_id=1, source_target_pairs={{0,3},{1,0},{2,1},{3,2},{4,7},{5,4},{6,5},{7,6},{8,11},{9,8},{10,9... | collective-permute-start | bytes 196616 | tf_op jit(solution)/shard_map/ppermute | solution.py:342
  85.3 0.1 collective-permute-start.9
  85.4 0.6 collective-permute-start.10
  85.9 0.7 collective-permute-done.8.refs_2_
  86.6 3.4 %collective-permute-done.9.refs_3_ = bf16[4,64,128]{2,1,0:T(8,128)(2,1)S(1)} collective-permute-done((bf16[4,64,128]{2,1,0:T(8,128)(2,1)S(1)}, bf16[4,64,128]{2,1,0:T(8,128)(2,1)S(1)}, u32[]{:S(2)}, u32[]{:S(2)}) %collective-permute-start.9) | collective-permute-done | bytes 65568 | tf_op jit(solution)/shard_map/ppermute | solution.py:342
  90.0 0.4 collective-permute-done.10.refs_4_
  90.4 0.9 back.2
  91.3 3.3 %collective-permute-start.11 = (bf16[256,640]{1,0:T(8,128)(2,1)S(1)}, bf16[256,640]{1,0:T(8,128)(2,1)S(1)}, u32[]{:S(2)}, u32[]{:S(2)}) collective-permute-start(bf16[256,640]{1,0:T(8,128)(2,1)S(1)} %get-tuple-element.66), channel_id=1, source_target_pairs={{0,4},{4,0},{1,5},{5,1},{2,6},{6,2},{3,7},{7,3},{8,12},{12,8},{9,1... | collective-permute-start | bytes 983048 | tf_op jit(solution)/shard_map/ppermute | solution.py:346
  94.6 1.3 collective-permute-done.11.refs_1_
  96.0 16.1 %all_to_all.31 = bf16[32,8,640]{2,1,0:T(8,128)(2,1)S(1)} all-to-all(bf16[32,8,640]{2,1,0:T(8,128)(2,1)S(1)} %bitcast.21), channel_id=1, replica_groups=mesh['z'=8,'y'=4,'c'=2,'x'=4] {'z','y'}, dimensions={0} | all-to-all | bytes 655360 | tf_op jit(solution)/shard_map/all_to_all | solution.py:351
  112.1 0.2 shard.4
  112.3 15.0 %all_to_all.32 = bf16[32,8,512]{2,1,0:T(8,128)(2,1)S(1)} all-to-all(bf16[32,8,512]{2,1,0:T(8,128)(2,1)S(1)} %bitcast.31), channel_id=1, replica_groups=mesh['z'=8,'y'=4,'c'=2,'x'=4] {'z','y'}, dimensions={0} | all-to-all | bytes 524288 | tf_op jit(solution)/shard_map/all_to_all | solution.py:351
  127.3 3.5 %collective-permute-start.12 = (bf16[256,512]{1,0:T(8,128)(2,1)S(1)}, bf16[256,512]{1,0:T(8,128)(2,1)S(1)}, u32[]{:S(2)}, u32[]{:S(2)}) collective-permute-start(bf16[256,512]{1,0:T(8,128)(2,1)S(1)} %bitcast.27), channel_id=1, source_target_pairs={{0,4},{4,0},{1,5},{5,1},{2,6},{6,2},{3,7},{7,3},{8,12},{12,8},{9,1... | collective-permute-start | bytes 786440 | tf_op jit(solution)/shard_map/ppermute | solution.py:346
  130.8 1.2 collective-permute-done.12.refs_1_
  132.0 1.2 forward.3
  133.2 0.1 collective-permute-start.13
  133.3 1.4 collective-permute-start.14
  134.8 1.6 collective-permute-start.15
  136.4 3.1 %collective-permute-done.13.refs_1_ = bf16[4,64,128]{2,1,0:T(8,128)(2,1)S(1)} collective-permute-done((bf16[4,64,128]{2,1,0:T(8,128)(2,1)S(1)}, bf16[4,64,128]{2,1,0:T(8,128)(2,1)S(1)}, u32[]{:S(2)}, u32[]{:S(2)}) %collective-permute-start.13) | collective-permute-done | bytes 65568 | tf_op jit(solution)/shard_map/ppermute | solution.py:342
  139.6 2.8 %data.3 = (f32[64,128]{1,0:T(8,128)S(1)}, bf16[4,64,128]{2,1,0:T(8,128)(2,1)S(1)}, bf16[4,64,128]{2,1,0:T(8,128)(2,1)S(1)}, bf16[4,64,128]{2,1,0:T(8,128)(2,1)S(1)}, bf16[4,64,128]{2,1,0:T(8,128)(2,1)S(1)}) custom-call(bf16[4,64,128]{2,1,0:T(8,128)(2,1)S(1)} %get-tuple-element.71.refs_0_, bf16[4,64,128]{2,1,0:T(8,128)(2,1)S(1)} %collective-permute-done.13.refs_1_, ...), custom_call_target="tpu_custom_call" | custom-call | tf_op jit(solution)/shard_map/data/pallas_call | solution.py:31
  142.4 2.5 %collective-permute-start.16 = (bf16[4,64,128]{2,1,0:T(8,128)(2,1)S(1)}, bf16[4,64,128]{2,1,0:T(8,128)(2,1)S(1)}, u32[]{:S(2)}, u32[]{:S(2)}) collective-permute-start(bf16[4,64,128]{2,1,0:T(8,128)(2,1)S(1)} %get-tuple-element.77), channel_id=1, source_target_pairs={{0,3},{1,0},{2,1},{3,2},{4,7},{5,4},{6,5},{7,6},{8,11},{9,8},{10,9... | collective-permute-start | bytes 196616 | tf_op jit(solution)/shard_map/ppermute | solution.py:342
  144.9 0.2 collective-permute-start.17
  145.0 0.5 collective-permute-start.18
  145.5 0.7 collective-permute-done.16.refs_2_
  146.2 3.4 %collective-permute-done.17.refs_3_ = bf16[4,64,128]{2,1,0:T(8,128)(2,1)S(1)} collective-permute-done((bf16[4,64,128]{2,1,0:T(8,128)(2,1)S(1)}, bf16[4,64,128]{2,1,0:T(8,128)(2,1)S(1)}, u32[]{:S(2)}, u32[]{:S(2)}) %collective-permute-start.17) | collective-permute-done | bytes 65568 | tf_op jit(solution)/shard_map/ppermute | solution.py:342
  149.6 0.5 collective-permute-done.18.refs_4_
  150.1 0.9 back.3
  151.0 3.0 %collective-permute-start.19 = (bf16[256,640]{1,0:T(8,128)(2,1)S(1)}, bf16[256,640]{1,0:T(8,128)(2,1)S(1)}, u32[]{:S(2)}, u32[]{:S(2)}) collective-permute-start(bf16[256,640]{1,0:T(8,128)(2,1)S(1)} %get-tuple-element.81), channel_id=1, source_target_pairs={{0,4},{4,0},{1,5},{5,1},{2,6},{6,2},{3,7},{7,3},{8,12},{12,8},{9,1... | collective-permute-start | bytes 983048 | tf_op jit(solution)/shard_map/ppermute | solution.py:346
  154.0 1.3 collective-permute-done.19.refs_1_
  155.3 16.0 %all_to_all.33 = bf16[32,8,640]{2,1,0:T(8,128)(2,1)S(1)} all-to-all(bf16[32,8,640]{2,1,0:T(8,128)(2,1)S(1)} %bitcast.22), channel_id=1, replica_groups=mesh['z'=8,'y'=4,'c'=2,'x'=4] {'z','y'}, dimensions={0} | all-to-all | bytes 655360 | tf_op jit(solution)/shard_map/all_to_all | solution.py:351
  171.4 0.8 shard.5
  172.2 15.0 %all_to_all.34 = bf16[32,8,512]{2,1,0:T(8,128)(2,1)S(1)} all-to-all(bf16[32,8,512]{2,1,0:T(8,128)(2,1)S(1)} %bitcast.32), channel_id=1, replica_groups=mesh['z'=8,'y'=4,'c'=2,'x'=4] {'z','y'}, dimensions={0} | all-to-all | bytes 524288 | tf_op jit(solution)/shard_map/all_to_all | solution.py:351
  187.1 3.5 %collective-permute-start.20 = (bf16[256,512]{1,0:T(8,128)(2,1)S(1)}, bf16[256,512]{1,0:T(8,128)(2,1)S(1)}, u32[]{:S(2)}, u32[]{:S(2)}) collective-permute-start(bf16[256,512]{1,0:T(8,128)(2,1)S(1)} %bitcast.29), channel_id=1, source_target_pairs={{0,4},{4,0},{1,5},{5,1},{2,6},{6,2},{3,7},{7,3},{8,12},{12,8},{9,1... | collective-permute-start | bytes 786440 | tf_op jit(solution)/shard_map/ppermute | solution.py:346
  190.7 1.2 collective-permute-done.20.refs_1_
  191.8 0.4 last_model.1
  192.2 0.4 collective-permute-start.23
  192.6 0.9 collective-permute-start.22
  193.4 0.8 collective-permute-start.21
  194.2 1.4 solve.1
  195.6 0.6 slice_reduce_fusion
  196.2 0.6 collective-permute-done.22.refs_7_
  196.9 0.6 collective-permute-done.21.refs_6_
  197.5 1.2 direct.1
  (21 shorter events, 0.2 us)
Async XLA Ops:
  6.2 10.6 %collective-permute-start = (bf16[256,640]{1,0:T(8,128)(2,1)S(1)}, bf16[256,640]{1,0:T(8,128)(2,1)S(1)}, u32[]{:S(2)}, u32[]{:S(2)}) collective-permute-start(bf16[256,640]{1,0:T(8,128)(2,1)S(1)} %get-tuple-element.49.refs_2_), channel_id=1, source_target_pairs={{0,4},{4,0},{1,5},{5,1},{2,6},{6,2},{3,7},{7,3},{8,12},{12,8},{9,1... | collective-permute-start | bytes 983048 | tf_op jit(solution)/shard_map/ppermute | solution.py:346
  12.9 0.8 copy-start.1
  13.7 3.2 %copy-start.4 = (bf16[5,64,512]{2,1,0:T(8,128)(2,1)}, bf16[5,64,512]{2,1,0:T(8,128)(2,1)S(1)}, u32[]{:S(2)}) copy-start(bf16[5,64,512]{2,1,0:T(8,128)(2,1)S(1)} %get-tuple-element.60.refs_8_) | copy-start | bytes 983044
  13.7 58.2 %copy-start = (bf16[2,5,4,32,1024]{4,3,2,1,0:T(8,128)(2,1)S(1)}, bf16[2,5,4,32,1024]{4,3,2,1,0:T(8,128)(2,1)}, u32[]{:S(2)}) copy-start(bf16[2,5,4,32,1024]{4,3,2,1,0:T(8,128)(2,1)} %param.4) | copy-start | bytes 7864324
  13.7 31.8 %collective-permute-start.1 = (bf16[5,128,512]{2,1,0:T(8,128)(2,1)}, bf16[5,128,512]{2,1,0:T(8,128)(2,1)S(1)}, u32[]{:S(2)}, u32[]{:S(2)}) collective-permute-start(bf16[5,128,512]{2,1,0:T(8,128)(2,1)} %get-tuple-element.50), channel_id=1, source_target_pairs={{0,1},{1,2},{2,3},{3,0},{4,5},{5,6},{6,7},{7,4},{8,9},{9,10},{10,1... | collective-permute-start | bytes 1966088 | tf_op jit(solution)/shard_map/ppermute | solution.py:342
  13.7 31.8 %collective-permute-start.2 = (bf16[5,128,512]{2,1,0:T(8,128)(2,1)}, bf16[5,128,512]{2,1,0:T(8,128)(2,1)}, u32[]{:S(2)}, u32[]{:S(2)}) collective-permute-start(bf16[5,128,512]{2,1,0:T(8,128)(2,1)} %get-tuple-element.51), channel_id=1, source_target_pairs={{0,2},{1,3},{2,0},{3,1},{4,6},{5,7},{6,4},{7,5},{8,10},{9,11},{10,... | collective-permute-start | bytes 1966088 | tf_op jit(solution)/shard_map/ppermute | solution.py:342
  15.6 30.3 %collective-permute-start.3 = (bf16[5,128,512]{2,1,0:T(8,128)(2,1)}, bf16[5,128,512]{2,1,0:T(8,128)(2,1)}, u32[]{:S(2)}, u32[]{:S(2)}) collective-permute-start(bf16[5,128,512]{2,1,0:T(8,128)(2,1)} %get-tuple-element.52), channel_id=1, source_target_pairs={{0,3},{1,0},{2,1},{3,2},{4,7},{5,4},{6,5},{7,6},{8,11},{9,8},{10,9... | collective-permute-start | bytes 1966088 | tf_op jit(solution)/shard_map/ppermute | solution.py:342
  16.9 0.7 copy-start.3
  17.6 28.3 %all-to-all-start = ((bf16[32,8,640]{2,1,0:T(8,128)(2,1)}), bf16[32,8,640]{2,1,0:T(8,128)(2,1)}, u32[]{:S(2)}, u32[]{:S(2)}) async-start(bf16[32,8,640]{2,1,0:T(8,128)(2,1)} %bitcast.20), calls=%async_computation | async-start | bytes 655360 | tf_op jit(solution)/shard_map/all_to_all | solution.py:351
  45.9 34.4 %copy-start.2 = (bf16[5,128,512]{2,1,0:T(8,128)(2,1)S(1)}, bf16[5,128,512]{2,1,0:T(8,128)(2,1)}, u32[]{:S(2)}) copy-start(bf16[5,128,512]{2,1,0:T(8,128)(2,1)} %copy-done.1) | copy-start | bytes 1966084
  45.9 34.4 %copy-start.5 = (bf16[5,64,512]{2,1,0:T(8,128)(2,1)S(1)}, bf16[5,64,512]{2,1,0:T(8,128)(2,1)}, u32[]{:S(2)}) copy-start(bf16[5,64,512]{2,1,0:T(8,128)(2,1)} %copy-done.4) | copy-start | bytes 983044
  68.3 3.6 %collective-permute-start.4 = (bf16[256,512]{1,0:T(8,128)(2,1)S(1)}, bf16[256,512]{1,0:T(8,128)(2,1)S(1)}, u32[]{:S(2)}, u32[]{:S(2)}) collective-permute-start(bf16[256,512]{1,0:T(8,128)(2,1)S(1)} %bitcast.25), channel_id=1, source_target_pairs={{0,4},{4,0},{1,5},{5,1},{2,6},{6,2},{3,7},{7,3},{8,12},{12,8},{9,1... | collective-permute-start | bytes 786440 | tf_op jit(solution)/shard_map/ppermute | solution.py:346
  73.2 4.4 %collective-permute-start.5 = (bf16[4,64,128]{2,1,0:T(8,128)(2,1)S(1)}, bf16[4,64,128]{2,1,0:T(8,128)(2,1)S(1)}, u32[]{:S(2)}, u32[]{:S(2)}) collective-permute-start(bf16[4,64,128]{2,1,0:T(8,128)(2,1)S(1)} %get-tuple-element.56), channel_id=1, source_target_pairs={{0,1},{1,2},{2,3},{3,0},{4,5},{5,6},{6,7},{7,4},{8,9},{9,10},{10,1... | collective-permute-start | bytes 196616 | tf_op jit(solution)/shard_map/ppermute | solution.py:342
  74.2 5.6 %collective-permute-start.6 = (bf16[4,64,128]{2,1,0:T(8,128)(2,1)S(1)}, bf16[4,64,128]{2,1,0:T(8,128)(2,1)S(1)}, u32[]{:S(2)}, u32[]{:S(2)}) collective-permute-start(bf16[4,64,128]{2,1,0:T(8,128)(2,1)S(1)} %get-tuple-element.57), channel_id=1, source_target_pairs={{0,2},{1,3},{2,0},{3,1},{4,6},{5,7},{6,4},{7,5},{8,10},{9,11},{10,... | collective-permute-start | bytes 196616 | tf_op jit(solution)/shard_map/ppermute | solution.py:342
  76.9 3.4 %collective-permute-start.7 = (bf16[4,64,128]{2,1,0:T(8,128)(2,1)S(1)}, bf16[4,64,128]{2,1,0:T(8,128)(2,1)S(1)}, u32[]{:S(2)}, u32[]{:S(2)}) collective-permute-start(bf16[4,64,128]{2,1,0:T(8,128)(2,1)S(1)} %get-tuple-element.58), channel_id=1, source_target_pairs={{0,3},{1,0},{2,1},{3,2},{4,7},{5,4},{6,5},{7,6},{8,11},{9,8},{10,9... | collective-permute-start | bytes 196616 | tf_op jit(solution)/shard_map/ppermute | solution.py:342
  83.1 3.5 %collective-permute-start.8 = (bf16[4,64,128]{2,1,0:T(8,128)(2,1)S(1)}, bf16[4,64,128]{2,1,0:T(8,128)(2,1)S(1)}, u32[]{:S(2)}, u32[]{:S(2)}) collective-permute-start(bf16[4,64,128]{2,1,0:T(8,128)(2,1)S(1)} %get-tuple-element.62), channel_id=1, source_target_pairs={{0,3},{1,0},{2,1},{3,2},{4,7},{5,4},{6,5},{7,6},{8,11},{9,8},{10,9... | collective-permute-start | bytes 196616 | tf_op jit(solution)/shard_map/ppermute | solution.py:342
  85.3 4.7 %collective-permute-start.9 = (bf16[4,64,128]{2,1,0:T(8,128)(2,1)S(1)}, bf16[4,64,128]{2,1,0:T(8,128)(2,1)S(1)}, u32[]{:S(2)}, u32[]{:S(2)}) collective-permute-start(bf16[4,64,128]{2,1,0:T(8,128)(2,1)S(1)} %get-tuple-element.63), channel_id=1, source_target_pairs={{0,2},{1,3},{2,0},{3,1},{4,6},{5,7},{6,4},{7,5},{8,10},{9,11},{10,... | collective-permute-start | bytes 196616 | tf_op jit(solution)/shard_map/ppermute | solution.py:342
  85.4 5.0 %collective-permute-start.10 = (bf16[4,64,128]{2,1,0:T(8,128)(2,1)S(1)}, bf16[4,64,128]{2,1,0:T(8,128)(2,1)S(1)}, u32[]{:S(2)}, u32[]{:S(2)}) collective-permute-start(bf16[4,64,128]{2,1,0:T(8,128)(2,1)S(1)} %get-tuple-element.64), channel_id=1, source_target_pairs={{0,1},{1,2},{2,3},{3,0},{4,5},{5,6},{6,7},{7,4},{8,9},{9,10},{10,1... | collective-permute-start | bytes 196616 | tf_op jit(solution)/shard_map/ppermute | solution.py:342
  91.3 4.6 %collective-permute-start.11 = (bf16[256,640]{1,0:T(8,128)(2,1)S(1)}, bf16[256,640]{1,0:T(8,128)(2,1)S(1)}, u32[]{:S(2)}, u32[]{:S(2)}) collective-permute-start(bf16[256,640]{1,0:T(8,128)(2,1)S(1)} %get-tuple-element.66), channel_id=1, source_target_pairs={{0,4},{4,0},{1,5},{5,1},{2,6},{6,2},{3,7},{7,3},{8,12},{12,8},{9,1... | collective-permute-start | bytes 983048 | tf_op jit(solution)/shard_map/ppermute | solution.py:346
  127.3 4.7 %collective-permute-start.12 = (bf16[256,512]{1,0:T(8,128)(2,1)S(1)}, bf16[256,512]{1,0:T(8,128)(2,1)S(1)}, u32[]{:S(2)}, u32[]{:S(2)}) collective-permute-start(bf16[256,512]{1,0:T(8,128)(2,1)S(1)} %bitcast.27), channel_id=1, source_target_pairs={{0,4},{4,0},{1,5},{5,1},{2,6},{6,2},{3,7},{7,3},{8,12},{12,8},{9,1... | collective-permute-start | bytes 786440 | tf_op jit(solution)/shard_map/ppermute | solution.py:346
  133.2 6.3 %collective-permute-start.13 = (bf16[4,64,128]{2,1,0:T(8,128)(2,1)S(1)}, bf16[4,64,128]{2,1,0:T(8,128)(2,1)S(1)}, u32[]{:S(2)}, u32[]{:S(2)}) collective-permute-start(bf16[4,64,128]{2,1,0:T(8,128)(2,1)S(1)} %get-tuple-element.72), channel_id=1, source_target_pairs={{0,1},{1,2},{2,3},{3,0},{4,5},{5,6},{6,7},{7,4},{8,9},{9,10},{10,1... | collective-permute-start | bytes 196616 | tf_op jit(solution)/shard_map/ppermute | solution.py:342
  133.3 6.3 %collective-permute-start.14 = (bf16[4,64,128]{2,1,0:T(8,128)(2,1)S(1)}, bf16[4,64,128]{2,1,0:T(8,128)(2,1)S(1)}, u32[]{:S(2)}, u32[]{:S(2)}) collective-permute-start(bf16[4,64,128]{2,1,0:T(8,128)(2,1)S(1)} %get-tuple-element.73), channel_id=1, source_target_pairs={{0,2},{1,3},{2,0},{3,1},{4,6},{5,7},{6,4},{7,5},{8,10},{9,11},{10,... | collective-permute-start | bytes 196616 | tf_op jit(solution)/shard_map/ppermute | solution.py:342
  134.8 4.8 %collective-permute-start.15 = (bf16[4,64,128]{2,1,0:T(8,128)(2,1)S(1)}, bf16[4,64,128]{2,1,0:T(8,128)(2,1)S(1)}, u32[]{:S(2)}, u32[]{:S(2)}) collective-permute-start(bf16[4,64,128]{2,1,0:T(8,128)(2,1)S(1)} %get-tuple-element.74), channel_id=1, source_target_pairs={{0,3},{1,0},{2,1},{3,2},{4,7},{5,4},{6,5},{7,6},{8,11},{9,8},{10,9... | collective-permute-start | bytes 196616 | tf_op jit(solution)/shard_map/ppermute | solution.py:342
  142.4 3.8 %collective-permute-start.16 = (bf16[4,64,128]{2,1,0:T(8,128)(2,1)S(1)}, bf16[4,64,128]{2,1,0:T(8,128)(2,1)S(1)}, u32[]{:S(2)}, u32[]{:S(2)}) collective-permute-start(bf16[4,64,128]{2,1,0:T(8,128)(2,1)S(1)} %get-tuple-element.77), channel_id=1, source_target_pairs={{0,3},{1,0},{2,1},{3,2},{4,7},{5,4},{6,5},{7,6},{8,11},{9,8},{10,9... | collective-permute-start | bytes 196616 | tf_op jit(solution)/shard_map/ppermute | solution.py:342
  144.9 4.7 %collective-permute-start.17 = (bf16[4,64,128]{2,1,0:T(8,128)(2,1)S(1)}, bf16[4,64,128]{2,1,0:T(8,128)(2,1)S(1)}, u32[]{:S(2)}, u32[]{:S(2)}) collective-permute-start(bf16[4,64,128]{2,1,0:T(8,128)(2,1)S(1)} %get-tuple-element.78), channel_id=1, source_target_pairs={{0,2},{1,3},{2,0},{3,1},{4,6},{5,7},{6,4},{7,5},{8,10},{9,11},{10,... | collective-permute-start | bytes 196616 | tf_op jit(solution)/shard_map/ppermute | solution.py:342
  145.0 5.0 %collective-permute-start.18 = (bf16[4,64,128]{2,1,0:T(8,128)(2,1)S(1)}, bf16[4,64,128]{2,1,0:T(8,128)(2,1)S(1)}, u32[]{:S(2)}, u32[]{:S(2)}) collective-permute-start(bf16[4,64,128]{2,1,0:T(8,128)(2,1)S(1)} %get-tuple-element.79), channel_id=1, source_target_pairs={{0,1},{1,2},{2,3},{3,0},{4,5},{5,6},{6,7},{7,4},{8,9},{9,10},{10,1... | collective-permute-start | bytes 196616 | tf_op jit(solution)/shard_map/ppermute | solution.py:342
  151.0 4.3 %collective-permute-start.19 = (bf16[256,640]{1,0:T(8,128)(2,1)S(1)}, bf16[256,640]{1,0:T(8,128)(2,1)S(1)}, u32[]{:S(2)}, u32[]{:S(2)}) collective-permute-start(bf16[256,640]{1,0:T(8,128)(2,1)S(1)} %get-tuple-element.81), channel_id=1, source_target_pairs={{0,4},{4,0},{1,5},{5,1},{2,6},{6,2},{3,7},{7,3},{8,12},{12,8},{9,1... | collective-permute-start | bytes 983048 | tf_op jit(solution)/shard_map/ppermute | solution.py:346
  187.1 4.7 %collective-permute-start.20 = (bf16[256,512]{1,0:T(8,128)(2,1)S(1)}, bf16[256,512]{1,0:T(8,128)(2,1)S(1)}, u32[]{:S(2)}, u32[]{:S(2)}) collective-permute-start(bf16[256,512]{1,0:T(8,128)(2,1)S(1)} %bitcast.29), channel_id=1, source_target_pairs={{0,4},{4,0},{1,5},{5,1},{2,6},{6,2},{3,7},{7,3},{8,12},{12,8},{9,1... | collective-permute-start | bytes 786440 | tf_op jit(solution)/shard_map/ppermute | solution.py:346
  192.2 4.0 %collective-permute-start.23 = (f32[64,128]{1,0:T(8,128)S(1)}, f32[64,128]{1,0:T(8,128)S(1)}, u32[]{:S(2)}, u32[]{:S(2)}) collective-permute-start(f32[64,128]{1,0:T(8,128)S(1)} %get-tuple-element.88.refs_7_.refs_5_), channel_id=1, source_target_pairs={{0,3},{1,0},{2,1},{3,2},{4,7},{5,4},{6,5},{7,6},{8,11},{9,8},{10,9... | collective-permute-start | bytes 98312 | tf_op jit(solution)/shard_map/ppermute | solution.py:342
  192.6 4.3 %collective-permute-start.22 = (f32[64,128]{1,0:T(8,128)S(1)}, f32[64,128]{1,0:T(8,128)S(1)}, u32[]{:S(2)}, u32[]{:S(2)}) collective-permute-start(f32[64,128]{1,0:T(8,128)S(1)} %get-tuple-element.88.refs_7_.refs_5_), channel_id=1, source_target_pairs={{0,2},{1,3},{2,0},{3,1},{4,6},{5,7},{6,4},{7,5},{8,10},{9,11},{10,... | collective-permute-start | bytes 98312 | tf_op jit(solution)/shard_map/ppermute | solution.py:342
  193.4 4.0 %collective-permute-start.21 = (f32[64,128]{1,0:T(8,128)S(1)}, f32[64,128]{1,0:T(8,128)S(1)}, u32[]{:S(2)}, u32[]{:S(2)}) collective-permute-start(f32[64,128]{1,0:T(8,128)S(1)} %get-tuple-element.88.refs_7_.refs_5_), channel_id=1, source_target_pairs={{0,1},{1,2},{2,3},{3,0},{4,5},{5,6},{6,7},{7,4},{8,9},{9,10},{10,1... | collective-permute-start | bytes 98312 | tf_op jit(solution)/shard_map/ppermute | solution.py:342

commit v4 on v3

--- a/solution.py
+++ b/solution.py
@@ -12,11 +12,10 @@
 EPSILON = 1e-06
 BF = jnp.bfloat16
 F32 = jnp.float32
-VMEM_LIMIT = 24 * 1024 * 1024
-LOADING_LIMIT = 52 * 1024 * 1024
-
-
-def call(kernel, outs, scratch=(), name=None, space=pltpu.VMEM, after=(), limit=VMEM_LIMIT):
+VMEM_LIMIT = 20 * 1024 * 1024
+
+
+def call(kernel, outs, scratch=(), name=None, after=()):
     given = kernel
 
     def run(*operands):
@@ -31,14 +30,14 @@
         return pl.pallas_call(
             kernel,
             out_shape=[jax.ShapeDtypeStruct(out[0], out[1]) for out in outs],
-            in_specs=[pl.BlockSpec(memory_space=space)] * len(operands)
+            in_specs=[pl.BlockSpec(memory_space=pltpu.VMEM)] * len(operands)
             + [pl.BlockSpec(memory_space=pl.ANY)] * len(after),
             out_specs=[pl.BlockSpec(memory_space=pltpu.VMEM)] * len(outs),
             scratch_shapes=[
                 pltpu.VMEM(*entry) if isinstance(entry, tuple) else entry
                 for entry in scratch
             ],
-            compiler_params=pltpu.CompilerParams(vmem_limit_bytes=limit),
+            compiler_params=pltpu.CompilerParams(vmem_limit_bytes=VMEM_LIMIT),
             name=name,
         )(*operands, *after)
 
@@ -96,10 +95,8 @@
     return lane_sum(jnp.where(diagonal(), row, 0.0))
 
 
-def write_partial(places, coeffs, right, squares, keep, send, field, loads=None):
+def write_partial(places, coeffs, right, squares, keep, send, field):
     for t in range(4):
-        if loads:
-            loads[t].wait()
         factors = jnp.concatenate([right[pair, t] for pair in range(10)], axis=0)
         value = dot(coeffs(t), factors)
         for i in range(8):
@@ -123,70 +120,32 @@
     )
 
 
-def start_kernel(
-    places, left, right, observations, keep, send, field, slots, left_here, right_here,
-    values_here, sems,
-):
-    loads = []
+def start_kernel(places, left, observations, slots, squares):
+    total = jnp.zeros((64, 128), F32)
     for pair in range(10):
-        loads.append(
-            (
-                pltpu.make_async_copy(
-                    observations.at[pair], values_here.at[pair], sems.at[2 * pair]
-                ),
-                pltpu.make_async_copy(
-                    left.at[pair], left_here.at[pair], sems.at[2 * pair + 1]
-                ),
-            )
-        )
-    right_loads = [
-        pltpu.make_async_copy(right.at[:, t], right_here.at[:, t], sems.at[20 + t])
-        for t in range(4)
-    ]
-    for first, second in loads:
-        first.start()
-        second.start()
-    for load in right_loads:
-        load.start()
-    total = jnp.zeros((64, 128), F32)
-    for pair, (first, second) in enumerate(loads):
-        first.wait()
-        values = values_here[pair]
+        values = observations[pair]
         wide = values.astype(F32)
         wide = wide * wide
         total = total + sum(wide[:, 128 * i : 128 * i + 128] for i in range(8))
-        second.wait()
-        slots[pair] = dot_nt(values, left_here[pair]).astype(BF)
-    squares = lane_sum(total)
-    write_partial(
-        places, in_slots(slots), right_here, squares, keep, send, field, right_loads
-    )
-
-
-def pack_kernel(places, left, values, own, one, two, three, own_field, sems):
-    here = places[0]
-    copies = []
-
-    def copy(source, target):
-        copies.append(pltpu.make_async_copy(source, target, sems.at[len(copies)]))
-        copies[-1].start()
-
-    for step, out in enumerate((own, one, two, three)):
-        peer = lax.rem(here + step, 4)
-        half = pl.ds(pl.multiple_of(512 * lax.rem(peer, 2), 512), 512)
-        for pair in range(2):
-            for part in range(2):
-                source = left.at[2 * peer + pair, :, pl.ds(512 * part, 512)]
-                copy(source, out.at[2 * pair + part])
-        copy(left.at[8 + peer // 2, :, half], out.at[4])
-    half = pl.ds(pl.multiple_of(512 * lax.rem(here, 2), 512), 512)
-    for pair in range(2):
-        for part in range(2):
-            source = values.at[2 * here + pair, :, pl.ds(512 * part, 512)]
-            copy(source, own_field.at[2 * pair + part])
-    copy(values.at[8 + here // 2, :, half], own_field.at[4])
-    for started in copies:
-        started.wait()
+        slots[pair] = dot_nt(values, left[pair]).astype(BF)
+    squares[...] = jnp.broadcast_to(lane_sum(total), (64, 128))
+
+
+def first_back_kernel(places, right, slots, squares, keep, send, field):
+    write_partial(places, in_slots(slots), right, squares[:, 0:1], keep, send, field)
+
+
+def pack_kernel(steps, places, left, *outs):
+    for step, out in zip(steps, outs):
+        for unit in range(5):
+            out[unit] = unit_of(left, lax.rem(places[0] + step, 4), unit)
+
+
+def unit_of(ref, owner, unit):
+    if unit < 4:
+        return ref[2 * owner + unit // 2, :, 512 * (unit % 2) : 512 * (unit % 2) + 512]
+    half = pl.ds(pl.multiple_of(512 * lax.rem(owner, 2), 512), 512)
+    return ref[8 + owner // 2, :, half]
 
 
 def back_kernel(places, right, own, one, two, three, keep, send, field, slots, shared):
@@ -260,7 +219,7 @@
 
 
 def data_kernel(last, places, *refs):
-    coeffs, left, (field, data_len), refs = refs[:4], refs[4:8], refs[8:10], refs[10:]
+    coeffs, blocks, (left, field, data_len), refs = refs[:4], refs[4:7], refs[7:10], refs[10:]
     model_len, outs = refs[0], refs[1:5]
     squares = sum(lane_sum(chunk[3].astype(F32)) for chunk in coeffs)
     length = jnp.sqrt(squares + EPSILON)
@@ -272,8 +231,10 @@
         given = jnp.concatenate([chunk[i] for chunk in coeffs], axis=1)
         back = None
         for unit in range(2 * i, min(2 * i + 2, 5)):
-            factors = jnp.concatenate([block[unit] for block in left], axis=0)
-            value = dot(given, factors) * inverse - ratio * field[unit].astype(F32)
+            factors = [unit_of(left, places[0], unit)] + [block[unit] for block in blocks]
+            factors = jnp.concatenate(factors, axis=0)
+            before = field[unit] if last else unit_of(field, places[0], unit).astype(F32)
+            value = dot(given, factors) * inverse - ratio * before
             if not last:
                 refs[5][unit] = value
             term = dot_nt(value.astype(BF), factors)
@@ -366,8 +327,7 @@
     right = right.reshape(10, 4, 32, 1024)
     observations = observations.reshape(10, 64, 1024)
 
-    def sum_dp(keep, send, extra, before_shard=()):
-        whole = call(core_kernel, [((256, 640), BF)], name="core_sum")(keep, swap_core(send))[0]
+    def sum_dp(whole, extra, before_shard=()):
         raw, data_len, send = call(
             functools.partial(shard_kernel, not extra),
             [((8, 512), F32), COLUMN, ((256, 512), BF)],
@@ -377,31 +337,25 @@
         mine = exchange(send)
         return raw, data_len, mine, swap_core(mine)
 
-    keep, send = call(
-        start_kernel,
-        PARTIAL,
-        PARTIAL_SCRATCH
-        + [
-            ((10, 128, 1024), BF),
-            ((10, 4, 32, 1024), BF),
-            ((10, 64, 1024), BF),
-            pltpu.SemaphoreType.DMA((24,)),
-        ],
-        name="start",
-        space=pltpu.HBM,
-        limit=LOADING_LIMIT,
-    )(left, right, observations)
-    own, one, two, three, field = call(
-        pack_kernel,
-        [((5, 128, 512), BF)] * 4 + [((5, 64, 512), BF)],
-        [pltpu.SemaphoreType.DMA((25,))],
-        name="pack",
-        space=pltpu.HBM,
-        after=(send,),
-        limit=LOADING_LIMIT,
+    slots, squares = call(
+        start_kernel, [((10, 64, 128), BF), COLUMN], name="start"
     )(left, observations)
-    one, two, three = shift(one, 1), shift(two, 2), shift(three, 3)
-    raw, data_len, mine, other = sum_dp(keep, send, (), (one, two, three))
+    keep, send = call(first_back_kernel, PARTIAL, PARTIAL_SCRATCH[:1], name="start_sum")(
+        right, slots, squares
+    )
+    block = ((5, 128, 512), BF)
+    one, three = call(
+        functools.partial(pack_kernel, (1, 3)), [block] * 2, name="pack", after=(send,)
+    )(left)
+    one, three = shift(one, 1), shift(three, 3)
+    two = call(
+        functools.partial(pack_kernel, (2,)), [block], name="pack_two", after=(one, three)
+    )(left)[0]
+    blocks = [one, shift(two, 2), three]
+    whole = call(core_kernel, [((256, 640), BF)], name="core_sum")(
+        keep, swap_core(send)
+    )[0]
+    raw, data_len, mine, other = sum_dp(whole, (), ())
     models, model_lens, data_lens = [], [], [data_len]
     for sweep in range(ITERS):
         model, *chunks = call(
@@ -409,6 +363,7 @@
             [MODEL] + CHUNKS,
             [((4, 512, 128), F32), ((10, 64, 128), BF)],
             name="forward",
+            after=() if sweep == 0 else (),
         )(mine, other, right)
         models.append(model)
         chunks = [chunks[0]] + [shift(chunks[step], step) for step in (1, 2, 3)]
@@ -417,14 +372,17 @@
             functools.partial(data_kernel, last),
             [COLUMN] + CHUNKS + ([] if last else [((5, 64, 512), F32)]),
             name="data",
-        )(*chunks, own, one, two, three, field, data_lens[-1])
+        )(*chunks, *blocks, left, observations if sweep == 0 else field, data_lens[-1])
         model_lens.append(outs[0])
         field = None if last else outs[5]
         chunks = [outs[1]] + [shift(outs[1 + step], -step) for step in (1, 2, 3)]
         keep, send = call(
             back_kernel, PARTIAL, PARTIAL_SCRATCH + [((4, 64, 128), F32)], name="back"
         )(right, *chunks)
-        raw, data_len, mine, other = sum_dp(keep, send, (raw, model_lens[-1]))
+        whole = call(core_kernel, [((256, 640), BF)], name="core_sum")(
+            keep, swap_core(send)
+        )[0]
+        raw, data_len, mine, other = sum_dp(whole, (raw, model_lens[-1]))
         data_lens.append(data_len)
 
     model, squares = call(

time: 199 us -> 188 us (0.945)
  blocking collectives: 83.3 us -> 63.7 us
  starting transfers between devices: 49.2 us -> 56.8 us
  local copies, waits for them, and re-layouts: 2.18 us -> 7.45 us
  Pallas kernels: 24.2 us -> 19.9 us
    all_to_all x5 -> x4, blocking collectives: 83.3 us -> 63.7 us  [exchange(): lax.all_to_all(value.reshape(32, 8, width), ('z', 'y'), split_axis=0, con...]
    ppermute x18, waiting for transfers between devices: 33 us -> 15.4 us  [shift(): return lax.ppermute(value, 'x', [(i, (i + step) % 4) for i in range(4)])]
    all_to_all x1 -> x2, waiting for transfers between devices: 0.01 us -> 15.7 us  [exchange(): lax.all_to_all(value.reshape(32, 8, width), ('z', 'y'), split_axis=0, con...]
    unnamed x12 -> x20, local copies, waits for them, and re-layouts: 1.56 us -> 6.83 us
    pallas_call x17 -> x19, Pallas kernels: 24.2 us -> 19.9 us  [run(): pl.pallas_call(kernel, out_shape=[jax.ShapeDtypeStruct(out[0], out[1]) fo...]
    ppermute x18, starting transfers between devices: 18.7 us -> 21.8 us  [shift(): return lax.ppermute(value, 'x', [(i, (i + step) % 4) for i in range(4)])]
    all_to_all x1 -> x2, starting transfers between devices: 11.3 us -> 14.3 us  [exchange(): lax.all_to_all(value.reshape(32, 8, width), ('z', 'y'), split_axis=0, con...]
  transfers between devices with their start and end apart: 25 -> 26, of which waited for: 18 -> 19; matrix products, arithmetic and copies ran while one was open for 0% -> 0% of each run, Pallas kernels for 2% -> 3%
where the time goes in v4:
time: 188 us; the launch traced here: 187 us
  blocking collectives  63.7 us (34%)
  starting transfers between devices  56.8 us (30%)
  waiting for transfers between devices  38.3 us (20%)
  Pallas kernels  19.9 us (11%)
  local copies, waits for them, and re-layouts  7.45 us (4%)
    all_to_all x4, blocking collectives, exchange(): lax.all_to_all(value.reshape(32, 8, width), ('z', 'y'), split_axis=0, con...  63.7 us
    ppermute x18, starting transfers between devices, shift(): return lax.ppermute(value, 'x', [(i, (i + step) % 4) for i in range(4)])  21.8 us
    ppermute x6, starting transfers between devices, swap_core(): return lax.ppermute(value, 'c', [(0, 1), (1, 0)])  20.6 us
    pallas_call x19, Pallas kernels, run(): pl.pallas_call(kernel, out_shape=[jax.ShapeDtypeStruct(out[0], out[1]) fo...  19.9 us
    all_to_all x2, waiting for transfers between devices, exchange(): lax.all_to_all(value.reshape(32, 8, width), ('z', 'y'), split_axis=0, con...  15.7 us
    ppermute x18, waiting for transfers between devices, shift(): return lax.ppermute(value, 'x', [(i, (i + step) % 4) for i in range(4)])  15.4 us
    all_to_all x2, starting transfers between devices, exchange(): lax.all_to_all(value.reshape(32, 8, width), ('z', 'y'), split_axis=0, con...  14.3 us
    ppermute x6, waiting for transfers between devices, swap_core(): return lax.ppermute(value, 'c', [(0, 1), (1, 0)])  7.25 us
  transfers between devices with their start and end apart: 26, of which 19 were waited for; matrix products, arithmetic and copies ran while one was open for 0% of the time, Pallas kernels for 3%

profile of v4, /device:TPU:1, one launch (start us, length us, event | category | flops | bytes accessed | tf_op | source)
XLA Modules:
  0.0 187.0 jit_solution(315584542293260822)
XLA Ops:
  0.6 1.7 copy-done
  2.4 1.3 copy-done.5
  3.7 1.0 start.1
  4.7 0.7 copy-done.2
  5.4 0.8 start_sum.1
  6.3 3.3 %collective-permute-start = (bf16[256,640]{1,0:T(8,128)(2,1)S(1)}, bf16[256,640]{1,0:T(8,128)(2,1)S(1)}, u32[]{:S(2)}, u32[]{:S(2)}) collective-permute-start(bf16[256,640]{1,0:T(8,128)(2,1)S(1)} %get-tuple-element.50.refs_1_), channel_id=1, source_target_pairs={{0,4},{4,0},{1,5},{5,1},{2,6},{6,2},{3,7},{7,3},{8,12},{12,8},{9,1... | collective-permute-start | bytes 983048 | tf_op jit(solution)/shard_map/ppermute | solution.py:307
  9.6 1.3 collective-permute-done.refs_1_
  10.9 0.8 core_sum.3
  11.7 9.6 %all-to-all-start = ((bf16[32,8,640]{2,1,0:T(8,128)(2,1)}), bf16[32,8,640]{2,1,0:T(8,128)(2,1)}, u32[]{:S(2)}, u32[]{:S(2)}) async-start(bf16[32,8,640]{2,1,0:T(8,128)(2,1)} %bitcast.3), calls=%async_computation | async-start | bytes 655360 | tf_op jit(solution)/shard_map/all_to_all | solution.py:312
  21.3 1.1 pack.1
  22.4 1.2 collective-permute-start.5
  23.6 1.5 collective-permute-start.6
  25.1 8.9 %all-to-all-done = bf16[32,8,640]{2,1,0:T(8,128)(2,1)} async-done(((bf16[32,8,640]{2,1,0:T(8,128)(2,1)}), bf16[32,8,640]{2,1,0:T(8,128)(2,1)}, u32[]{:S(2)}, u32[]{:S(2)}) %all-to-all-start) | async-done | bytes 327712 | tf_op jit(solution)/shard_map/all_to_all | solution.py:312
  34.0 1.2 shard.3
  35.2 0.6 copy-done.7
  35.8 0.7 copy-done.9
  36.5 4.8 %all-to-all-start.1 = ((bf16[32,8,512]{2,1,0:T(8,128)(2,1)}), bf16[32,8,512]{2,1,0:T(8,128)(2,1)S(1)}, u32[]{:S(2)}, u32[]{:S(2)}) async-start(bf16[32,8,512]{2,1,0:T(8,128)(2,1)} %bitcast.37), calls=%async_computation.1 | async-start | bytes 524288 | tf_op jit(solution)/shard_map/all_to_all | solution.py:312
  41.3 0.9 pack_two.1
  42.2 2.7 %collective-permute-start.7 = (bf16[5,128,512]{2,1,0:T(8,128)(2,1)}, bf16[5,128,512]{2,1,0:T(8,128)(2,1)}, u32[]{:S(2)}, u32[]{:S(2)}) collective-permute-start(bf16[5,128,512]{2,1,0:T(8,128)(2,1)} %pack_two.1), channel_id=1, source_target_pairs={{0,2},{1,3},{2,0},{3,1},{4,6},{5,7},{6,4},{7,5},{8,10},{9,11},{10,... | collective-permute-start | bytes 1966088 | tf_op jit(solution)/shard_map/ppermute | solution.py:303
  44.9 6.8 %all-to-all-done.1 = bf16[32,8,512]{2,1,0:T(8,128)(2,1)S(1)} async-done(((bf16[32,8,512]{2,1,0:T(8,128)(2,1)}), bf16[32,8,512]{2,1,0:T(8,128)(2,1)S(1)}, u32[]{:S(2)}, u32[]{:S(2)}) %all-to-all-start.1) | async-done | bytes 262176 | tf_op jit(solution)/shard_map/all_to_all | solution.py:312
  51.7 3.5 %collective-permute-start.1 = (bf16[256,512]{1,0:T(8,128)(2,1)S(1)}, bf16[256,512]{1,0:T(8,128)(2,1)S(1)}, u32[]{:S(2)}, u32[]{:S(2)}) collective-permute-start(bf16[256,512]{1,0:T(8,128)(2,1)S(1)} %bitcast.31), channel_id=1, source_target_pairs={{0,4},{4,0},{1,5},{5,1},{2,6},{6,2},{3,7},{7,3},{8,12},{12,8},{9,1... | collective-permute-start | bytes 786440 | tf_op jit(solution)/shard_map/ppermute | solution.py:307
  55.2 1.2 collective-permute-done.1.refs_1_
  56.4 1.7 copy-done.3
  58.2 1.2 forward.2
  59.4 1.3 collective-permute-start.2
  60.7 2.5 %collective-permute-start.3 = (bf16[4,64,128]{2,1,0:T(8,128)(2,1)S(1)}, bf16[4,64,128]{2,1,0:T(8,128)(2,1)S(1)}, u32[]{:S(2)}, u32[]{:S(2)}) collective-permute-start(bf16[4,64,128]{2,1,0:T(8,128)(2,1)S(1)} %get-tuple-element.55), channel_id=1, source_target_pairs={{0,2},{1,3},{2,0},{3,1},{4,6},{5,7},{6,4},{7,5},{8,10},{9,11},{10,... | collective-permute-start | bytes 196616 | tf_op jit(solution)/shard_map/ppermute | solution.py:303
  63.1 1.2 collective-permute-start.4
  64.3 1.8 collective-permute-done.3.refs_2_
  66.5 2.9 %data.2 = (f32[64,128]{1,0:T(8,128)S(1)}, bf16[4,64,128]{2,1,0:T(8,128)(2,1)S(1)}, bf16[4,64,128]{2,1,0:T(8,128)(2,1)S(1)}, bf16[4,64,128]{2,1,0:T(8,128)(2,1)S(...) custom-call(bf16[4,64,128]{2,1,0:T(8,128)(2,1)S(1)} %get-tuple-element.53.refs_0_, ...), custom_call_target="tpu_custom_call" | custom-call | tf_op jit(solution)/shard_map/data/pallas_call | solution.py:30
  69.4 2.2 %collective-permute-start.8 = (bf16[4,64,128]{2,1,0:T(8,128)(2,1)S(1)}, bf16[4,64,128]{2,1,0:T(8,128)(2,1)S(1)}, u32[]{:S(2)}, u32[]{:S(2)}) collective-permute-start(bf16[4,64,128]{2,1,0:T(8,128)(2,1)S(1)} %get-tuple-element.60), channel_id=1, source_target_pairs={{0,3},{1,0},{2,1},{3,2},{4,7},{5,4},{6,5},{7,6},{8,11},{9,8},{10,9... | collective-permute-start | bytes 196616 | tf_op jit(solution)/shard_map/ppermute | solution.py:303
  71.6 0.7 collective-permute-start.10
  72.2 0.7 collective-permute-done.8.refs_2_
  72.9 3.4 %collective-permute-done.9.refs_3_ = bf16[4,64,128]{2,1,0:T(8,128)(2,1)S(1)} collective-permute-done((bf16[4,64,128]{2,1,0:T(8,128)(2,1)S(1)}, bf16[4,64,128]{2,1,0:T(8,128)(2,1)S(1)}, u32[]{:S(2)}, u32[]{:S(2)}) %collective-permute-start.9) | collective-permute-done | bytes 65568 | tf_op jit(solution)/shard_map/ppermute | solution.py:303
  76.6 0.9 back.2
  77.5 3.6 %collective-permute-start.11 = (bf16[256,640]{1,0:T(8,128)(2,1)S(1)}, bf16[256,640]{1,0:T(8,128)(2,1)S(1)}, u32[]{:S(2)}, u32[]{:S(2)}) collective-permute-start(bf16[256,640]{1,0:T(8,128)(2,1)S(1)} %get-tuple-element.64), channel_id=1, source_target_pairs={{0,4},{4,0},{1,5},{5,1},{2,6},{6,2},{3,7},{7,3},{8,12},{12,8},{9,1... | collective-permute-start | bytes 983048 | tf_op jit(solution)/shard_map/ppermute | solution.py:307
  81.1 1.3 collective-permute-done.11.refs_1_
  82.4 17.7 %all_to_all.30 = bf16[32,8,640]{2,1,0:T(8,128)(2,1)S(1)} all-to-all(bf16[32,8,640]{2,1,0:T(8,128)(2,1)S(1)} %bitcast.27), channel_id=1, replica_groups=mesh['z'=8,'y'=4,'c'=2,'x'=4] {'z','y'}, dimensions={0} | all-to-all | bytes 655360 | tf_op jit(solution)/shard_map/all_to_all | solution.py:312
  100.3 15.0 %all_to_all.31 = bf16[32,8,512]{2,1,0:T(8,128)(2,1)S(1)} all-to-all(bf16[32,8,512]{2,1,0:T(8,128)(2,1)S(1)} %bitcast.38), channel_id=1, replica_groups=mesh['z'=8,'y'=4,'c'=2,'x'=4] {'z','y'}, dimensions={0} | all-to-all | bytes 524288 | tf_op jit(solution)/shard_map/all_to_all | solution.py:312
  115.3 3.5 %collective-permute-start.12 = (bf16[256,512]{1,0:T(8,128)(2,1)S(1)}, bf16[256,512]{1,0:T(8,128)(2,1)S(1)}, u32[]{:S(2)}, u32[]{:S(2)}) collective-permute-start(bf16[256,512]{1,0:T(8,128)(2,1)S(1)} %bitcast.33), channel_id=1, source_target_pairs={{0,4},{4,0},{1,5},{5,1},{2,6},{6,2},{3,7},{7,3},{8,12},{12,8},{9,1... | collective-permute-start | bytes 786440 | tf_op jit(solution)/shard_map/ppermute | solution.py:307
  118.8 1.2 collective-permute-done.12.refs_1_
  120.0 1.2 forward.3
  121.3 1.4 collective-permute-start.14
  122.8 1.6 collective-permute-start.15
  124.4 3.1 %collective-permute-done.13.refs_1_ = bf16[4,64,128]{2,1,0:T(8,128)(2,1)S(1)} collective-permute-done((bf16[4,64,128]{2,1,0:T(8,128)(2,1)S(1)}, bf16[4,64,128]{2,1,0:T(8,128)(2,1)S(1)}, u32[]{:S(2)}, u32[]{:S(2)}) %collective-permute-start.13) | collective-permute-done | bytes 65568 | tf_op jit(solution)/shard_map/ppermute | solution.py:303
  127.6 2.8 %data.3 = (f32[64,128]{1,0:T(8,128)S(1)}, bf16[4,64,128]{2,1,0:T(8,128)(2,1)S(1)}, bf16[4,64,128]{2,1,0:T(8,128)(2,1)S(1)}, bf16[4,64,128]{2,1,0:T(8,128)(2,1)S(1)}, bf16[4,64,128]{2,1,0:T(8,128)(2,1)S(1)}) custom-call(bf16[4,64,128]{2,1,0:T(8,128)(2,1)S(1)} %get-tuple-element.69.refs_0_, bf16[4,64,128]{2,1,0:T(8,128)(2,1)S(1)} %collective-permute-done.13.refs_1_, ...), custom_call_target="tpu_custom_call" | custom-call | tf_op jit(solution)/shard_map/data/pallas_call | solution.py:30
  130.4 2.6 %collective-permute-start.16 = (bf16[4,64,128]{2,1,0:T(8,128)(2,1)S(1)}, bf16[4,64,128]{2,1,0:T(8,128)(2,1)S(1)}, u32[]{:S(2)}, u32[]{:S(2)}) collective-permute-start(bf16[4,64,128]{2,1,0:T(8,128)(2,1)S(1)} %get-tuple-element.75), channel_id=1, source_target_pairs={{0,3},{1,0},{2,1},{3,2},{4,7},{5,4},{6,5},{7,6},{8,11},{9,8},{10,9... | collective-permute-start | bytes 196616 | tf_op jit(solution)/shard_map/ppermute | solution.py:303
  133.1 0.6 collective-permute-start.18
  133.7 0.7 collective-permute-done.16.refs_2_
  134.4 3.4 %collective-permute-done.17.refs_3_ = bf16[4,64,128]{2,1,0:T(8,128)(2,1)S(1)} collective-permute-done((bf16[4,64,128]{2,1,0:T(8,128)(2,1)S(1)}, bf16[4,64,128]{2,1,0:T(8,128)(2,1)S(1)}, u32[]{:S(2)}, u32[]{:S(2)}) %collective-permute-start.17) | collective-permute-done | bytes 65568 | tf_op jit(solution)/shard_map/ppermute | solution.py:303
  138.1 0.9 back.3
  139.0 3.0 %collective-permute-start.19 = (bf16[256,640]{1,0:T(8,128)(2,1)S(1)}, bf16[256,640]{1,0:T(8,128)(2,1)S(1)}, u32[]{:S(2)}, u32[]{:S(2)}) collective-permute-start(bf16[256,640]{1,0:T(8,128)(2,1)S(1)} %get-tuple-element.79), channel_id=1, source_target_pairs={{0,4},{4,0},{1,5},{5,1},{2,6},{6,2},{3,7},{7,3},{8,12},{12,8},{9,1... | collective-permute-start | bytes 983048 | tf_op jit(solution)/shard_map/ppermute | solution.py:307
  142.1 1.3 collective-permute-done.19.refs_1_
  143.4 16.0 %all_to_all.32 = bf16[32,8,640]{2,1,0:T(8,128)(2,1)S(1)} all-to-all(bf16[32,8,640]{2,1,0:T(8,128)(2,1)S(1)} %bitcast.28), channel_id=1, replica_groups=mesh['z'=8,'y'=4,'c'=2,'x'=4] {'z','y'}, dimensions={0} | all-to-all | bytes 655360 | tf_op jit(solution)/shard_map/all_to_all | solution.py:312
  159.4 0.8 shard.5
  160.2 15.0 %all_to_all.33 = bf16[32,8,512]{2,1,0:T(8,128)(2,1)S(1)} all-to-all(bf16[32,8,512]{2,1,0:T(8,128)(2,1)S(1)} %bitcast.39), channel_id=1, replica_groups=mesh['z'=8,'y'=4,'c'=2,'x'=4] {'z','y'}, dimensions={0} | all-to-all | bytes 524288 | tf_op jit(solution)/shard_map/all_to_all | solution.py:312
  175.2 3.5 %collective-permute-start.20 = (bf16[256,512]{1,0:T(8,128)(2,1)S(1)}, bf16[256,512]{1,0:T(8,128)(2,1)S(1)}, u32[]{:S(2)}, u32[]{:S(2)}) collective-permute-start(bf16[256,512]{1,0:T(8,128)(2,1)S(1)} %bitcast.35), channel_id=1, source_target_pairs={{0,4},{4,0},{1,5},{5,1},{2,6},{6,2},{3,7},{7,3},{8,12},{12,8},{9,1... | collective-permute-start | bytes 786440 | tf_op jit(solution)/shard_map/ppermute | solution.py:307
  178.7 1.2 collective-permute-done.20.refs_1_
  180.9 0.9 collective-permute-start.22
  181.7 0.8 collective-permute-start.21
  182.5 1.4 solve.1
  183.9 0.6 slice_reduce_fusion
  184.5 0.6 collective-permute-done.22.refs_7_
  185.1 0.6 collective-permute-done.21.refs_6_
  185.7 1.2 direct.1
  (32 shorter events, 2.6 us)
Async XLA Ops:
  0.6 1.7 copy-start
  2.4 1.3 copy-start.5
  3.7 1.7 copy-start.2
  4.7 16.5 %copy-start.1 = (bf16[2,5,4,32,1024]{4,3,2,1,0:T(8,128)(2,1)S(1)}, bf16[2,5,4,32,1024]{4,3,2,1,0:T(8,128)(2,1)}, u32[]{:S(2)}) copy-start(bf16[2,5,4,32,1024]{4,3,2,1,0:T(8,128)(2,1)} %param.3) | copy-start | bytes 7864324
  6.3 4.6 %collective-permute-start = (bf16[256,640]{1,0:T(8,128)(2,1)S(1)}, bf16[256,640]{1,0:T(8,128)(2,1)S(1)}, u32[]{:S(2)}, u32[]{:S(2)}) collective-permute-start(bf16[256,640]{1,0:T(8,128)(2,1)S(1)} %get-tuple-element.50.refs_1_), channel_id=1, source_target_pairs={{0,4},{4,0},{1,5},{5,1},{2,6},{6,2},{3,7},{7,3},{8,12},{12,8},{9,1... | collective-permute-start | bytes 983048 | tf_op jit(solution)/shard_map/ppermute | solution.py:307
  11.7 22.3 %all-to-all-start = ((bf16[32,8,640]{2,1,0:T(8,128)(2,1)}), bf16[32,8,640]{2,1,0:T(8,128)(2,1)}, u32[]{:S(2)}, u32[]{:S(2)}) async-start(bf16[32,8,640]{2,1,0:T(8,128)(2,1)} %bitcast.3), calls=%async_computation | async-start | bytes 655360 | tf_op jit(solution)/shard_map/all_to_all | solution.py:312
  22.4 18.9 %collective-permute-start.5 = (bf16[5,128,512]{2,1,0:T(8,128)(2,1)}, bf16[5,128,512]{2,1,0:T(8,128)(2,1)S(1)}, u32[]{:S(2)}, u32[]{:S(2)}) collective-permute-start(bf16[5,128,512]{2,1,0:T(8,128)(2,1)} %get-tuple-element.57), channel_id=1, source_target_pairs={{0,1},{1,2},{2,3},{3,0},{4,5},{5,6},{6,7},{7,4},{8,9},{9,10},{10,1... | collective-permute-start | bytes 1966088 | tf_op jit(solution)/shard_map/ppermute | solution.py:303
  23.6 17.7 %collective-permute-start.6 = (bf16[5,128,512]{2,1,0:T(8,128)(2,1)}, bf16[5,128,512]{2,1,0:T(8,128)(2,1)}, u32[]{:S(2)}, u32[]{:S(2)}) collective-permute-start(bf16[5,128,512]{2,1,0:T(8,128)(2,1)} %get-tuple-element.58), channel_id=1, source_target_pairs={{0,3},{1,0},{2,1},{3,2},{4,7},{5,4},{6,5},{7,6},{8,11},{9,8},{10,9... | collective-permute-start | bytes 1966088 | tf_op jit(solution)/shard_map/ppermute | solution.py:303
  35.2 0.6 copy-start.7
  35.8 0.7 copy-start.9
  36.5 15.2 %all-to-all-start.1 = ((bf16[32,8,512]{2,1,0:T(8,128)(2,1)}), bf16[32,8,512]{2,1,0:T(8,128)(2,1)S(1)}, u32[]{:S(2)}, u32[]{:S(2)}) async-start(bf16[32,8,512]{2,1,0:T(8,128)(2,1)} %bitcast.37), calls=%async_computation.1 | async-start | bytes 524288 | tf_op jit(solution)/shard_map/all_to_all | solution.py:312
  42.2 22.1 %collective-permute-start.7 = (bf16[5,128,512]{2,1,0:T(8,128)(2,1)}, bf16[5,128,512]{2,1,0:T(8,128)(2,1)}, u32[]{:S(2)}, u32[]{:S(2)}) collective-permute-start(bf16[5,128,512]{2,1,0:T(8,128)(2,1)} %pack_two.1), channel_id=1, source_target_pairs={{0,2},{1,3},{2,0},{3,1},{4,6},{5,7},{6,4},{7,5},{8,10},{9,11},{10,... | collective-permute-start | bytes 1966088 | tf_op jit(solution)/shard_map/ppermute | solution.py:303
  51.7 4.7 %collective-permute-start.1 = (bf16[256,512]{1,0:T(8,128)(2,1)S(1)}, bf16[256,512]{1,0:T(8,128)(2,1)S(1)}, u32[]{:S(2)}, u32[]{:S(2)}) collective-permute-start(bf16[256,512]{1,0:T(8,128)(2,1)S(1)} %bitcast.31), channel_id=1, source_target_pairs={{0,4},{4,0},{1,5},{5,1},{2,6},{6,2},{3,7},{7,3},{8,12},{12,8},{9,1... | collective-permute-start | bytes 786440 | tf_op jit(solution)/shard_map/ppermute | solution.py:307
  56.4 1.7 copy-start.3
  58.1 8.4 %copy-start.6 = (bf16[2,5,64,1024]{3,2,1,0:T(8,128)(2,1)S(1)}, bf16[2,5,64,1024]{3,2,1,0:T(8,128)(2,1)}, u32[]{:S(2)}) copy-start(bf16[2,5,64,1024]{3,2,1,0:T(8,128)(2,1)} %param.5) | copy-start | bytes 3932164
  58.1 8.4 %copy-start.8 = (f32[64,128]{1,0:T(8,128)S(1)}, f32[64,128]{1,0:T(8,128)}, u32[]{:S(2)}) copy-start(f32[64,128]{1,0:T(8,128)} %copy-done.7) | copy-start | bytes 98308
  59.4 4.9 %collective-permute-start.2 = (bf16[4,64,128]{2,1,0:T(8,128)(2,1)S(1)}, bf16[4,64,128]{2,1,0:T(8,128)(2,1)S(1)}, u32[]{:S(2)}, u32[]{:S(2)}) collective-permute-start(bf16[4,64,128]{2,1,0:T(8,128)(2,1)S(1)} %get-tuple-element.54), channel_id=1, source_target_pairs={{0,1},{1,2},{2,3},{3,0},{4,5},{5,6},{6,7},{7,4},{8,9},{9,10},{10,1... | collective-permute-start | bytes 196616 | tf_op jit(solution)/shard_map/ppermute | solution.py:303
  60.7 5.4 %collective-permute-start.3 = (bf16[4,64,128]{2,1,0:T(8,128)(2,1)S(1)}, bf16[4,64,128]{2,1,0:T(8,128)(2,1)S(1)}, u32[]{:S(2)}, u32[]{:S(2)}) collective-permute-start(bf16[4,64,128]{2,1,0:T(8,128)(2,1)S(1)} %get-tuple-element.55), channel_id=1, source_target_pairs={{0,2},{1,3},{2,0},{3,1},{4,6},{5,7},{6,4},{7,5},{8,10},{9,11},{10,... | collective-permute-start | bytes 196616 | tf_op jit(solution)/shard_map/ppermute | solution.py:303
  63.1 3.4 %collective-permute-start.4 = (bf16[4,64,128]{2,1,0:T(8,128)(2,1)S(1)}, bf16[4,64,128]{2,1,0:T(8,128)(2,1)S(1)}, u32[]{:S(2)}, u32[]{:S(2)}) collective-permute-start(bf16[4,64,128]{2,1,0:T(8,128)(2,1)S(1)} %get-tuple-element.56), channel_id=1, source_target_pairs={{0,3},{1,0},{2,1},{3,2},{4,7},{5,4},{6,5},{7,6},{8,11},{9,8},{10,9... | collective-permute-start | bytes 196616 | tf_op jit(solution)/shard_map/ppermute | solution.py:303
  69.4 3.5 %collective-permute-start.8 = (bf16[4,64,128]{2,1,0:T(8,128)(2,1)S(1)}, bf16[4,64,128]{2,1,0:T(8,128)(2,1)S(1)}, u32[]{:S(2)}, u32[]{:S(2)}) collective-permute-start(bf16[4,64,128]{2,1,0:T(8,128)(2,1)S(1)} %get-tuple-element.60), channel_id=1, source_target_pairs={{0,3},{1,0},{2,1},{3,2},{4,7},{5,4},{6,5},{7,6},{8,11},{9,8},{10,9... | collective-permute-start | bytes 196616 | tf_op jit(solution)/shard_map/ppermute | solution.py:303
  71.5 4.7 %collective-permute-start.9 = (bf16[4,64,128]{2,1,0:T(8,128)(2,1)S(1)}, bf16[4,64,128]{2,1,0:T(8,128)(2,1)S(1)}, u32[]{:S(2)}, u32[]{:S(2)}) collective-permute-start(bf16[4,64,128]{2,1,0:T(8,128)(2,1)S(1)} %get-tuple-element.61), channel_id=1, source_target_pairs={{0,2},{1,3},{2,0},{3,1},{4,6},{5,7},{6,4},{7,5},{8,10},{9,11},{10,... | collective-permute-start | bytes 196616 | tf_op jit(solution)/shard_map/ppermute | solution.py:303
  71.6 5.0 %collective-permute-start.10 = (bf16[4,64,128]{2,1,0:T(8,128)(2,1)S(1)}, bf16[4,64,128]{2,1,0:T(8,128)(2,1)S(1)}, u32[]{:S(2)}, u32[]{:S(2)}) collective-permute-start(bf16[4,64,128]{2,1,0:T(8,128)(2,1)S(1)} %get-tuple-element.62), channel_id=1, source_target_pairs={{0,1},{1,2},{2,3},{3,0},{4,5},{5,6},{6,7},{7,4},{8,9},{9,10},{10,1... | collective-permute-start | bytes 196616 | tf_op jit(solution)/shard_map/ppermute | solution.py:303
  76.6 43.4 %copy-start.4 = (bf16[2,5,4,32,1024]{4,3,2,1,0:T(8,128)(2,1)S(1)}, bf16[2,5,4,32,1024]{4,3,2,1,0:T(8,128)(2,1)}, u32[]{:S(2)}) copy-start(bf16[2,5,4,32,1024]{4,3,2,1,0:T(8,128)(2,1)} %param.4) | copy-start | bytes 7864324
  77.5 4.9 %collective-permute-start.11 = (bf16[256,640]{1,0:T(8,128)(2,1)S(1)}, bf16[256,640]{1,0:T(8,128)(2,1)S(1)}, u32[]{:S(2)}, u32[]{:S(2)}) collective-permute-start(bf16[256,640]{1,0:T(8,128)(2,1)S(1)} %get-tuple-element.64), channel_id=1, source_target_pairs={{0,4},{4,0},{1,5},{5,1},{2,6},{6,2},{3,7},{7,3},{8,12},{12,8},{9,1... | collective-permute-start | bytes 983048 | tf_op jit(solution)/shard_map/ppermute | solution.py:307
  115.3 4.7 %collective-permute-start.12 = (bf16[256,512]{1,0:T(8,128)(2,1)S(1)}, bf16[256,512]{1,0:T(8,128)(2,1)S(1)}, u32[]{:S(2)}, u32[]{:S(2)}) collective-permute-start(bf16[256,512]{1,0:T(8,128)(2,1)S(1)} %bitcast.33), channel_id=1, source_target_pairs={{0,4},{4,0},{1,5},{5,1},{2,6},{6,2},{3,7},{7,3},{8,12},{12,8},{9,1... | collective-permute-start | bytes 786440 | tf_op jit(solution)/shard_map/ppermute | solution.py:307
  121.2 6.3 %collective-permute-start.13 = (bf16[4,64,128]{2,1,0:T(8,128)(2,1)S(1)}, bf16[4,64,128]{2,1,0:T(8,128)(2,1)S(1)}, u32[]{:S(2)}, u32[]{:S(2)}) collective-permute-start(bf16[4,64,128]{2,1,0:T(8,128)(2,1)S(1)} %get-tuple-element.70), channel_id=1, source_target_pairs={{0,1},{1,2},{2,3},{3,0},{4,5},{5,6},{6,7},{7,4},{8,9},{9,10},{10,1... | collective-permute-start | bytes 196616 | tf_op jit(solution)/shard_map/ppermute | solution.py:303
  121.3 6.3 %collective-permute-start.14 = (bf16[4,64,128]{2,1,0:T(8,128)(2,1)S(1)}, bf16[4,64,128]{2,1,0:T(8,128)(2,1)S(1)}, u32[]{:S(2)}, u32[]{:S(2)}) collective-permute-start(bf16[4,64,128]{2,1,0:T(8,128)(2,1)S(1)} %get-tuple-element.71), channel_id=1, source_target_pairs={{0,2},{1,3},{2,0},{3,1},{4,6},{5,7},{6,4},{7,5},{8,10},{9,11},{10,... | collective-permute-start | bytes 196616 | tf_op jit(solution)/shard_map/ppermute | solution.py:303
  122.8 4.8 %collective-permute-start.15 = (bf16[4,64,128]{2,1,0:T(8,128)(2,1)S(1)}, bf16[4,64,128]{2,1,0:T(8,128)(2,1)S(1)}, u32[]{:S(2)}, u32[]{:S(2)}) collective-permute-start(bf16[4,64,128]{2,1,0:T(8,128)(2,1)S(1)} %get-tuple-element.72), channel_id=1, source_target_pairs={{0,3},{1,0},{2,1},{3,2},{4,7},{5,4},{6,5},{7,6},{8,11},{9,8},{10,9... | collective-permute-start | bytes 196616 | tf_op jit(solution)/shard_map/ppermute | solution.py:303
  130.4 3.9 %collective-permute-start.16 = (bf16[4,64,128]{2,1,0:T(8,128)(2,1)S(1)}, bf16[4,64,128]{2,1,0:T(8,128)(2,1)S(1)}, u32[]{:S(2)}, u32[]{:S(2)}) collective-permute-start(bf16[4,64,128]{2,1,0:T(8,128)(2,1)S(1)} %get-tuple-element.75), channel_id=1, source_target_pairs={{0,3},{1,0},{2,1},{3,2},{4,7},{5,4},{6,5},{7,6},{8,11},{9,8},{10,9... | collective-permute-start | bytes 196616 | tf_op jit(solution)/shard_map/ppermute | solution.py:303
  133.0 4.7 %collective-permute-start.17 = (bf16[4,64,128]{2,1,0:T(8,128)(2,1)S(1)}, bf16[4,64,128]{2,1,0:T(8,128)(2,1)S(1)}, u32[]{:S(2)}, u32[]{:S(2)}) collective-permute-start(bf16[4,64,128]{2,1,0:T(8,128)(2,1)S(1)} %get-tuple-element.76), channel_id=1, source_target_pairs={{0,2},{1,3},{2,0},{3,1},{4,6},{5,7},{6,4},{7,5},{8,10},{9,11},{10,... | collective-permute-start | bytes 196616 | tf_op jit(solution)/shard_map/ppermute | solution.py:303
  133.1 5.0 %collective-permute-start.18 = (bf16[4,64,128]{2,1,0:T(8,128)(2,1)S(1)}, bf16[4,64,128]{2,1,0:T(8,128)(2,1)S(1)}, u32[]{:S(2)}, u32[]{:S(2)}) collective-permute-start(bf16[4,64,128]{2,1,0:T(8,128)(2,1)S(1)} %get-tuple-element.77), channel_id=1, source_target_pairs={{0,1},{1,2},{2,3},{3,0},{4,5},{5,6},{6,7},{7,4},{8,9},{9,10},{10,1... | collective-permute-start | bytes 196616 | tf_op jit(solution)/shard_map/ppermute | solution.py:303
  139.0 4.3 %collective-permute-start.19 = (bf16[256,640]{1,0:T(8,128)(2,1)S(1)}, bf16[256,640]{1,0:T(8,128)(2,1)S(1)}, u32[]{:S(2)}, u32[]{:S(2)}) collective-permute-start(bf16[256,640]{1,0:T(8,128)(2,1)S(1)} %get-tuple-element.79), channel_id=1, source_target_pairs={{0,4},{4,0},{1,5},{5,1},{2,6},{6,2},{3,7},{7,3},{8,12},{12,8},{9,1... | collective-permute-start | bytes 983048 | tf_op jit(solution)/shard_map/ppermute | solution.py:307
  175.2 4.7 %collective-permute-start.20 = (bf16[256,512]{1,0:T(8,128)(2,1)S(1)}, bf16[256,512]{1,0:T(8,128)(2,1)S(1)}, u32[]{:S(2)}, u32[]{:S(2)}) collective-permute-start(bf16[256,512]{1,0:T(8,128)(2,1)S(1)} %bitcast.35), channel_id=1, source_target_pairs={{0,4},{4,0},{1,5},{5,1},{2,6},{6,2},{3,7},{7,3},{8,12},{12,8},{9,1... | collective-permute-start | bytes 786440 | tf_op jit(solution)/shard_map/ppermute | solution.py:307
  180.3 4.2 %collective-permute-start.23 = (f32[64,128]{1,0:T(8,128)S(1)}, f32[64,128]{1,0:T(8,128)S(1)}, u32[]{:S(2)}, u32[]{:S(2)}) collective-permute-start(f32[64,128]{1,0:T(8,128)S(1)} %get-tuple-element.86.refs_7_.refs_5_), channel_id=1, source_target_pairs={{0,3},{1,0},{2,1},{3,2},{4,7},{5,4},{6,5},{7,6},{8,11},{9,8},{10,9... | collective-permute-start | bytes 98312 | tf_op jit(solution)/shard_map/ppermute | solution.py:303
  180.9 4.3 %collective-permute-start.22 = (f32[64,128]{1,0:T(8,128)S(1)}, f32[64,128]{1,0:T(8,128)S(1)}, u32[]{:S(2)}, u32[]{:S(2)}) collective-permute-start(f32[64,128]{1,0:T(8,128)S(1)} %get-tuple-element.86.refs_7_.refs_5_), channel_id=1, source_target_pairs={{0,2},{1,3},{2,0},{3,1},{4,6},{5,7},{6,4},{7,5},{8,10},{9,11},{10,... | collective-permute-start | bytes 98312 | tf_op jit(solution)/shard_map/ppermute | solution.py:303
  181.7 4.0 %collective-permute-start.21 = (f32[64,128]{1,0:T(8,128)S(1)}, f32[64,128]{1,0:T(8,128)S(1)}, u32[]{:S(2)}, u32[]{:S(2)}) collective-permute-start(f32[64,128]{1,0:T(8,128)S(1)} %get-tuple-element.86.refs_7_.refs_5_), channel_id=1, source_target_pairs={{0,1},{1,2},{2,3},{3,0},{4,5},{5,6},{6,7},{7,4},{8,9},{9,10},{10,1... | collective-permute-start | bytes 98312 | tf_op jit(solution)/shard_map/ppermute | solution.py:303

commit v5 on v4

--- a/solution.py
+++ b/solution.py
@@ -15,7 +15,7 @@
 VMEM_LIMIT = 20 * 1024 * 1024
 
 
-def call(kernel, outs, scratch=(), name=None, after=()):
+def call(kernel, outs, scratch=(), name=None, after=(), out_space=pltpu.VMEM):
     given = kernel
 
     def run(*operands):
@@ -32,7 +32,7 @@
             out_shape=[jax.ShapeDtypeStruct(out[0], out[1]) for out in outs],
             in_specs=[pl.BlockSpec(memory_space=pltpu.VMEM)] * len(operands)
             + [pl.BlockSpec(memory_space=pl.ANY)] * len(after),
-            out_specs=[pl.BlockSpec(memory_space=pltpu.VMEM)] * len(outs),
+            out_specs=[pl.BlockSpec(memory_space=out_space)] * len(outs),
             scratch_shapes=[
                 pltpu.VMEM(*entry) if isinstance(entry, tuple) else entry
                 for entry in scratch
@@ -65,20 +65,24 @@
     return jnp.sum(value, axis=-1, keepdims=True)
 
 
-def pieces_in_lanes(column):
-    first, second, third = split(column)
-    lane = lax.broadcasted_iota(jnp.int32, (64, 128), 1)
-    return jnp.where(
-        lane == 0, first, jnp.where(lane == 1, second, jnp.where(lane == 2, third, 0.0))
-    )
-
-
-def pieces_in_rows(row):
+def pieces_in_rows(row, count=8):
     first, second, third = split(row)
-    at = lax.broadcasted_iota(jnp.int32, (8, 128), 0)
+    at = lax.broadcasted_iota(jnp.int32, (count, 128), 0)
     return jnp.where(
         at == 0, first, jnp.where(at == 1, second, jnp.where(at == 2, third, 0.0))
     )
+
+
+def part(index):
+    return pl.ds(64 * index, 64)
+
+
+TAIL = pl.ds(192, 16)
+
+
+def squares_of(chunks):
+    total = sum(chunk[TAIL, :].astype(F32) for chunk in chunks)
+    return to_column(jnp.sum(total, axis=0, keepdims=True))
 
 
 def diagonal():
@@ -120,7 +124,9 @@
     )
 
 
-def start_kernel(places, left, observations, slots, squares):
+def start_kernel(places, left, observations, slots, squares, own_field):
+    for unit in range(5):
+        own_field[unit] = unit_of(observations, places[0], unit)
     total = jnp.zeros((64, 128), F32)
     for pair in range(10):
         values = observations[pair]
@@ -135,10 +141,25 @@
     write_partial(places, in_slots(slots), right, squares[:, 0:1], keep, send, field)
 
 
-def pack_kernel(steps, places, left, *outs):
-    for step, out in zip(steps, outs):
-        for unit in range(5):
-            out[unit] = unit_of(left, lax.rem(places[0] + step, 4), unit)
+def pack_kernel(places, left, one, two, three):
+    here = places[0]
+    for unit in range(5):
+        for step, out in ((1, one), (2, two), (3, three)):
+            out[unit] = unit_of(left, lax.rem(here + step, 4), unit)
+
+
+def hold(value, kept=(), after=()):
+    return pl.pallas_call(
+        lambda *refs: None,
+        out_shape=jax.ShapeDtypeStruct(value.shape, value.dtype),
+        in_specs=[pl.BlockSpec(memory_space=pl.ANY)]
+        + [pl.BlockSpec(memory_space=pltpu.VMEM)] * len(kept)
+        + [pl.BlockSpec(memory_space=pl.ANY)] * len(after),
+        out_specs=pl.BlockSpec(memory_space=pl.ANY),
+        input_output_aliases={0: 0},
+        compiler_params=pltpu.CompilerParams(vmem_limit_bytes=VMEM_LIMIT),
+        name="hold",
+    )(value, *kept, *after)
 
 
 def unit_of(ref, owner, unit):
@@ -150,13 +171,13 @@
 
 def back_kernel(places, right, own, one, two, three, keep, send, field, slots, shared):
     here = places[0]
-    squares = jnp.zeros((64, 1), F32)
-    for step, chunk in enumerate((own, one, two, three)):
+    chunks = (own, one, two, three)
+    squares = squares_of(chunks)
+    for step, chunk in enumerate(chunks):
         peer = lax.rem(here + step, 4)
-        slots[2 * peer] = chunk[0]
-        slots[2 * peer + 1] = chunk[1]
-        shared[peer] = chunk[2].astype(F32)
-        squares = squares + lane_sum(chunk[3].astype(F32))
+        slots[2 * peer] = chunk[part(0), :]
+        slots[2 * peer + 1] = chunk[part(1), :]
+        shared[peer] = chunk[part(2), :].astype(F32)
     slots[8] = (shared[0] + shared[1]).astype(BF)
     slots[9] = (shared[2] + shared[3]).astype(BF)
     write_partial(places, in_slots(slots), right, squares, keep, send, field)
@@ -170,20 +191,26 @@
 
 
 def shard_kernel(first, places, got, *refs):
-    previous, model_len = (None, None) if first else refs[:2]
-    raw, data_len, send = refs[0 if first else 2 :][:3]
+    before, model_len = (None, None) if first else refs[:2]
+    state, send, column = refs[0 if first else 2 :]
     total = jnp.sum(got[...].astype(F32).reshape(32, 8, 640), axis=0)
     squares = jnp.sum(total[:, 512:640], axis=0, keepdims=True)
-    data_len[...] = jnp.broadcast_to(
-        to_column(jnp.sqrt(squares + EPSILON)), (64, 128)
-    )
+    data_len = jnp.sqrt(squares + EPSILON)
+    column[...] = jnp.broadcast_to(to_column(data_len), (64, 128))
     row = places[2]
-    length = data_len[pl.ds(row, 1), 0:1]
+    length = column[pl.ds(row, 1), 0:1]
     value = total[:, 0:512] / length
     if not first:
-        value = value - (length / model_len[pl.ds(row, 1), 0:1]) * previous[...]
-    raw[...] = value
+        ratio = length / model_len[pl.ds(row, 1), 0:1]
+        value = value - ratio * before[0:8, :]
+    state[0:8, :] = value
+    state[8:16, 0:128] = jnp.broadcast_to(data_len, (8, 128))
+    state[8:16, 128:512] = jnp.zeros((8, 384), F32)
     send[...] = jnp.concatenate([value] * 32, axis=0).astype(BF)
+
+
+def length_column(state):
+    return jnp.broadcast_to(to_column(state[8:9, 0:128]), (64, 128))
 
 
 def read_model(places, mine, other, model, field):
@@ -208,48 +235,48 @@
         value = dot_nt(model[:, 1024 * t : 1024 * t + 1024], factors).astype(BF)
         for j in range(10):
             slots[j, :, 32 * t : 32 * t + 32] = value[:, 32 * j : 32 * j + 32]
-    tail = pieces_in_lanes(squares).astype(BF)
+    tail = pieces_in_rows(to_row(squares), 16).astype(BF)
     here = places[0]
     for step, chunk in enumerate((own, one, two, three)):
         peer = lax.rem(here + step, 4)
-        chunk[0] = slots[2 * peer]
-        chunk[1] = slots[2 * peer + 1]
-        chunk[2] = slots[8 + peer // 2]
-        chunk[3] = tail
+        chunk[part(0), :] = slots[2 * peer]
+        chunk[part(1), :] = slots[2 * peer + 1]
+        chunk[part(2), :] = slots[8 + peer // 2]
+        chunk[TAIL, :] = tail
 
 
 def data_kernel(last, places, *refs):
-    coeffs, blocks, (left, field, data_len), refs = refs[:4], refs[4:7], refs[7:10], refs[10:]
-    model_len, outs = refs[0], refs[1:5]
-    squares = sum(lane_sum(chunk[3].astype(F32)) for chunk in coeffs)
-    length = jnp.sqrt(squares + EPSILON)
+    coeffs, blocks, (left, field, state), refs = refs[:4], refs[4:7], refs[7:10], refs[10:]
+    model_len, data_len, outs = refs[0], refs[1], refs[2:6]
+    data_len[...] = length_column(state)
+    length = jnp.sqrt(squares_of(coeffs) + EPSILON)
     model_len[...] = jnp.broadcast_to(length, (64, 128))
     inverse = 1.0 / length
     ratio = length / data_len[:, 0:1]
     total = jnp.zeros((64, 128), F32)
     for i in range(3):
-        given = jnp.concatenate([chunk[i] for chunk in coeffs], axis=1)
+        given = jnp.concatenate([chunk[part(i), :] for chunk in coeffs], axis=1)
         back = None
         for unit in range(2 * i, min(2 * i + 2, 5)):
             factors = [unit_of(left, places[0], unit)] + [block[unit] for block in blocks]
             factors = jnp.concatenate(factors, axis=0)
-            before = field[unit] if last else unit_of(field, places[0], unit).astype(F32)
-            value = dot(given, factors) * inverse - ratio * before
+            value = dot(given, factors) * inverse - ratio * field[unit].astype(F32)
             if not last:
-                refs[5][unit] = value
+                refs[6][unit] = value
             term = dot_nt(value.astype(BF), factors)
             back = term if back is None else back + term
             value = value * value
             total = total + sum(value[:, 128 * k : 128 * k + 128] for k in range(4))
         back = back.astype(BF)
         for step in range(4):
-            outs[step][i] = back[:, 128 * step : 128 * step + 128]
-    tail = pieces_in_lanes(lane_sum(total)).astype(BF)
+            outs[step][part(i), :] = back[:, 128 * step : 128 * step + 128]
+    tail = pieces_in_rows(to_row(lane_sum(total)), 16).astype(BF)
     for step in range(4):
-        outs[step][3] = tail
-
-
-def last_model_kernel(places, mine, other, model, squares, field):
+        outs[step][TAIL, :] = tail
+
+
+def last_model_kernel(places, mine, other, state, model, data_len, squares, field):
+    data_len[...] = length_column(state)
     squares[...] = jnp.broadcast_to(
         read_model(places, mine, other, model, field), (64, 128)
     )
@@ -290,13 +317,17 @@
 
 def direction_kernel(places, *refs):
     data_lens, model_lens, squares = refs[:3], refs[3:5], refs[5:9]
-    third, last_direction, out = refs[9:]
+    third, last_direction, out, made, sems = refs[9:]
+    copies = [pltpu.make_async_copy(made.at[t], out.at[t], sems.at[t]) for t in range(4)]
     length = jnp.sqrt(sum(ref[:, 0:1] for ref in squares) + EPSILON)
     model_lens = [ref[:, 0:1] for ref in model_lens] + [length]
     steps, residual = scalars([ref[:, 0:1] for ref in data_lens], model_lens)
     for t in range(4):
         model = third[:, 1024 * t : 1024 * t + 1024].astype(F32) / length
-        out[t] = model - steps[1][1] * last_direction[t]
+        made[t] = model - steps[1][1] * last_direction[t]
+        copies[t].start()
+    for copy in copies:
+        copy.wait()
 
 
 def shift(value, step):
@@ -317,7 +348,7 @@
 
 PARTIAL = [((256, 640), F32), ((256, 640), BF)]
 PARTIAL_SCRATCH = [((4, 512, 128), F32), ((10, 64, 128), BF)]
-CHUNKS = [((4, 64, 128), BF)] * 4
+CHUNKS = [((208, 128), BF)] * 4
 COLUMN = ((64, 128), F32)
 MODEL = ((64, 4096), BF)
 
@@ -327,67 +358,71 @@
     right = right.reshape(10, 4, 32, 1024)
     observations = observations.reshape(10, 64, 1024)
 
-    def sum_dp(whole, extra, before_shard=()):
-        raw, data_len, send = call(
+    def sum_dp(whole, extra, before_gather=()):
+        state, send = call(
             functools.partial(shard_kernel, not extra),
-            [((8, 512), F32), COLUMN, ((256, 512), BF)],
+            [((16, 512), F32), ((256, 512), BF)],
+            [COLUMN],
             name="shard",
-            after=before_shard,
         )(exchange(whole), *extra)
         mine = exchange(send)
-        return raw, data_len, mine, swap_core(mine)
-
-    slots, squares = call(
-        start_kernel, [((10, 64, 128), BF), COLUMN], name="start"
+        if before_gather:
+            mine = hold(mine, (), before_gather)
+        return state, mine, swap_core(mine)
+
+    one, two, three = call(pack_kernel, [((5, 128, 512), BF)] * 3, name="pack")(left)
+    slots, squares, own_field = call(
+        start_kernel,
+        [((10, 64, 128), BF), COLUMN, ((5, 64, 512), BF)],
+        name="start",
+        after=(one, two, three),
     )(left, observations)
     keep, send = call(first_back_kernel, PARTIAL, PARTIAL_SCRATCH[:1], name="start_sum")(
         right, slots, squares
     )
-    block = ((5, 128, 512), BF)
-    one, three = call(
-        functools.partial(pack_kernel, (1, 3)), [block] * 2, name="pack", after=(send,)
-    )(left)
     one, three = shift(one, 1), shift(three, 3)
-    two = call(
-        functools.partial(pack_kernel, (2,)), [block], name="pack_two", after=(one, three)
-    )(left)[0]
-    blocks = [one, shift(two, 2), three]
+    two = shift(hold(two, (right,), (one, three)), 2)
+    blocks = [one, two, three]
     whole = call(core_kernel, [((256, 640), BF)], name="core_sum")(
         keep, swap_core(send)
     )[0]
-    raw, data_len, mine, other = sum_dp(whole, (), ())
-    models, model_lens, data_lens = [], [], [data_len]
+    state, mine, other = sum_dp(whole, (), (two,))
+    field = own_field
+    models, model_lens, data_lens = [], [], []
     for sweep in range(ITERS):
         model, *chunks = call(
             forward_kernel,
             [MODEL] + CHUNKS,
             [((4, 512, 128), F32), ((10, 64, 128), BF)],
             name="forward",
-            after=() if sweep == 0 else (),
         )(mine, other, right)
         models.append(model)
         chunks = [chunks[0]] + [shift(chunks[step], step) for step in (1, 2, 3)]
         last = sweep == ITERS - 1
         outs = call(
             functools.partial(data_kernel, last),
-            [COLUMN] + CHUNKS + ([] if last else [((5, 64, 512), F32)]),
+            [COLUMN, COLUMN] + CHUNKS + ([] if last else [((5, 64, 512), F32)]),
             name="data",
-        )(*chunks, *blocks, left, observations if sweep == 0 else field, data_lens[-1])
+        )(*chunks, *blocks, left, field, state)
         model_lens.append(outs[0])
-        field = None if last else outs[5]
-        chunks = [outs[1]] + [shift(outs[1 + step], -step) for step in (1, 2, 3)]
+        data_lens.append(outs[1])
+        field = None if last else outs[6]
+        chunks = [outs[2]] + [shift(outs[2 + step], -step) for step in (1, 2, 3)]
         keep, send = call(
             back_kernel, PARTIAL, PARTIAL_SCRATCH + [((4, 64, 128), F32)], name="back"
         )(right, *chunks)
         whole = call(core_kernel, [((256, 640), BF)], name="core_sum")(
             keep, swap_core(send)
         )[0]
-        raw, data_len, mine, other = sum_dp(whole, (raw, model_lens[-1]))
-        data_lens.append(data_len)
-
-    model, squares = call(
-        last_model_kernel, [MODEL, COLUMN], [((4, 512, 128), F32)], name="last_model"
-    )(mine, other)
+        state, mine, other = sum_dp(whole, (state, model_lens[-1]))
+
+    model, data_len, squares = call(
+        last_model_kernel,
+        [MODEL, COLUMN, COLUMN],
+        [((4, 512, 128), F32)],
+        name="last_model",
+    )(mine, other, state)
+    data_lens.append(data_len)
     solve_after = (squares,)
     squares = [squares] + [shift(squares, step) for step in (1, 2, 3)]
     solved, residual, last_direction = call(
@@ -396,7 +431,13 @@
         name="solve",
         after=solve_after,
     )(*data_lens, *model_lens, *models)
-    direction = call(direction_kernel, [((4, 64, 1024), F32)], name="direct")(
+    direction = call(
+        direction_kernel,
+        [((4, 64, 1024), F32)],
+        [((4, 64, 1024), F32), pltpu.SemaphoreType.DMA((4,))],
+        name="direct",
+        out_space=pl.ANY,
+    )(
         *data_lens, *model_lens, *squares, model, last_direction
     )[0]
     return solved, direction, residual[:, 0]

time: 188 us -> 184 us (0.979)
  waiting for transfers between devices: 38.3 us -> 42.6 us
  starting transfers between devices: 56.8 us -> 54.4 us
  Pallas kernels: 19.9 us -> 18 us
    ppermute x18, waiting for transfers between devices: 15.4 us -> 21.3 us  [shift(): return lax.ppermute(value, 'x', [(i, (i + step) % 4) for i in range(4)])]
    ppermute x18, starting transfers between devices: 21.8 us -> 19.4 us  [shift(): return lax.ppermute(value, 'x', [(i, (i + step) % 4) for i in range(4)])]
    pallas_call x19 -> x18, Pallas kernels: 19.9 us -> 18 us  [run(): pl.pallas_call(kernel, out_shape=[jax.ShapeDtypeStruct(out[0], out[1]) fo...]
  transfers between devices with their start and end apart: 26 -> 26, of which waited for: 19 -> 21; matrix products, arithmetic and copies ran while one was open for 0% -> 0% of each run, Pallas kernels for 3% -> 1%
where the time goes in v5:
time: 184 us
  blocking collectives  62.1 us (34%)
  starting transfers between devices  54.4 us (30%)
  waiting for transfers between devices  42.6 us (23%)
  Pallas kernels  18 us (10%)
  local copies, waits for them, and re-layouts  5.59 us (3%)
    all_to_all x4, blocking collectives, exchange(): lax.all_to_all(value.reshape(32, 8, width), ('z', 'y'), split_axis=0, con...  62.1 us
    ppermute x18, waiting for transfers between devices, shift(): return lax.ppermute(value, 'x', [(i, (i + step) % 4) for i in range(4)])  21.3 us
    ppermute x6, starting transfers between devices, swap_core(): return lax.ppermute(value, 'c', [(0, 1), (1, 0)])  20.4 us
    ppermute x18, starting transfers between devices, shift(): return lax.ppermute(value, 'x', [(i, (i + step) % 4) for i in range(4)])  19.4 us
    pallas_call x18, Pallas kernels, run(): pl.pallas_call(kernel, out_shape=[jax.ShapeDtypeStruct(out[0], out[1]) fo...  18 us
    all_to_all x2, waiting for transfers between devices, exchange(): lax.all_to_all(value.reshape(32, 8, width), ('z', 'y'), split_axis=0, con...  15.2 us
    all_to_all x2, starting transfers between devices, exchange(): lax.all_to_all(value.reshape(32, 8, width), ('z', 'y'), split_axis=0, con...  14.6 us
    ppermute x6, waiting for transfers between devices, swap_core(): return lax.ppermute(value, 'c', [(0, 1), (1, 0)])  6 us
  transfers between devices with their start and end apart: 26, of which 21 were waited for; matrix products, arithmetic and copies ran while one was open for 0% of the time, Pallas kernels for 1%

profile of v5, /device:TPU:1, one launch (start us, length us, event | category | flops | bytes accessed | tf_op | source)
XLA Modules:
  0.0 183.6 jit_solution(7798536202021714767)
XLA Ops:
  0.6 1.7 copy-done.1
  2.4 1.4 pack.1
  3.8 0.5 copy-done.4
  4.3 1.0 start.1
  5.4 0.7 copy-done
  6.0 0.9 start_sum.1
  6.9 3.3 %collective-permute-start = (bf16[256,640]{1,0:T(8,128)(2,1)S(1)}, bf16[256,640]{1,0:T(8,128)(2,1)S(1)}, u32[]{:S(2)}, u32[]{:S(2)}) collective-permute-start(bf16[256,640]{1,0:T(8,128)(2,1)S(1)} %get-tuple-element.56), channel_id=1, source_target_pairs={{0,4},{4,0},{1,5},{5,1},{2,6},{6,2},{3,7},{7,3},{8,12},{12,8},{9,1... | collective-permute-start | bytes 983048 | tf_op jit(solution)/shard_map/ppermute | solution.py:338
  10.2 2.7 %collective-permute-start.2 = (bf16[5,128,512]{2,1,0:T(8,128)(2,1)}, bf16[5,128,512]{2,1,0:T(8,128)(2,1)}, u32[]{:S(2)}, u32[]{:S(2)}) collective-permute-start(bf16[5,128,512]{2,1,0:T(8,128)(2,1)} %get-tuple-element.52.refs_4_), channel_id=1, source_target_pairs={{0,3},{1,0},{2,1},{3,2},{4,7},{5,4},{6,5},{7,6},{8,11},{9,8},{10,9... | collective-permute-start | bytes 1966088 | tf_op jit(solution)/shard_map/ppermute | solution.py:334
  13.0 0.7 copy-done.3
  13.7 9.6 %all-to-all-start = ((bf16[32,8,640]{2,1,0:T(8,128)(2,1)}), bf16[32,8,640]{2,1,0:T(8,128)(2,1)}, u32[]{:S(2)}, u32[]{:S(2)}) async-start(bf16[32,8,640]{2,1,0:T(8,128)(2,1)} %bitcast.26), calls=%async_computation | async-start | bytes 655360 | tf_op jit(solution)/shard_map/all_to_all | solution.py:343
  23.3 4.6 %collective-permute-done.1.refs_2_.refs_4_ = bf16[5,128,512]{2,1,0:T(8,128)(2,1)S(1)} collective-permute-done((bf16[5,128,512]{2,1,0:T(8,128)(2,1)}, bf16[5,128,512]{2,1,0:T(8,128)(2,1)S(1)}, u32[]{:S(2)}, u32[]{:S(2)}) %collective-permute-start.1) | collective-permute-done | bytes 655392 | tf_op jit(solution)/shard_map/ppermute | solution.py:334
  28.0 1.3 collective-permute-start.3
  29.2 6.6 %all-to-all-done = bf16[32,8,640]{2,1,0:T(8,128)(2,1)} async-done(((bf16[32,8,640]{2,1,0:T(8,128)(2,1)}), bf16[32,8,640]{2,1,0:T(8,128)(2,1)}, u32[]{:S(2)}, u32[]{:S(2)}) %all-to-all-start) | async-done | bytes 327712 | tf_op jit(solution)/shard_map/all_to_all | solution.py:343
  35.9 1.2 shard.3
  37.0 0.7 copy-done.7
  37.7 0.6 copy-done.8
  38.3 5.0 %all-to-all-start.1 = ((bf16[32,8,512]{2,1,0:T(8,128)(2,1)}), bf16[32,8,512]{2,1,0:T(8,128)(2,1)S(1)}, u32[]{:S(2)}, u32[]{:S(2)}) async-start(bf16[32,8,512]{2,1,0:T(8,128)(2,1)} %bitcast.36), calls=%async_computation.1 | async-start | bytes 524288 | tf_op jit(solution)/shard_map/all_to_all | solution.py:343
  43.3 1.8 collective-permute-done.3.refs_1_.refs_5_
  45.2 8.6 %all-to-all-done.1 = bf16[32,8,512]{2,1,0:T(8,128)(2,1)S(1)} async-done(((bf16[32,8,512]{2,1,0:T(8,128)(2,1)}), bf16[32,8,512]{2,1,0:T(8,128)(2,1)S(1)}, u32[]{:S(2)}, u32[]{:S(2)}) %all-to-all-start.1) | async-done | bytes 262176 | tf_op jit(solution)/shard_map/all_to_all | solution.py:343
  53.8 3.6 %collective-permute-start.4 = (bf16[256,512]{1,0:T(8,128)(2,1)S(1)}, bf16[256,512]{1,0:T(8,128)(2,1)S(1)}, u32[]{:S(2)}, u32[]{:S(2)}) collective-permute-start(bf16[256,512]{1,0:T(8,128)(2,1)S(1)} %hold.3.refs_0_), channel_id=1, source_target_pairs={{0,4},{4,0},{1,5},{5,1},{2,6},{6,2},{3,7},{7,3},{8,12},{12,8},{9,1... | collective-permute-start | bytes 786440 | tf_op jit(solution)/shard_map/ppermute | solution.py:338
  57.4 1.2 collective-permute-done.4.refs_1_
  58.5 1.2 forward.2
  59.9 2.4 %collective-permute-start.6 = (bf16[208,128]{1,0:T(8,128)(2,1)S(1)}, bf16[208,128]{1,0:T(8,128)(2,1)S(1)}, u32[]{:S(2)}, u32[]{:S(2)}) collective-permute-start(bf16[208,128]{1,0:T(8,128)(2,1)S(1)} %get-tuple-element.60), channel_id=1, source_target_pairs={{0,2},{1,3},{2,0},{3,1},{4,6},{5,7},{6,4},{7,5},{8,10},{9,11},{10,... | collective-permute-start | bytes 159752 | tf_op jit(solution)/shard_map/ppermute | solution.py:334
  62.3 1.2 collective-permute-start.7
  63.5 1.4 collective-permute-done.5.refs_1_
  64.9 0.9 collective-permute-done.7.refs_3_
  65.8 2.8 %data.2 = (f32[64,128]{1,0:T(8,128)S(1)}, f32[64,128]{1,0:T(8,128)S(1)}, bf16[208,128]{1,0:T(8,128)(2,1)S(1)}, bf16[208,128]{1,0:T(8,128)(2,1)S(1)}, bf16[208,12...) custom-call(bf16[208,128]{1,0:T(8,128)(2,1)S(1)} %get-tuple-element.58.refs_0_, ...), custom_call_target="tpu_custom_call" | custom-call | tf_op jit(solution)/shard_map/data/pallas_call | solution.py:30
  68.6 2.3 %collective-permute-start.8 = (bf16[208,128]{1,0:T(8,128)(2,1)S(1)}, bf16[208,128]{1,0:T(8,128)(2,1)S(1)}, u32[]{:S(2)}, u32[]{:S(2)}) collective-permute-start(bf16[208,128]{1,0:T(8,128)(2,1)S(1)} %get-tuple-element.66), channel_id=1, source_target_pairs={{0,3},{1,0},{2,1},{3,2},{4,7},{5,4},{6,5},{7,6},{8,11},{9,8},{10,9... | collective-permute-start | bytes 159752 | tf_op jit(solution)/shard_map/ppermute | solution.py:334
  71.6 0.5 collective-permute-done.8.refs_2_
  72.1 3.4 %collective-permute-done.9.refs_3_ = bf16[208,128]{1,0:T(8,128)(2,1)S(1)} collective-permute-done((bf16[208,128]{1,0:T(8,128)(2,1)S(1)}, bf16[208,128]{1,0:T(8,128)(2,1)S(1)}, u32[]{:S(2)}, u32[]{:S(2)}) %collective-permute-start.9) | collective-permute-done | bytes 53280 | tf_op jit(solution)/shard_map/ppermute | solution.py:334
  75.5 0.4 collective-permute-done.10.refs_4_
  75.9 0.9 back.2
  76.8 3.3 %collective-permute-start.11 = (bf16[256,640]{1,0:T(8,128)(2,1)S(1)}, bf16[256,640]{1,0:T(8,128)(2,1)S(1)}, u32[]{:S(2)}, u32[]{:S(2)}) collective-permute-start(bf16[256,640]{1,0:T(8,128)(2,1)S(1)} %get-tuple-element.70), channel_id=1, source_target_pairs={{0,4},{4,0},{1,5},{5,1},{2,6},{6,2},{3,7},{7,3},{8,12},{12,8},{9,1... | collective-permute-start | bytes 983048 | tf_op jit(solution)/shard_map/ppermute | solution.py:338
  80.1 1.3 collective-permute-done.11.refs_1_
  81.5 16.0 %all_to_all.30 = bf16[32,8,640]{2,1,0:T(8,128)(2,1)S(1)} all-to-all(bf16[32,8,640]{2,1,0:T(8,128)(2,1)S(1)} %bitcast.27), channel_id=1, replica_groups=mesh['z'=8,'y'=4,'c'=2,'x'=4] {'z','y'}, dimensions={0} | all-to-all | bytes 655360 | tf_op jit(solution)/shard_map/all_to_all | solution.py:343
  97.7 15.0 %all_to_all.31 = bf16[32,8,512]{2,1,0:T(8,128)(2,1)S(1)} all-to-all(bf16[32,8,512]{2,1,0:T(8,128)(2,1)S(1)} %bitcast.37), channel_id=1, replica_groups=mesh['z'=8,'y'=4,'c'=2,'x'=4] {'z','y'}, dimensions={0} | all-to-all | bytes 524288 | tf_op jit(solution)/shard_map/all_to_all | solution.py:343
  112.7 3.5 %collective-permute-start.12 = (bf16[256,512]{1,0:T(8,128)(2,1)S(1)}, bf16[256,512]{1,0:T(8,128)(2,1)S(1)}, u32[]{:S(2)}, u32[]{:S(2)}) collective-permute-start(bf16[256,512]{1,0:T(8,128)(2,1)S(1)} %bitcast.32), channel_id=1, source_target_pairs={{0,4},{4,0},{1,5},{5,1},{2,6},{6,2},{3,7},{7,3},{8,12},{12,8},{9,1... | collective-permute-start | bytes 786440 | tf_op jit(solution)/shard_map/ppermute | solution.py:338
  116.2 1.2 collective-permute-done.12.refs_1_
  117.4 1.2 forward.3
  118.7 1.5 collective-permute-start.14
  120.2 1.8 collective-permute-start.15
  122.0 2.0 %collective-permute-done.13.refs_1_ = bf16[208,128]{1,0:T(8,128)(2,1)S(1)} collective-permute-done((bf16[208,128]{1,0:T(8,128)(2,1)S(1)}, bf16[208,128]{1,0:T(8,128)(2,1)S(1)}, u32[]{:S(2)}, u32[]{:S(2)}) %collective-permute-start.13) | collective-permute-done | bytes 53280 | tf_op jit(solution)/shard_map/ppermute | solution.py:334
  124.3 2.8 %data.3 = (f32[64,128]{1,0:T(8,128)S(1)}, f32[64,128]{1,0:T(8,128)S(1)}, bf16[208,128]{1,0:T(8,128)(2,1)S(1)}, bf16[208,128]{1,0:T(8,128)(2,1)S(1)}, bf16[208,12...) custom-call(bf16[208,128]{1,0:T(8,128)(2,1)S(1)} %get-tuple-element.73.refs_0_, ...), custom_call_target="tpu_custom_call" | custom-call | tf_op jit(solution)/shard_map/data/pallas_call | solution.py:30
  127.2 2.5 %collective-permute-start.16 = (bf16[208,128]{1,0:T(8,128)(2,1)S(1)}, bf16[208,128]{1,0:T(8,128)(2,1)S(1)}, u32[]{:S(2)}, u32[]{:S(2)}) collective-permute-start(bf16[208,128]{1,0:T(8,128)(2,1)S(1)} %get-tuple-element.81), channel_id=1, source_target_pairs={{0,3},{1,0},{2,1},{3,2},{4,7},{5,4},{6,5},{7,6},{8,11},{9,8},{10,9... | collective-permute-start | bytes 159752 | tf_op jit(solution)/shard_map/ppermute | solution.py:334
  129.6 0.6 collective-permute-start.17
  130.3 0.5 collective-permute-done.16.refs_2_
  130.9 3.3 %collective-permute-done.17.refs_3_ = bf16[208,128]{1,0:T(8,128)(2,1)S(1)} collective-permute-done((bf16[208,128]{1,0:T(8,128)(2,1)S(1)}, bf16[208,128]{1,0:T(8,128)(2,1)S(1)}, u32[]{:S(2)}, u32[]{:S(2)}) %collective-permute-start.17) | collective-permute-done | bytes 53280 | tf_op jit(solution)/shard_map/ppermute | solution.py:334
  134.2 0.5 collective-permute-done.18.refs_4_
  134.7 0.9 back.3
  135.6 3.0 %collective-permute-start.19 = (bf16[256,640]{1,0:T(8,128)(2,1)S(1)}, bf16[256,640]{1,0:T(8,128)(2,1)S(1)}, u32[]{:S(2)}, u32[]{:S(2)}) collective-permute-start(bf16[256,640]{1,0:T(8,128)(2,1)S(1)} %get-tuple-element.85), channel_id=1, source_target_pairs={{0,4},{4,0},{1,5},{5,1},{2,6},{6,2},{3,7},{7,3},{8,12},{12,8},{9,1... | collective-permute-start | bytes 983048 | tf_op jit(solution)/shard_map/ppermute | solution.py:338
  138.6 1.3 collective-permute-done.19.refs_1_
  140.0 16.1 %all_to_all.32 = bf16[32,8,640]{2,1,0:T(8,128)(2,1)S(1)} all-to-all(bf16[32,8,640]{2,1,0:T(8,128)(2,1)S(1)} %bitcast.28), channel_id=1, replica_groups=mesh['z'=8,'y'=4,'c'=2,'x'=4] {'z','y'}, dimensions={0} | all-to-all | bytes 655360 | tf_op jit(solution)/shard_map/all_to_all | solution.py:343
  156.2 15.0 %all_to_all.33 = bf16[32,8,512]{2,1,0:T(8,128)(2,1)S(1)} all-to-all(bf16[32,8,512]{2,1,0:T(8,128)(2,1)S(1)} %bitcast.38), channel_id=1, replica_groups=mesh['z'=8,'y'=4,'c'=2,'x'=4] {'z','y'}, dimensions={0} | all-to-all | bytes 524288 | tf_op jit(solution)/shard_map/all_to_all | solution.py:343
  171.2 3.5 %collective-permute-start.20 = (bf16[256,512]{1,0:T(8,128)(2,1)S(1)}, bf16[256,512]{1,0:T(8,128)(2,1)S(1)}, u32[]{:S(2)}, u32[]{:S(2)}) collective-permute-start(bf16[256,512]{1,0:T(8,128)(2,1)S(1)} %bitcast.34), channel_id=1, source_target_pairs={{0,4},{4,0},{1,5},{5,1},{2,6},{6,2},{3,7},{7,3},{8,12},{12,8},{9,1... | collective-permute-start | bytes 786440 | tf_op jit(solution)/shard_map/ppermute | solution.py:338
  174.8 1.2 collective-permute-done.20.refs_1_
  175.9 0.4 last_model.1
  176.3 0.6 collective-permute-start.23
  176.9 1.0 collective-permute-start.22
  177.9 0.8 collective-permute-start.21
  178.7 1.4 solve.1
  180.1 0.6 slice_reduce_fusion
  180.7 0.5 collective-permute-done.22.refs_7_
  181.2 1.0 collective-permute-done.21.refs_6_
  182.2 1.2 direct.1
  (33 shorter events, 2.0 us)
Async XLA Ops:
  0.6 1.7 copy-start.1
  2.4 1.9 %copy-start.4 = (bf16[2,5,64,1024]{3,2,1,0:T(8,128)(2,1)S(1)}, bf16[2,5,64,1024]{3,2,1,0:T(8,128)(2,1)}, u32[]{:S(2)}) copy-start(bf16[2,5,64,1024]{3,2,1,0:T(8,128)(2,1)} %param.5) | copy-start | bytes 3932164
  4.3 1.7 copy-start
  5.4 7.6 %copy-start.5 = (bf16[5,64,512]{2,1,0:T(8,128)(2,1)}, bf16[5,64,512]{2,1,0:T(8,128)(2,1)S(1)}, u32[]{:S(2)}) copy-start(bf16[5,64,512]{2,1,0:T(8,128)(2,1)S(1)} %get-tuple-element.62.refs_8_) | copy-start | bytes 983044
  6.9 6.0 %collective-permute-start = (bf16[256,640]{1,0:T(8,128)(2,1)S(1)}, bf16[256,640]{1,0:T(8,128)(2,1)S(1)}, u32[]{:S(2)}, u32[]{:S(2)}) collective-permute-start(bf16[256,640]{1,0:T(8,128)(2,1)S(1)} %get-tuple-element.56), channel_id=1, source_target_pairs={{0,4},{4,0},{1,5},{5,1},{2,6},{6,2},{3,7},{7,3},{8,12},{12,8},{9,1... | collective-permute-start | bytes 983048 | tf_op jit(solution)/shard_map/ppermute | solution.py:338
  10.2 17.7 %collective-permute-start.1 = (bf16[5,128,512]{2,1,0:T(8,128)(2,1)}, bf16[5,128,512]{2,1,0:T(8,128)(2,1)S(1)}, u32[]{:S(2)}, u32[]{:S(2)}) collective-permute-start(bf16[5,128,512]{2,1,0:T(8,128)(2,1)} %get-tuple-element.50.refs_2_), channel_id=1, source_target_pairs={{0,1},{1,2},{2,3},{3,0},{4,5},{5,6},{6,7},{7,4},{8,9},{9,10},{10,1... | collective-permute-start | bytes 1966088 | tf_op jit(solution)/shard_map/ppermute | solution.py:334
  10.2 17.7 %collective-permute-start.2 = (bf16[5,128,512]{2,1,0:T(8,128)(2,1)}, bf16[5,128,512]{2,1,0:T(8,128)(2,1)}, u32[]{:S(2)}, u32[]{:S(2)}) collective-permute-start(bf16[5,128,512]{2,1,0:T(8,128)(2,1)} %get-tuple-element.52.refs_4_), channel_id=1, source_target_pairs={{0,3},{1,0},{2,1},{3,2},{4,7},{5,4},{6,5},{7,6},{8,11},{9,8},{10,9... | collective-permute-start | bytes 1966088 | tf_op jit(solution)/shard_map/ppermute | solution.py:334
  13.0 0.7 copy-start.3
  13.7 22.1 %all-to-all-start = ((bf16[32,8,640]{2,1,0:T(8,128)(2,1)}), bf16[32,8,640]{2,1,0:T(8,128)(2,1)}, u32[]{:S(2)}, u32[]{:S(2)}) async-start(bf16[32,8,640]{2,1,0:T(8,128)(2,1)} %bitcast.26), calls=%async_computation | async-start | bytes 655360 | tf_op jit(solution)/shard_map/all_to_all | solution.py:343
  28.0 17.2 %collective-permute-start.3 = (bf16[5,128,512]{2,1,0:T(8,128)(2,1)}, bf16[5,128,512]{2,1,0:T(8,128)(2,1)}, u32[]{:S(2)}, u32[]{:S(2)}) collective-permute-start(bf16[5,128,512]{2,1,0:T(8,128)(2,1)} %hold.2), channel_id=1, source_target_pairs={{0,2},{1,3},{2,0},{3,1},{4,6},{5,7},{6,4},{7,5},{8,10},{9,11},{10,... | collective-permute-start | bytes 1966088 | tf_op jit(solution)/shard_map/ppermute | solution.py:334
  37.0 0.7 copy-start.7
  37.7 0.6 copy-start.8
  38.3 15.4 %all-to-all-start.1 = ((bf16[32,8,512]{2,1,0:T(8,128)(2,1)}), bf16[32,8,512]{2,1,0:T(8,128)(2,1)S(1)}, u32[]{:S(2)}, u32[]{:S(2)}) async-start(bf16[32,8,512]{2,1,0:T(8,128)(2,1)} %bitcast.36), calls=%async_computation.1 | async-start | bytes 524288 | tf_op jit(solution)/shard_map/all_to_all | solution.py:343
  53.8 12.0 %copy-start.2 = (bf16[2,5,4,32,1024]{4,3,2,1,0:T(8,128)(2,1)S(1)}, bf16[2,5,4,32,1024]{4,3,2,1,0:T(8,128)(2,1)}, u32[]{:S(2)}) copy-start(bf16[2,5,4,32,1024]{4,3,2,1,0:T(8,128)(2,1)} %param.3) | copy-start | bytes 7864324
  53.8 12.0 %copy-start.6 = (bf16[5,64,512]{2,1,0:T(8,128)(2,1)S(1)}, bf16[5,64,512]{2,1,0:T(8,128)(2,1)}, u32[]{:S(2)}) copy-start(bf16[5,64,512]{2,1,0:T(8,128)(2,1)} %copy-done.5) | copy-start | bytes 983044
  53.8 12.0 %copy-start.9 = (f32[16,512]{1,0:T(8,128)S(1)}, f32[16,512]{1,0:T(8,128)}, u32[]{:S(2)}) copy-start(f32[16,512]{1,0:T(8,128)} %copy-done.8) | copy-start | bytes 98308
  53.8 4.8 %collective-permute-start.4 = (bf16[256,512]{1,0:T(8,128)(2,1)S(1)}, bf16[256,512]{1,0:T(8,128)(2,1)S(1)}, u32[]{:S(2)}, u32[]{:S(2)}) collective-permute-start(bf16[256,512]{1,0:T(8,128)(2,1)S(1)} %hold.3.refs_0_), channel_id=1, source_target_pairs={{0,4},{4,0},{1,5},{5,1},{2,6},{6,2},{3,7},{7,3},{8,12},{12,8},{9,1... | collective-permute-start | bytes 786440 | tf_op jit(solution)/shard_map/ppermute | solution.py:338
  59.8 5.1 %collective-permute-start.5 = (bf16[208,128]{1,0:T(8,128)(2,1)S(1)}, bf16[208,128]{1,0:T(8,128)(2,1)S(1)}, u32[]{:S(2)}, u32[]{:S(2)}) collective-permute-start(bf16[208,128]{1,0:T(8,128)(2,1)S(1)} %get-tuple-element.59), channel_id=1, source_target_pairs={{0,1},{1,2},{2,3},{3,0},{4,5},{5,6},{6,7},{7,4},{8,9},{9,10},{10,1... | collective-permute-start | bytes 159752 | tf_op jit(solution)/shard_map/ppermute | solution.py:334
  59.9 5.0 %collective-permute-start.6 = (bf16[208,128]{1,0:T(8,128)(2,1)S(1)}, bf16[208,128]{1,0:T(8,128)(2,1)S(1)}, u32[]{:S(2)}, u32[]{:S(2)}) collective-permute-start(bf16[208,128]{1,0:T(8,128)(2,1)S(1)} %get-tuple-element.60), channel_id=1, source_target_pairs={{0,2},{1,3},{2,0},{3,1},{4,6},{5,7},{6,4},{7,5},{8,10},{9,11},{10,... | collective-permute-start | bytes 159752 | tf_op jit(solution)/shard_map/ppermute | solution.py:334
  62.3 3.5 %collective-permute-start.7 = (bf16[208,128]{1,0:T(8,128)(2,1)S(1)}, bf16[208,128]{1,0:T(8,128)(2,1)S(1)}, u32[]{:S(2)}, u32[]{:S(2)}) collective-permute-start(bf16[208,128]{1,0:T(8,128)(2,1)S(1)} %get-tuple-element.61), channel_id=1, source_target_pairs={{0,3},{1,0},{2,1},{3,2},{4,7},{5,4},{6,5},{7,6},{8,11},{9,8},{10,9... | collective-permute-start | bytes 159752 | tf_op jit(solution)/shard_map/ppermute | solution.py:334
  68.6 3.5 %collective-permute-start.8 = (bf16[208,128]{1,0:T(8,128)(2,1)S(1)}, bf16[208,128]{1,0:T(8,128)(2,1)S(1)}, u32[]{:S(2)}, u32[]{:S(2)}) collective-permute-start(bf16[208,128]{1,0:T(8,128)(2,1)S(1)} %get-tuple-element.66), channel_id=1, source_target_pairs={{0,3},{1,0},{2,1},{3,2},{4,7},{5,4},{6,5},{7,6},{8,11},{9,8},{10,9... | collective-permute-start | bytes 159752 | tf_op jit(solution)/shard_map/ppermute | solution.py:334
  70.9 4.6 %collective-permute-start.9 = (bf16[208,128]{1,0:T(8,128)(2,1)S(1)}, bf16[208,128]{1,0:T(8,128)(2,1)S(1)}, u32[]{:S(2)}, u32[]{:S(2)}) collective-permute-start(bf16[208,128]{1,0:T(8,128)(2,1)S(1)} %get-tuple-element.67), channel_id=1, source_target_pairs={{0,2},{1,3},{2,0},{3,1},{4,6},{5,7},{6,4},{7,5},{8,10},{9,11},{10,... | collective-permute-start | bytes 159752 | tf_op jit(solution)/shard_map/ppermute | solution.py:334
  71.2 4.8 %collective-permute-start.10 = (bf16[208,128]{1,0:T(8,128)(2,1)S(1)}, bf16[208,128]{1,0:T(8,128)(2,1)S(1)}, u32[]{:S(2)}, u32[]{:S(2)}) collective-permute-start(bf16[208,128]{1,0:T(8,128)(2,1)S(1)} %get-tuple-element.68), channel_id=1, source_target_pairs={{0,1},{1,2},{2,3},{3,0},{4,5},{5,6},{6,7},{7,4},{8,9},{9,10},{10,1... | collective-permute-start | bytes 159752 | tf_op jit(solution)/shard_map/ppermute | solution.py:334
  76.8 4.6 %collective-permute-start.11 = (bf16[256,640]{1,0:T(8,128)(2,1)S(1)}, bf16[256,640]{1,0:T(8,128)(2,1)S(1)}, u32[]{:S(2)}, u32[]{:S(2)}) collective-permute-start(bf16[256,640]{1,0:T(8,128)(2,1)S(1)} %get-tuple-element.70), channel_id=1, source_target_pairs={{0,4},{4,0},{1,5},{5,1},{2,6},{6,2},{3,7},{7,3},{8,12},{12,8},{9,1... | collective-permute-start | bytes 983048 | tf_op jit(solution)/shard_map/ppermute | solution.py:338
  112.7 4.7 %collective-permute-start.12 = (bf16[256,512]{1,0:T(8,128)(2,1)S(1)}, bf16[256,512]{1,0:T(8,128)(2,1)S(1)}, u32[]{:S(2)}, u32[]{:S(2)}) collective-permute-start(bf16[256,512]{1,0:T(8,128)(2,1)S(1)} %bitcast.32), channel_id=1, source_target_pairs={{0,4},{4,0},{1,5},{5,1},{2,6},{6,2},{3,7},{7,3},{8,12},{12,8},{9,1... | collective-permute-start | bytes 786440 | tf_op jit(solution)/shard_map/ppermute | solution.py:338
  118.6 5.3 %collective-permute-start.13 = (bf16[208,128]{1,0:T(8,128)(2,1)S(1)}, bf16[208,128]{1,0:T(8,128)(2,1)S(1)}, u32[]{:S(2)}, u32[]{:S(2)}) collective-permute-start(bf16[208,128]{1,0:T(8,128)(2,1)S(1)} %get-tuple-element.74), channel_id=1, source_target_pairs={{0,1},{1,2},{2,3},{3,0},{4,5},{5,6},{6,7},{7,4},{8,9},{9,10},{10,1... | collective-permute-start | bytes 159752 | tf_op jit(solution)/shard_map/ppermute | solution.py:334
  118.7 5.3 %collective-permute-start.14 = (bf16[208,128]{1,0:T(8,128)(2,1)S(1)}, bf16[208,128]{1,0:T(8,128)(2,1)S(1)}, u32[]{:S(2)}, u32[]{:S(2)}) collective-permute-start(bf16[208,128]{1,0:T(8,128)(2,1)S(1)} %get-tuple-element.75), channel_id=1, source_target_pairs={{0,2},{1,3},{2,0},{3,1},{4,6},{5,7},{6,4},{7,5},{8,10},{9,11},{10,... | collective-permute-start | bytes 159752 | tf_op jit(solution)/shard_map/ppermute | solution.py:334
  120.2 4.2 %collective-permute-start.15 = (bf16[208,128]{1,0:T(8,128)(2,1)S(1)}, bf16[208,128]{1,0:T(8,128)(2,1)S(1)}, u32[]{:S(2)}, u32[]{:S(2)}) collective-permute-start(bf16[208,128]{1,0:T(8,128)(2,1)S(1)} %get-tuple-element.76), channel_id=1, source_target_pairs={{0,3},{1,0},{2,1},{3,2},{4,7},{5,4},{6,5},{7,6},{8,11},{9,8},{10,9... | collective-permute-start | bytes 159752 | tf_op jit(solution)/shard_map/ppermute | solution.py:334
  127.2 3.7 %collective-permute-start.16 = (bf16[208,128]{1,0:T(8,128)(2,1)S(1)}, bf16[208,128]{1,0:T(8,128)(2,1)S(1)}, u32[]{:S(2)}, u32[]{:S(2)}) collective-permute-start(bf16[208,128]{1,0:T(8,128)(2,1)S(1)} %get-tuple-element.81), channel_id=1, source_target_pairs={{0,3},{1,0},{2,1},{3,2},{4,7},{5,4},{6,5},{7,6},{8,11},{9,8},{10,9... | collective-permute-start | bytes 159752 | tf_op jit(solution)/shard_map/ppermute | solution.py:334
  129.6 4.5 %collective-permute-start.17 = (bf16[208,128]{1,0:T(8,128)(2,1)S(1)}, bf16[208,128]{1,0:T(8,128)(2,1)S(1)}, u32[]{:S(2)}, u32[]{:S(2)}) collective-permute-start(bf16[208,128]{1,0:T(8,128)(2,1)S(1)} %get-tuple-element.82), channel_id=1, source_target_pairs={{0,2},{1,3},{2,0},{3,1},{4,6},{5,7},{6,4},{7,5},{8,10},{9,11},{10,... | collective-permute-start | bytes 159752 | tf_op jit(solution)/shard_map/ppermute | solution.py:334
  130.2 4.5 %collective-permute-start.18 = (bf16[208,128]{1,0:T(8,128)(2,1)S(1)}, bf16[208,128]{1,0:T(8,128)(2,1)S(1)}, u32[]{:S(2)}, u32[]{:S(2)}) collective-permute-start(bf16[208,128]{1,0:T(8,128)(2,1)S(1)} %get-tuple-element.83), channel_id=1, source_target_pairs={{0,1},{1,2},{2,3},{3,0},{4,5},{5,6},{6,7},{7,4},{8,9},{9,10},{10,1... | collective-permute-start | bytes 159752 | tf_op jit(solution)/shard_map/ppermute | solution.py:334
  135.6 4.3 %collective-permute-start.19 = (bf16[256,640]{1,0:T(8,128)(2,1)S(1)}, bf16[256,640]{1,0:T(8,128)(2,1)S(1)}, u32[]{:S(2)}, u32[]{:S(2)}) collective-permute-start(bf16[256,640]{1,0:T(8,128)(2,1)S(1)} %get-tuple-element.85), channel_id=1, source_target_pairs={{0,4},{4,0},{1,5},{5,1},{2,6},{6,2},{3,7},{7,3},{8,12},{12,8},{9,1... | collective-permute-start | bytes 983048 | tf_op jit(solution)/shard_map/ppermute | solution.py:338
  171.2 4.7 %collective-permute-start.20 = (bf16[256,512]{1,0:T(8,128)(2,1)S(1)}, bf16[256,512]{1,0:T(8,128)(2,1)S(1)}, u32[]{:S(2)}, u32[]{:S(2)}) collective-permute-start(bf16[256,512]{1,0:T(8,128)(2,1)S(1)} %bitcast.34), channel_id=1, source_target_pairs={{0,4},{4,0},{1,5},{5,1},{2,6},{6,2},{3,7},{7,3},{8,12},{12,8},{9,1... | collective-permute-start | bytes 786440 | tf_op jit(solution)/shard_map/ppermute | solution.py:338
  176.3 4.4 %collective-permute-start.23 = (f32[64,128]{1,0:T(8,128)S(1)}, f32[64,128]{1,0:T(8,128)S(1)}, u32[]{:S(2)}, u32[]{:S(2)}) collective-permute-start(f32[64,128]{1,0:T(8,128)S(1)} %get-tuple-element.92.refs_7_.refs_5_), channel_id=1, source_target_pairs={{0,3},{1,0},{2,1},{3,2},{4,7},{5,4},{6,5},{7,6},{8,11},{9,8},{10,9... | collective-permute-start | bytes 98312 | tf_op jit(solution)/shard_map/ppermute | solution.py:334
  176.9 4.3 %collective-permute-start.22 = (f32[64,128]{1,0:T(8,128)S(1)}, f32[64,128]{1,0:T(8,128)S(1)}, u32[]{:S(2)}, u32[]{:S(2)}) collective-permute-start(f32[64,128]{1,0:T(8,128)S(1)} %get-tuple-element.92.refs_7_.refs_5_), channel_id=1, source_target_pairs={{0,2},{1,3},{2,0},{3,1},{4,6},{5,7},{6,4},{7,5},{8,10},{9,11},{10,... | collective-permute-start | bytes 98312 | tf_op jit(solution)/shard_map/ppermute | solution.py:334
  177.9 4.3 %collective-permute-start.21 = (f32[64,128]{1,0:T(8,128)S(1)}, f32[64,128]{1,0:T(8,128)S(1)}, u32[]{:S(2)}, u32[]{:S(2)}) collective-permute-start(f32[64,128]{1,0:T(8,128)S(1)} %get-tuple-element.92.refs_7_.refs_5_), channel_id=1, source_target_pairs={{0,1},{1,2},{2,3},{3,0},{4,5},{5,6},{6,7},{7,4},{8,9},{9,10},{10,1... | collective-permute-start | bytes 98312 | tf_op jit(solution)/shard_map/ppermute | solution.py:334

commit v6 on v5

--- a/solution.py
+++ b/solution.py
@@ -15,7 +15,7 @@
 VMEM_LIMIT = 20 * 1024 * 1024
 
 
-def call(kernel, outs, scratch=(), name=None, after=(), out_space=pltpu.VMEM):
+def call(kernel, outs, scratch=(), name=None, after=()):
     given = kernel
 
     def run(*operands):
@@ -32,7 +32,7 @@
             out_shape=[jax.ShapeDtypeStruct(out[0], out[1]) for out in outs],
             in_specs=[pl.BlockSpec(memory_space=pltpu.VMEM)] * len(operands)
             + [pl.BlockSpec(memory_space=pl.ANY)] * len(after),
-            out_specs=[pl.BlockSpec(memory_space=out_space)] * len(outs),
+            out_specs=[pl.BlockSpec(memory_space=pltpu.VMEM)] * len(outs),
             scratch_shapes=[
                 pltpu.VMEM(*entry) if isinstance(entry, tuple) else entry
                 for entry in scratch
@@ -82,7 +82,7 @@
 
 def squares_of(chunks):
     total = sum(chunk[TAIL, :].astype(F32) for chunk in chunks)
-    return to_column(jnp.sum(total, axis=0, keepdims=True))
+    return jnp.sum(total, axis=0, keepdims=True)
 
 
 def diagonal():
@@ -113,7 +113,7 @@
     for i in range(4):
         keep[:, 128 * i : 128 * i + 128] = field[i, kept, :]
         send[:, 128 * i : 128 * i + 128] = field[i, sent, :].astype(BF)
-    tail = jnp.concatenate([pieces_in_rows(to_row(squares))] * 32, axis=0)
+    tail = jnp.concatenate([pieces_in_rows(squares)] * 32, axis=0)
     keep[:, 512:640] = tail
     send[:, 512:640] = tail.astype(BF)
 
@@ -134,11 +134,11 @@
         wide = wide * wide
         total = total + sum(wide[:, 128 * i : 128 * i + 128] for i in range(8))
         slots[pair] = dot_nt(values, left[pair]).astype(BF)
-    squares[...] = jnp.broadcast_to(lane_sum(total), (64, 128))
+    squares[...] = jnp.broadcast_to(to_row(lane_sum(total)), (8, 128))
 
 
 def first_back_kernel(places, right, slots, squares, keep, send, field):
-    write_partial(places, in_slots(slots), right, squares[:, 0:1], keep, send, field)
+    write_partial(places, in_slots(slots), right, squares[0:1, :], keep, send, field)
 
 
 def pack_kernel(places, left, one, two, three):
@@ -192,13 +192,13 @@
 
 def shard_kernel(first, places, got, *refs):
     before, model_len = (None, None) if first else refs[:2]
-    state, send, column = refs[0 if first else 2 :]
+    state, send = refs[0 if first else 2 :]
     total = jnp.sum(got[...].astype(F32).reshape(32, 8, 640), axis=0)
     squares = jnp.sum(total[:, 512:640], axis=0, keepdims=True)
     data_len = jnp.sqrt(squares + EPSILON)
-    column[...] = jnp.broadcast_to(to_column(data_len), (64, 128))
     row = places[2]
-    length = column[pl.ds(row, 1), 0:1]
+    at = lax.broadcasted_iota(jnp.int32, (1, 128), 1)
+    length = lane_sum(jnp.where(at == row, data_len, 0.0))
     value = total[:, 0:512] / length
     if not first:
         ratio = length / model_len[pl.ds(row, 1), 0:1]
@@ -246,10 +246,17 @@
 
 
 def data_kernel(last, places, *refs):
-    coeffs, blocks, (left, field, state), refs = refs[:4], refs[4:7], refs[7:10], refs[10:]
+    coeffs, refs = refs[:4], refs[4:]
+    (field, state, units), refs = (refs[:3], refs[3:]) if last else ((*refs[:2], refs[-1]), refs[2:])
+    if not last:
+        blocks, refs = refs[:4], refs[4:]
+        for unit in range(5):
+            units[unit, 0:128, :] = unit_of(blocks[0], places[0], unit)
+            for step in (1, 2, 3):
+                units[unit, 128 * step : 128 * step + 128, :] = blocks[step][unit]
     model_len, data_len, outs = refs[0], refs[1], refs[2:6]
     data_len[...] = length_column(state)
-    length = jnp.sqrt(squares_of(coeffs) + EPSILON)
+    length = to_column(jnp.sqrt(squares_of(coeffs) + EPSILON))
     model_len[...] = jnp.broadcast_to(length, (64, 128))
     inverse = 1.0 / length
     ratio = length / data_len[:, 0:1]
@@ -258,8 +265,7 @@
         given = jnp.concatenate([chunk[part(i), :] for chunk in coeffs], axis=1)
         back = None
         for unit in range(2 * i, min(2 * i + 2, 5)):
-            factors = [unit_of(left, places[0], unit)] + [block[unit] for block in blocks]
-            factors = jnp.concatenate(factors, axis=0)
+            factors = units[unit]
             value = dot(given, factors) * inverse - ratio * field[unit].astype(F32)
             if not last:
                 refs[6][unit] = value
@@ -277,9 +283,8 @@
 
 def last_model_kernel(places, mine, other, state, model, data_len, squares, field):
     data_len[...] = length_column(state)
-    squares[...] = jnp.broadcast_to(
-        read_model(places, mine, other, model, field), (64, 128)
-    )
+    total = to_row(read_model(places, mine, other, model, field))
+    squares[...] = jnp.broadcast_to(total, (8, 128))
 
 
 def scalars(data_lens, model_lens):
@@ -317,17 +322,14 @@
 
 def direction_kernel(places, *refs):
     data_lens, model_lens, squares = refs[:3], refs[3:5], refs[5:9]
-    third, last_direction, out, made, sems = refs[9:]
-    copies = [pltpu.make_async_copy(made.at[t], out.at[t], sems.at[t]) for t in range(4)]
-    length = jnp.sqrt(sum(ref[:, 0:1] for ref in squares) + EPSILON)
+    third, last_direction, out = refs[9:]
+    squares = sum(ref[0:1, :] for ref in squares)
+    length = jnp.sqrt(to_column(squares) + EPSILON)
     model_lens = [ref[:, 0:1] for ref in model_lens] + [length]
     steps, residual = scalars([ref[:, 0:1] for ref in data_lens], model_lens)
     for t in range(4):
         model = third[:, 1024 * t : 1024 * t + 1024].astype(F32) / length
-        made[t] = model - steps[1][1] * last_direction[t]
-        copies[t].start()
-    for copy in copies:
-        copy.wait()
+        out[t] = model - steps[1][1] * last_direction[t]
 
 
 def shift(value, step):
@@ -362,7 +364,6 @@
         state, send = call(
             functools.partial(shard_kernel, not extra),
             [((16, 512), F32), ((256, 512), BF)],
-            [COLUMN],
             name="shard",
         )(exchange(whole), *extra)
         mine = exchange(send)
@@ -373,7 +374,7 @@
     one, two, three = call(pack_kernel, [((5, 128, 512), BF)] * 3, name="pack")(left)
     slots, squares, own_field = call(
         start_kernel,
-        [((10, 64, 128), BF), COLUMN, ((5, 64, 512), BF)],
+        [((10, 64, 128), BF), ((8, 128), F32), ((5, 64, 512), BF)],
         name="start",
         after=(one, two, three),
     )(left, observations)
@@ -387,7 +388,7 @@
         keep, swap_core(send)
     )[0]
     state, mine, other = sum_dp(whole, (), (two,))
-    field = own_field
+    field, factors = own_field, (left, *blocks)
     models, model_lens, data_lens = [], [], []
     for sweep in range(ITERS):
         model, *chunks = call(
@@ -401,12 +402,14 @@
         last = sweep == ITERS - 1
         outs = call(
             functools.partial(data_kernel, last),
-            [COLUMN, COLUMN] + CHUNKS + ([] if last else [((5, 64, 512), F32)]),
+            [COLUMN, COLUMN]
+            + CHUNKS
+            + ([] if last else [((5, 64, 512), F32), ((5, 512, 512), BF)]),
             name="data",
-        )(*chunks, *blocks, left, field, state)
+        )(*chunks, field, state, *factors)
         model_lens.append(outs[0])
         data_lens.append(outs[1])
-        field = None if last else outs[6]
+        field, factors = (None, None) if last else (outs[6], outs[7:])
         chunks = [outs[2]] + [shift(outs[2 + step], -step) for step in (1, 2, 3)]
         keep, send = call(
             back_kernel, PARTIAL, PARTIAL_SCRATCH + [((4, 64, 128), F32)], name="back"
@@ -418,7 +421,7 @@
 
     model, data_len, squares = call(
         last_model_kernel,
-        [MODEL, COLUMN, COLUMN],
+        [MODEL, COLUMN, ((8, 128), F32)],
         [((4, 512, 128), F32)],
         name="last_model",
     )(mine, other, state)
@@ -431,13 +434,7 @@
         name="solve",
         after=solve_after,
     )(*data_lens, *model_lens, *models)
-    direction = call(
-        direction_kernel,
-        [((4, 64, 1024), F32)],
-        [((4, 64, 1024), F32), pltpu.SemaphoreType.DMA((4,))],
-        name="direct",
-        out_space=pl.ANY,
-    )(
+    direction = call(direction_kernel, [((4, 64, 1024), F32)], name="direct")(
         *data_lens, *model_lens, *squares, model, last_direction
     )[0]
     return solved, direction, residual[:, 0]

time: 184 us -> 182 us (0.989)
  no operation moved by 1% of the time
where the time goes in v6:
time: 182 us
  blocking collectives  62 us (34%)
  starting transfers between devices  54.4 us (30%)
  waiting for transfers between devices  42.3 us (23%)
  Pallas kernels  16.7 us (9%)
  local copies, waits for them, and re-layouts  5.6 us (3%)
    all_to_all x4, blocking collectives, exchange(): lax.all_to_all(value.reshape(32, 8, width), ('z', 'y'), split_axis=0, con...  62 us
    ppermute x18, waiting for transfers between devices, shift(): return lax.ppermute(value, 'x', [(i, (i + step) % 4) for i in range(4)])  21.1 us
    ppermute x6, starting transfers between devices, swap_core(): return lax.ppermute(value, 'c', [(0, 1), (1, 0)])  20.4 us
    ppermute x18, starting transfers between devices, shift(): return lax.ppermute(value, 'x', [(i, (i + step) % 4) for i in range(4)])  19.4 us
    pallas_call x18, Pallas kernels, run(): pl.pallas_call(kernel, out_shape=[jax.ShapeDtypeStruct(out[0], out[1]) fo...  16.7 us
    all_to_all x2, waiting for transfers between devices, exchange(): lax.all_to_all(value.reshape(32, 8, width), ('z', 'y'), split_axis=0, con...  15.2 us
    all_to_all x2, starting transfers between devices, exchange(): lax.all_to_all(value.reshape(32, 8, width), ('z', 'y'), split_axis=0, con...  14.6 us
    ppermute x6, waiting for transfers between devices, swap_core(): return lax.ppermute(value, 'c', [(0, 1), (1, 0)])  6 us
  transfers between devices with their start and end apart: 26, of which 21 were waited for; matrix products, arithmetic and copies ran while one was open for 0% of the time, Pallas kernels for 1%

profile of v6, /device:TPU:1, one launch (start us, length us, event | category | flops | bytes accessed | tf_op | source)
XLA Modules:
  0.0 181.8 jit_solution(5959315789722053063)
XLA Ops:
  0.6 1.7 copy-done.1
  2.4 1.4 pack.1
  3.8 0.5 copy-done.4
  4.3 1.0 start.1
  5.4 0.7 copy-done
  6.0 0.9 start_sum.1
  6.9 3.3 %collective-permute-start = (bf16[256,640]{1,0:T(8,128)(2,1)S(1)}, bf16[256,640]{1,0:T(8,128)(2,1)S(1)}, u32[]{:S(2)}, u32[]{:S(2)}) collective-permute-start(bf16[256,640]{1,0:T(8,128)(2,1)S(1)} %get-tuple-element.57), channel_id=1, source_target_pairs={{0,4},{4,0},{1,5},{5,1},{2,6},{6,2},{3,7},{7,3},{8,12},{12,8},{9,1... | collective-permute-start | bytes 983048 | tf_op jit(solution)/shard_map/ppermute | solution.py:340
  10.2 2.7 %collective-permute-start.2 = (bf16[5,128,512]{2,1,0:T(8,128)(2,1)}, bf16[5,128,512]{2,1,0:T(8,128)(2,1)}, u32[]{:S(2)}, u32[]{:S(2)}) collective-permute-start(bf16[5,128,512]{2,1,0:T(8,128)(2,1)} %get-tuple-element.53.refs_4_), channel_id=1, source_target_pairs={{0,3},{1,0},{2,1},{3,2},{4,7},{5,4},{6,5},{7,6},{8,11},{9,8},{10,9... | collective-permute-start | bytes 1966088 | tf_op jit(solution)/shard_map/ppermute | solution.py:336
  13.0 0.7 copy-done.3
  13.7 9.6 %all-to-all-start = ((bf16[32,8,640]{2,1,0:T(8,128)(2,1)}), bf16[32,8,640]{2,1,0:T(8,128)(2,1)}, u32[]{:S(2)}, u32[]{:S(2)}) async-start(bf16[32,8,640]{2,1,0:T(8,128)(2,1)} %bitcast.25), calls=%async_computation | async-start | bytes 655360 | tf_op jit(solution)/shard_map/all_to_all | solution.py:345
  23.3 4.6 %collective-permute-done.1.refs_2_.refs_7_ = bf16[5,128,512]{2,1,0:T(8,128)(2,1)S(1)} collective-permute-done((bf16[5,128,512]{2,1,0:T(8,128)(2,1)}, bf16[5,128,512]{2,1,0:T(8,128)(2,1)S(1)}, u32[]{:S(2)}, u32[]{:S(2)}) %collective-permute-start.1) | collective-permute-done | bytes 655392 | tf_op jit(solution)/shard_map/ppermute | solution.py:336
  28.0 1.3 collective-permute-start.3
  29.2 6.6 %all-to-all-done = bf16[32,8,640]{2,1,0:T(8,128)(2,1)} async-done(((bf16[32,8,640]{2,1,0:T(8,128)(2,1)}), bf16[32,8,640]{2,1,0:T(8,128)(2,1)}, u32[]{:S(2)}, u32[]{:S(2)}) %all-to-all-start) | async-done | bytes 327712 | tf_op jit(solution)/shard_map/all_to_all | solution.py:345
  35.9 1.1 shard.3
  37.0 0.6 copy-done.8
  37.6 0.7 copy-done.7
  38.3 5.0 %all-to-all-start.1 = ((bf16[32,8,512]{2,1,0:T(8,128)(2,1)}), bf16[32,8,512]{2,1,0:T(8,128)(2,1)S(1)}, u32[]{:S(2)}, u32[]{:S(2)}) async-start(bf16[32,8,512]{2,1,0:T(8,128)(2,1)} %bitcast.35), calls=%async_computation.1 | async-start | bytes 524288 | tf_op jit(solution)/shard_map/all_to_all | solution.py:345
  43.3 1.9 %collective-permute-done.3.refs_1_.refs_8_ = bf16[5,128,512]{2,1,0:T(8,128)(2,1)} collective-permute-done((bf16[5,128,512]{2,1,0:T(8,128)(2,1)}, bf16[5,128,512]{2,1,0:T(8,128)(2,1)}, u32[]{:S(2)}, u32[]{:S(2)}) %collective-permute-start.3) | collective-permute-done | bytes 655392 | tf_op jit(solution)/shard_map/ppermute | solution.py:336
  45.2 8.5 %all-to-all-done.1 = bf16[32,8,512]{2,1,0:T(8,128)(2,1)S(1)} async-done(((bf16[32,8,512]{2,1,0:T(8,128)(2,1)}), bf16[32,8,512]{2,1,0:T(8,128)(2,1)S(1)}, u32[]{:S(2)}, u32[]{:S(2)}) %all-to-all-start.1) | async-done | bytes 262176 | tf_op jit(solution)/shard_map/all_to_all | solution.py:345
  53.7 3.6 %collective-permute-start.4 = (bf16[256,512]{1,0:T(8,128)(2,1)S(1)}, bf16[256,512]{1,0:T(8,128)(2,1)S(1)}, u32[]{:S(2)}, u32[]{:S(2)}) collective-permute-start(bf16[256,512]{1,0:T(8,128)(2,1)S(1)} %hold.3.refs_0_), channel_id=1, source_target_pairs={{0,4},{4,0},{1,5},{5,1},{2,6},{6,2},{3,7},{7,3},{8,12},{12,8},{9,1... | collective-permute-start | bytes 786440 | tf_op jit(solution)/shard_map/ppermute | solution.py:340
  57.3 1.2 collective-permute-done.4.refs_1_
  58.5 1.2 forward.2
  59.8 2.4 %collective-permute-start.6 = (bf16[208,128]{1,0:T(8,128)(2,1)S(1)}, bf16[208,128]{1,0:T(8,128)(2,1)S(1)}, u32[]{:S(2)}, u32[]{:S(2)}) collective-permute-start(bf16[208,128]{1,0:T(8,128)(2,1)S(1)} %get-tuple-element.61), channel_id=1, source_target_pairs={{0,2},{1,3},{2,0},{3,1},{4,6},{5,7},{6,4},{7,5},{8,10},{9,11},{10,... | collective-permute-start | bytes 159752 | tf_op jit(solution)/shard_map/ppermute | solution.py:336
  62.3 1.2 collective-permute-start.7
  63.4 1.4 collective-permute-done.5.refs_1_
  64.9 0.9 collective-permute-done.7.refs_3_
  65.7 2.9 %data.2 = (f32[64,128]{1,0:T(8,128)S(1)}, f32[64,128]{1,0:T(8,128)S(1)}, bf16[208,128]{1,0:T(8,128)(2,1)S(1)}, bf16[208,128]{1,0:T(8,128)(2,1)S(1)}, bf16[208,12...) custom-call(bf16[208,128]{1,0:T(8,128)(2,1)S(1)} %get-tuple-element., ...), custom_call_target="tpu_custom_call" | custom-call | tf_op jit(solution)/shard_map/data/pallas_call | solution.py:30
  68.6 2.3 %collective-permute-start.8 = (bf16[208,128]{1,0:T(8,128)(2,1)S(1)}, bf16[208,128]{1,0:T(8,128)(2,1)S(1)}, u32[]{:S(2)}, u32[]{:S(2)}) collective-permute-start(bf16[208,128]{1,0:T(8,128)(2,1)S(1)} %get-tuple-element.67), channel_id=1, source_target_pairs={{0,3},{1,0},{2,1},{3,2},{4,7},{5,4},{6,5},{7,6},{8,11},{9,8},{10,9... | collective-permute-start | bytes 159752 | tf_op jit(solution)/shard_map/ppermute | solution.py:336
  71.1 0.4 collective-permute-start.10
  71.6 0.5 collective-permute-done.8.refs_2_
  72.1 3.4 %collective-permute-done.9.refs_3_ = bf16[208,128]{1,0:T(8,128)(2,1)S(1)} collective-permute-done((bf16[208,128]{1,0:T(8,128)(2,1)S(1)}, bf16[208,128]{1,0:T(8,128)(2,1)S(1)}, u32[]{:S(2)}, u32[]{:S(2)}) %collective-permute-start.9) | collective-permute-done | bytes 53280 | tf_op jit(solution)/shard_map/ppermute | solution.py:336
  75.5 0.4 collective-permute-done.10.refs_4_
  75.9 0.9 back.2
  76.8 3.3 %collective-permute-start.11 = (bf16[256,640]{1,0:T(8,128)(2,1)S(1)}, bf16[256,640]{1,0:T(8,128)(2,1)S(1)}, u32[]{:S(2)}, u32[]{:S(2)}) collective-permute-start(bf16[256,640]{1,0:T(8,128)(2,1)S(1)} %get-tuple-element.71), channel_id=1, source_target_pairs={{0,4},{4,0},{1,5},{5,1},{2,6},{6,2},{3,7},{7,3},{8,12},{12,8},{9,1... | collective-permute-start | bytes 983048 | tf_op jit(solution)/shard_map/ppermute | solution.py:340
  80.1 1.3 collective-permute-done.11.refs_1_
  81.4 16.1 %all_to_all.30 = bf16[32,8,640]{2,1,0:T(8,128)(2,1)S(1)} all-to-all(bf16[32,8,640]{2,1,0:T(8,128)(2,1)S(1)} %bitcast.26), channel_id=1, replica_groups=mesh['z'=8,'y'=4,'c'=2,'x'=4] {'z','y'}, dimensions={0} | all-to-all | bytes 655360 | tf_op jit(solution)/shard_map/all_to_all | solution.py:345
  97.7 15.0 %all_to_all.31 = bf16[32,8,512]{2,1,0:T(8,128)(2,1)S(1)} all-to-all(bf16[32,8,512]{2,1,0:T(8,128)(2,1)S(1)} %bitcast.36), channel_id=1, replica_groups=mesh['z'=8,'y'=4,'c'=2,'x'=4] {'z','y'}, dimensions={0} | all-to-all | bytes 524288 | tf_op jit(solution)/shard_map/all_to_all | solution.py:345
  112.7 3.6 %collective-permute-start.12 = (bf16[256,512]{1,0:T(8,128)(2,1)S(1)}, bf16[256,512]{1,0:T(8,128)(2,1)S(1)}, u32[]{:S(2)}, u32[]{:S(2)}) collective-permute-start(bf16[256,512]{1,0:T(8,128)(2,1)S(1)} %bitcast.31), channel_id=1, source_target_pairs={{0,4},{4,0},{1,5},{5,1},{2,6},{6,2},{3,7},{7,3},{8,12},{12,8},{9,1... | collective-permute-start | bytes 786440 | tf_op jit(solution)/shard_map/ppermute | solution.py:340
  116.2 1.2 collective-permute-done.12.refs_1_
  117.4 1.2 forward.3
  118.7 1.4 collective-permute-start.14
  120.2 1.8 collective-permute-start.15
  121.9 2.1 %collective-permute-done.13.refs_1_ = bf16[208,128]{1,0:T(8,128)(2,1)S(1)} collective-permute-done((bf16[208,128]{1,0:T(8,128)(2,1)S(1)}, bf16[208,128]{1,0:T(8,128)(2,1)S(1)}, u32[]{:S(2)}, u32[]{:S(2)}) %collective-permute-start.13) | collective-permute-done | bytes 53280 | tf_op jit(solution)/shard_map/ppermute | solution.py:336
  124.3 1.5 data.3
  125.9 2.5 %collective-permute-start.16 = (bf16[208,128]{1,0:T(8,128)(2,1)S(1)}, bf16[208,128]{1,0:T(8,128)(2,1)S(1)}, u32[]{:S(2)}, u32[]{:S(2)}) collective-permute-start(bf16[208,128]{1,0:T(8,128)(2,1)S(1)} %get-tuple-element.83), channel_id=1, source_target_pairs={{0,3},{1,0},{2,1},{3,2},{4,7},{5,4},{6,5},{7,6},{8,11},{9,8},{10,9... | collective-permute-start | bytes 159752 | tf_op jit(solution)/shard_map/ppermute | solution.py:336
  128.3 0.6 collective-permute-start.17
  129.0 0.5 collective-permute-done.16.refs_2_
  129.6 3.3 %collective-permute-done.17.refs_3_ = bf16[208,128]{1,0:T(8,128)(2,1)S(1)} collective-permute-done((bf16[208,128]{1,0:T(8,128)(2,1)S(1)}, bf16[208,128]{1,0:T(8,128)(2,1)S(1)}, u32[]{:S(2)}, u32[]{:S(2)}) %collective-permute-start.17) | collective-permute-done | bytes 53280 | tf_op jit(solution)/shard_map/ppermute | solution.py:336
  132.9 0.5 collective-permute-done.18.refs_4_
  133.4 0.9 back.3
  134.3 3.0 %collective-permute-start.19 = (bf16[256,640]{1,0:T(8,128)(2,1)S(1)}, bf16[256,640]{1,0:T(8,128)(2,1)S(1)}, u32[]{:S(2)}, u32[]{:S(2)}) collective-permute-start(bf16[256,640]{1,0:T(8,128)(2,1)S(1)} %get-tuple-element.87), channel_id=1, source_target_pairs={{0,4},{4,0},{1,5},{5,1},{2,6},{6,2},{3,7},{7,3},{8,12},{12,8},{9,1... | collective-permute-start | bytes 983048 | tf_op jit(solution)/shard_map/ppermute | solution.py:340
  137.3 1.3 collective-permute-done.19.refs_1_
  138.7 16.0 %all_to_all.32 = bf16[32,8,640]{2,1,0:T(8,128)(2,1)S(1)} all-to-all(bf16[32,8,640]{2,1,0:T(8,128)(2,1)S(1)} %bitcast.27), channel_id=1, replica_groups=mesh['z'=8,'y'=4,'c'=2,'x'=4] {'z','y'}, dimensions={0} | all-to-all | bytes 655360 | tf_op jit(solution)/shard_map/all_to_all | solution.py:345
  154.9 15.0 %all_to_all.33 = bf16[32,8,512]{2,1,0:T(8,128)(2,1)S(1)} all-to-all(bf16[32,8,512]{2,1,0:T(8,128)(2,1)S(1)} %bitcast.37), channel_id=1, replica_groups=mesh['z'=8,'y'=4,'c'=2,'x'=4] {'z','y'}, dimensions={0} | all-to-all | bytes 524288 | tf_op jit(solution)/shard_map/all_to_all | solution.py:345
  169.9 3.6 %collective-permute-start.20 = (bf16[256,512]{1,0:T(8,128)(2,1)S(1)}, bf16[256,512]{1,0:T(8,128)(2,1)S(1)}, u32[]{:S(2)}, u32[]{:S(2)}) collective-permute-start(bf16[256,512]{1,0:T(8,128)(2,1)S(1)} %bitcast.33), channel_id=1, source_target_pairs={{0,4},{4,0},{1,5},{5,1},{2,6},{6,2},{3,7},{7,3},{8,12},{12,8},{9,1... | collective-permute-start | bytes 786440 | tf_op jit(solution)/shard_map/ppermute | solution.py:340
  173.4 1.2 collective-permute-done.20.refs_1_
  174.6 0.4 last_model.1
  175.0 0.6 collective-permute-start.23
  175.6 1.0 collective-permute-start.22
  176.6 0.8 collective-permute-start.21
  177.3 1.4 solve.1
  178.7 0.6 slice_reduce_fusion
  179.5 1.0 collective-permute-done.21.refs_6_
  180.5 1.3 direct.1
  (33 shorter events, 1.7 us)
Async XLA Ops:
  0.6 1.7 copy-start.1
  2.4 1.9 %copy-start.4 = (bf16[2,5,64,1024]{3,2,1,0:T(8,128)(2,1)S(1)}, bf16[2,5,64,1024]{3,2,1,0:T(8,128)(2,1)}, u32[]{:S(2)}) copy-start(bf16[2,5,64,1024]{3,2,1,0:T(8,128)(2,1)} %param.5) | copy-start | bytes 3932164
  4.3 1.7 copy-start
  5.4 7.7 %copy-start.5 = (bf16[5,64,512]{2,1,0:T(8,128)(2,1)}, bf16[5,64,512]{2,1,0:T(8,128)(2,1)S(1)}, u32[]{:S(2)}) copy-start(bf16[5,64,512]{2,1,0:T(8,128)(2,1)S(1)} %get-tuple-element.63.refs_4_) | copy-start | bytes 983044
  6.9 6.0 %collective-permute-start = (bf16[256,640]{1,0:T(8,128)(2,1)S(1)}, bf16[256,640]{1,0:T(8,128)(2,1)S(1)}, u32[]{:S(2)}, u32[]{:S(2)}) collective-permute-start(bf16[256,640]{1,0:T(8,128)(2,1)S(1)} %get-tuple-element.57), channel_id=1, source_target_pairs={{0,4},{4,0},{1,5},{5,1},{2,6},{6,2},{3,7},{7,3},{8,12},{12,8},{9,1... | collective-permute-start | bytes 983048 | tf_op jit(solution)/shard_map/ppermute | solution.py:340
  10.2 17.7 %collective-permute-start.1 = (bf16[5,128,512]{2,1,0:T(8,128)(2,1)}, bf16[5,128,512]{2,1,0:T(8,128)(2,1)S(1)}, u32[]{:S(2)}, u32[]{:S(2)}) collective-permute-start(bf16[5,128,512]{2,1,0:T(8,128)(2,1)} %get-tuple-element.51.refs_2_), channel_id=1, source_target_pairs={{0,1},{1,2},{2,3},{3,0},{4,5},{5,6},{6,7},{7,4},{8,9},{9,10},{10,1... | collective-permute-start | bytes 1966088 | tf_op jit(solution)/shard_map/ppermute | solution.py:336
  10.2 17.7 %collective-permute-start.2 = (bf16[5,128,512]{2,1,0:T(8,128)(2,1)}, bf16[5,128,512]{2,1,0:T(8,128)(2,1)}, u32[]{:S(2)}, u32[]{:S(2)}) collective-permute-start(bf16[5,128,512]{2,1,0:T(8,128)(2,1)} %get-tuple-element.53.refs_4_), channel_id=1, source_target_pairs={{0,3},{1,0},{2,1},{3,2},{4,7},{5,4},{6,5},{7,6},{8,11},{9,8},{10,9... | collective-permute-start | bytes 1966088 | tf_op jit(solution)/shard_map/ppermute | solution.py:336
  13.0 0.7 copy-start.3
  13.7 22.1 %all-to-all-start = ((bf16[32,8,640]{2,1,0:T(8,128)(2,1)}), bf16[32,8,640]{2,1,0:T(8,128)(2,1)}, u32[]{:S(2)}, u32[]{:S(2)}) async-start(bf16[32,8,640]{2,1,0:T(8,128)(2,1)} %bitcast.25), calls=%async_computation | async-start | bytes 655360 | tf_op jit(solution)/shard_map/all_to_all | solution.py:345
  28.0 17.2 %collective-permute-start.3 = (bf16[5,128,512]{2,1,0:T(8,128)(2,1)}, bf16[5,128,512]{2,1,0:T(8,128)(2,1)}, u32[]{:S(2)}, u32[]{:S(2)}) collective-permute-start(bf16[5,128,512]{2,1,0:T(8,128)(2,1)} %hold.2), channel_id=1, source_target_pairs={{0,2},{1,3},{2,0},{3,1},{4,6},{5,7},{6,4},{7,5},{8,10},{9,11},{10,... | collective-permute-start | bytes 1966088 | tf_op jit(solution)/shard_map/ppermute | solution.py:336
  37.0 0.6 copy-start.8
  37.6 0.7 copy-start.7
  38.3 15.4 %all-to-all-start.1 = ((bf16[32,8,512]{2,1,0:T(8,128)(2,1)}), bf16[32,8,512]{2,1,0:T(8,128)(2,1)S(1)}, u32[]{:S(2)}, u32[]{:S(2)}) async-start(bf16[32,8,512]{2,1,0:T(8,128)(2,1)} %bitcast.35), calls=%async_computation.1 | async-start | bytes 524288 | tf_op jit(solution)/shard_map/all_to_all | solution.py:345
  53.7 12.0 %copy-start.2 = (bf16[2,5,4,32,1024]{4,3,2,1,0:T(8,128)(2,1)S(1)}, bf16[2,5,4,32,1024]{4,3,2,1,0:T(8,128)(2,1)}, u32[]{:S(2)}) copy-start(bf16[2,5,4,32,1024]{4,3,2,1,0:T(8,128)(2,1)} %param.3) | copy-start | bytes 7864324
  53.7 12.0 %copy-start.6 = (bf16[5,64,512]{2,1,0:T(8,128)(2,1)S(1)}, bf16[5,64,512]{2,1,0:T(8,128)(2,1)}, u32[]{:S(2)}) copy-start(bf16[5,64,512]{2,1,0:T(8,128)(2,1)} %copy-done.5) | copy-start | bytes 983044
  53.7 12.0 %copy-start.9 = (f32[16,512]{1,0:T(8,128)S(1)}, f32[16,512]{1,0:T(8,128)}, u32[]{:S(2)}) copy-start(f32[16,512]{1,0:T(8,128)} %copy-done.8) | copy-start | bytes 98308
  53.7 4.8 %collective-permute-start.4 = (bf16[256,512]{1,0:T(8,128)(2,1)S(1)}, bf16[256,512]{1,0:T(8,128)(2,1)S(1)}, u32[]{:S(2)}, u32[]{:S(2)}) collective-permute-start(bf16[256,512]{1,0:T(8,128)(2,1)S(1)} %hold.3.refs_0_), channel_id=1, source_target_pairs={{0,4},{4,0},{1,5},{5,1},{2,6},{6,2},{3,7},{7,3},{8,12},{12,8},{9,1... | collective-permute-start | bytes 786440 | tf_op jit(solution)/shard_map/ppermute | solution.py:340
  59.7 5.1 %collective-permute-start.5 = (bf16[208,128]{1,0:T(8,128)(2,1)S(1)}, bf16[208,128]{1,0:T(8,128)(2,1)S(1)}, u32[]{:S(2)}, u32[]{:S(2)}) collective-permute-start(bf16[208,128]{1,0:T(8,128)(2,1)S(1)} %get-tuple-element.60), channel_id=1, source_target_pairs={{0,1},{1,2},{2,3},{3,0},{4,5},{5,6},{6,7},{7,4},{8,9},{9,10},{10,1... | collective-permute-start | bytes 159752 | tf_op jit(solution)/shard_map/ppermute | solution.py:336
  59.8 5.0 %collective-permute-start.6 = (bf16[208,128]{1,0:T(8,128)(2,1)S(1)}, bf16[208,128]{1,0:T(8,128)(2,1)S(1)}, u32[]{:S(2)}, u32[]{:S(2)}) collective-permute-start(bf16[208,128]{1,0:T(8,128)(2,1)S(1)} %get-tuple-element.61), channel_id=1, source_target_pairs={{0,2},{1,3},{2,0},{3,1},{4,6},{5,7},{6,4},{7,5},{8,10},{9,11},{10,... | collective-permute-start | bytes 159752 | tf_op jit(solution)/shard_map/ppermute | solution.py:336
  62.3 3.5 %collective-permute-start.7 = (bf16[208,128]{1,0:T(8,128)(2,1)S(1)}, bf16[208,128]{1,0:T(8,128)(2,1)S(1)}, u32[]{:S(2)}, u32[]{:S(2)}) collective-permute-start(bf16[208,128]{1,0:T(8,128)(2,1)S(1)} %get-tuple-element.62), channel_id=1, source_target_pairs={{0,3},{1,0},{2,1},{3,2},{4,7},{5,4},{6,5},{7,6},{8,11},{9,8},{10,9... | collective-permute-start | bytes 159752 | tf_op jit(solution)/shard_map/ppermute | solution.py:336
  68.6 3.5 %collective-permute-start.8 = (bf16[208,128]{1,0:T(8,128)(2,1)S(1)}, bf16[208,128]{1,0:T(8,128)(2,1)S(1)}, u32[]{:S(2)}, u32[]{:S(2)}) collective-permute-start(bf16[208,128]{1,0:T(8,128)(2,1)S(1)} %get-tuple-element.67), channel_id=1, source_target_pairs={{0,3},{1,0},{2,1},{3,2},{4,7},{5,4},{6,5},{7,6},{8,11},{9,8},{10,9... | collective-permute-start | bytes 159752 | tf_op jit(solution)/shard_map/ppermute | solution.py:336
  70.9 4.6 %collective-permute-start.9 = (bf16[208,128]{1,0:T(8,128)(2,1)S(1)}, bf16[208,128]{1,0:T(8,128)(2,1)S(1)}, u32[]{:S(2)}, u32[]{:S(2)}) collective-permute-start(bf16[208,128]{1,0:T(8,128)(2,1)S(1)} %get-tuple-element.68), channel_id=1, source_target_pairs={{0,2},{1,3},{2,0},{3,1},{4,6},{5,7},{6,4},{7,5},{8,10},{9,11},{10,... | collective-permute-start | bytes 159752 | tf_op jit(solution)/shard_map/ppermute | solution.py:336
  71.1 4.8 %collective-permute-start.10 = (bf16[208,128]{1,0:T(8,128)(2,1)S(1)}, bf16[208,128]{1,0:T(8,128)(2,1)S(1)}, u32[]{:S(2)}, u32[]{:S(2)}) collective-permute-start(bf16[208,128]{1,0:T(8,128)(2,1)S(1)} %get-tuple-element.69), channel_id=1, source_target_pairs={{0,1},{1,2},{2,3},{3,0},{4,5},{5,6},{6,7},{7,4},{8,9},{9,10},{10,1... | collective-permute-start | bytes 159752 | tf_op jit(solution)/shard_map/ppermute | solution.py:336
  76.8 4.6 %collective-permute-start.11 = (bf16[256,640]{1,0:T(8,128)(2,1)S(1)}, bf16[256,640]{1,0:T(8,128)(2,1)S(1)}, u32[]{:S(2)}, u32[]{:S(2)}) collective-permute-start(bf16[256,640]{1,0:T(8,128)(2,1)S(1)} %get-tuple-element.71), channel_id=1, source_target_pairs={{0,4},{4,0},{1,5},{5,1},{2,6},{6,2},{3,7},{7,3},{8,12},{12,8},{9,1... | collective-permute-start | bytes 983048 | tf_op jit(solution)/shard_map/ppermute | solution.py:340
  112.7 4.7 %collective-permute-start.12 = (bf16[256,512]{1,0:T(8,128)(2,1)S(1)}, bf16[256,512]{1,0:T(8,128)(2,1)S(1)}, u32[]{:S(2)}, u32[]{:S(2)}) collective-permute-start(bf16[256,512]{1,0:T(8,128)(2,1)S(1)} %bitcast.31), channel_id=1, source_target_pairs={{0,4},{4,0},{1,5},{5,1},{2,6},{6,2},{3,7},{7,3},{8,12},{12,8},{9,1... | collective-permute-start | bytes 786440 | tf_op jit(solution)/shard_map/ppermute | solution.py:340
  118.6 5.4 %collective-permute-start.13 = (bf16[208,128]{1,0:T(8,128)(2,1)S(1)}, bf16[208,128]{1,0:T(8,128)(2,1)S(1)}, u32[]{:S(2)}, u32[]{:S(2)}) collective-permute-start(bf16[208,128]{1,0:T(8,128)(2,1)S(1)} %get-tuple-element.75), channel_id=1, source_target_pairs={{0,1},{1,2},{2,3},{3,0},{4,5},{5,6},{6,7},{7,4},{8,9},{9,10},{10,1... | collective-permute-start | bytes 159752 | tf_op jit(solution)/shard_map/ppermute | solution.py:336
  118.7 5.3 %collective-permute-start.14 = (bf16[208,128]{1,0:T(8,128)(2,1)S(1)}, bf16[208,128]{1,0:T(8,128)(2,1)S(1)}, u32[]{:S(2)}, u32[]{:S(2)}) collective-permute-start(bf16[208,128]{1,0:T(8,128)(2,1)S(1)} %get-tuple-element.76), channel_id=1, source_target_pairs={{0,2},{1,3},{2,0},{3,1},{4,6},{5,7},{6,4},{7,5},{8,10},{9,11},{10,... | collective-permute-start | bytes 159752 | tf_op jit(solution)/shard_map/ppermute | solution.py:336
  120.2 4.2 %collective-permute-start.15 = (bf16[208,128]{1,0:T(8,128)(2,1)S(1)}, bf16[208,128]{1,0:T(8,128)(2,1)S(1)}, u32[]{:S(2)}, u32[]{:S(2)}) collective-permute-start(bf16[208,128]{1,0:T(8,128)(2,1)S(1)} %get-tuple-element.77), channel_id=1, source_target_pairs={{0,3},{1,0},{2,1},{3,2},{4,7},{5,4},{6,5},{7,6},{8,11},{9,8},{10,9... | collective-permute-start | bytes 159752 | tf_op jit(solution)/shard_map/ppermute | solution.py:336
  125.9 3.7 %collective-permute-start.16 = (bf16[208,128]{1,0:T(8,128)(2,1)S(1)}, bf16[208,128]{1,0:T(8,128)(2,1)S(1)}, u32[]{:S(2)}, u32[]{:S(2)}) collective-permute-start(bf16[208,128]{1,0:T(8,128)(2,1)S(1)} %get-tuple-element.83), channel_id=1, source_target_pairs={{0,3},{1,0},{2,1},{3,2},{4,7},{5,4},{6,5},{7,6},{8,11},{9,8},{10,9... | collective-permute-start | bytes 159752 | tf_op jit(solution)/shard_map/ppermute | solution.py:336
  128.3 4.5 %collective-permute-start.17 = (bf16[208,128]{1,0:T(8,128)(2,1)S(1)}, bf16[208,128]{1,0:T(8,128)(2,1)S(1)}, u32[]{:S(2)}, u32[]{:S(2)}) collective-permute-start(bf16[208,128]{1,0:T(8,128)(2,1)S(1)} %get-tuple-element.84), channel_id=1, source_target_pairs={{0,2},{1,3},{2,0},{3,1},{4,6},{5,7},{6,4},{7,5},{8,10},{9,11},{10,... | collective-permute-start | bytes 159752 | tf_op jit(solution)/shard_map/ppermute | solution.py:336
  128.9 4.5 %collective-permute-start.18 = (bf16[208,128]{1,0:T(8,128)(2,1)S(1)}, bf16[208,128]{1,0:T(8,128)(2,1)S(1)}, u32[]{:S(2)}, u32[]{:S(2)}) collective-permute-start(bf16[208,128]{1,0:T(8,128)(2,1)S(1)} %get-tuple-element.85), channel_id=1, source_target_pairs={{0,1},{1,2},{2,3},{3,0},{4,5},{5,6},{6,7},{7,4},{8,9},{9,10},{10,1... | collective-permute-start | bytes 159752 | tf_op jit(solution)/shard_map/ppermute | solution.py:336
  134.3 4.3 %collective-permute-start.19 = (bf16[256,640]{1,0:T(8,128)(2,1)S(1)}, bf16[256,640]{1,0:T(8,128)(2,1)S(1)}, u32[]{:S(2)}, u32[]{:S(2)}) collective-permute-start(bf16[256,640]{1,0:T(8,128)(2,1)S(1)} %get-tuple-element.87), channel_id=1, source_target_pairs={{0,4},{4,0},{1,5},{5,1},{2,6},{6,2},{3,7},{7,3},{8,12},{12,8},{9,1... | collective-permute-start | bytes 983048 | tf_op jit(solution)/shard_map/ppermute | solution.py:340
  169.9 4.7 %collective-permute-start.20 = (bf16[256,512]{1,0:T(8,128)(2,1)S(1)}, bf16[256,512]{1,0:T(8,128)(2,1)S(1)}, u32[]{:S(2)}, u32[]{:S(2)}) collective-permute-start(bf16[256,512]{1,0:T(8,128)(2,1)S(1)} %bitcast.33), channel_id=1, source_target_pairs={{0,4},{4,0},{1,5},{5,1},{2,6},{6,2},{3,7},{7,3},{8,12},{12,8},{9,1... | collective-permute-start | bytes 786440 | tf_op jit(solution)/shard_map/ppermute | solution.py:340
  175.0 4.4 %collective-permute-start.23 = (f32[8,128]{1,0:T(8,128)S(1)}, f32[8,128]{1,0:T(8,128)S(1)}, u32[]{:S(2)}, u32[]{:S(2)}) collective-permute-start(f32[8,128]{1,0:T(8,128)S(1)} %get-tuple-element.94.refs_7_.refs_5_), channel_id=1, source_target_pairs={{0,3},{1,0},{2,1},{3,2},{4,7},{5,4},{6,5},{7,6},{8,11},{9,8},{10,9... | collective-permute-start | bytes 12296 | tf_op jit(solution)/shard_map/ppermute | solution.py:336
  175.6 4.0 %collective-permute-start.22 = (f32[8,128]{1,0:T(8,128)S(1)}, f32[8,128]{1,0:T(8,128)S(1)}, u32[]{:S(2)}, u32[]{:S(2)}) collective-permute-start(f32[8,128]{1,0:T(8,128)S(1)} %get-tuple-element.94.refs_7_.refs_5_), channel_id=1, source_target_pairs={{0,2},{1,3},{2,0},{3,1},{4,6},{5,7},{6,4},{7,5},{8,10},{9,11},{10,... | collective-permute-start | bytes 12296 | tf_op jit(solution)/shard_map/ppermute | solution.py:336
  176.6 4.0 %collective-permute-start.21 = (f32[8,128]{1,0:T(8,128)S(1)}, f32[8,128]{1,0:T(8,128)S(1)}, u32[]{:S(2)}, u32[]{:S(2)}) collective-permute-start(f32[8,128]{1,0:T(8,128)S(1)} %get-tuple-element.94.refs_7_.refs_5_), channel_id=1, source_target_pairs={{0,1},{1,2},{2,3},{3,0},{4,5},{5,6},{6,7},{7,4},{8,9},{9,10},{10,1... | collective-permute-start | bytes 12296 | tf_op jit(solution)/shard_map/ppermute | solution.py:336

commit v7 on v6

--- a/solution.py
+++ b/solution.py
@@ -15,7 +15,7 @@
 VMEM_LIMIT = 20 * 1024 * 1024
 
 
-def call(kernel, outs, scratch=(), name=None, after=()):
+def call(kernel, outs, scratch=(), name=None, after=(), anywhere=False):
     given = kernel
 
     def run(*operands):
@@ -30,7 +30,8 @@
         return pl.pallas_call(
             kernel,
             out_shape=[jax.ShapeDtypeStruct(out[0], out[1]) for out in outs],
-            in_specs=[pl.BlockSpec(memory_space=pltpu.VMEM)] * len(operands)
+            in_specs=[pl.BlockSpec(memory_space=pl.ANY if anywhere else pltpu.VMEM)]
+            * len(operands)
             + [pl.BlockSpec(memory_space=pl.ANY)] * len(after),
             out_specs=[pl.BlockSpec(memory_space=pltpu.VMEM)] * len(outs),
             scratch_shapes=[
@@ -243,6 +244,17 @@
         chunk[part(1), :] = slots[2 * peer + 1]
         chunk[part(2), :] = slots[8 + peer // 2]
         chunk[TAIL, :] = tail
+
+
+def fetch_kernel(places, two, three, two_here, three_here, sems):
+    copies = [
+        pltpu.make_async_copy(source, target, sems.at[at])
+        for at, (source, target) in enumerate(((two, two_here), (three, three_here)))
+    ]
+    for copy in copies:
+        copy.start()
+    for copy in copies:
+        copy.wait()
 
 
 def data_kernel(last, places, *refs):
@@ -388,7 +400,16 @@
         keep, swap_core(send)
     )[0]
     state, mine, other = sum_dp(whole, (), (two,))
-    field, factors = own_field, (left, *blocks)
+    one, *blocks = blocks
+    blocks = call(
+        fetch_kernel,
+        [((5, 128, 512), BF)] * 2,
+        [pltpu.SemaphoreType.DMA((2,))],
+        name="fetch",
+        after=(mine,),
+        anywhere=True,
+    )(*blocks)
+    field, factors = own_field, (left, one, *blocks)
     models, model_lens, data_lens = [], [], []
     for sweep in range(ITERS):
         model, *chunks = call(
@@ -396,6 +417,7 @@
             [MODEL] + CHUNKS,
             [((4, 512, 128), F32), ((10, 64, 128), BF)],
             name="forward",
+            after=tuple(blocks) if sweep == 0 else (),
         )(mine, other, right)
         models.append(model)
         chunks = [chunks[0]] + [shift(chunks[step], step) for step in (1, 2, 3)]

time: 182 us -> 181 us (level)
    pallas_call x18 -> x19, Pallas kernels: 16.7 us -> 16.7 us  [run(): pl.pallas_call(kernel, out_shape=[jax.ShapeDtypeStruct(out[0], out[1]) fo...]
  transfers between devices with their start and end apart: 26 -> 26, of which waited for: 21 -> 21; matrix products, arithmetic and copies ran while one was open for 0% -> 0% of each run, Pallas kernels for 1% -> 2%
where the time goes in v7:
time: 181 us; the launch traced here: 180 us
  blocking collectives  62 us (34%)
  starting transfers between devices  54.1 us (30%)
  waiting for transfers between devices  41.1 us (23%)
  Pallas kernels  16.7 us (9%)
  local copies, waits for them, and re-layouts  5.62 us (3%)
    all_to_all x4, blocking collectives, exchange(): lax.all_to_all(value.reshape(32, 8, width), ('z', 'y'), split_axis=0, con...  62 us
    ppermute x18, waiting for transfers between devices, shift(): return lax.ppermute(value, 'x', [(i, (i + step) % 4) for i in range(4)])  21.1 us
    ppermute x6, starting transfers between devices, swap_core(): return lax.ppermute(value, 'c', [(0, 1), (1, 0)])  19.9 us
    ppermute x18, starting transfers between devices, shift(): return lax.ppermute(value, 'x', [(i, (i + step) % 4) for i in range(4)])  19.6 us
    pallas_call x19, Pallas kernels, run(): pl.pallas_call(kernel, out_shape=[jax.ShapeDtypeStruct(out[0], out[1]) fo...  16.7 us
    all_to_all x2, waiting for transfers between devices, exchange(): lax.all_to_all(value.reshape(32, 8, width), ('z', 'y'), split_axis=0, con...  15.2 us
    all_to_all x2, starting transfers between devices, exchange(): lax.all_to_all(value.reshape(32, 8, width), ('z', 'y'), split_axis=0, con...  14.6 us
    unnamed x20, local copies, waits for them, and re-layouts  4.99 us
  transfers between devices with their start and end apart: 26, of which 21 were waited for; matrix products, arithmetic and copies ran while one was open for 0% of the time, Pallas kernels for 2%

profile of v7, /device:TPU:1, one launch (start us, length us, event | category | flops | bytes accessed | tf_op | source)
XLA Modules:
  0.0 180.4 jit_solution(10263085097098258534)
XLA Ops:
  0.6 1.7 copy-done.1
  2.4 1.4 pack.1
  3.8 0.5 copy-done.4
  4.3 1.0 start.1
  5.4 0.7 copy-done
  6.0 0.9 start_sum.1
  6.9 3.3 %collective-permute-start = (bf16[256,640]{1,0:T(8,128)(2,1)S(1)}, bf16[256,640]{1,0:T(8,128)(2,1)S(1)}, u32[]{:S(2)}, u32[]{:S(2)}) collective-permute-start(bf16[256,640]{1,0:T(8,128)(2,1)S(1)} %get-tuple-element.59), channel_id=1, source_target_pairs={{0,4},{4,0},{1,5},{5,1},{2,6},{6,2},{3,7},{7,3},{8,12},{12,8},{9,1... | collective-permute-start | bytes 983048 | tf_op jit(solution)/shard_map/ppermute | solution.py:352
  10.2 2.7 %collective-permute-start.2 = (bf16[5,128,512]{2,1,0:T(8,128)(2,1)}, bf16[5,128,512]{2,1,0:T(8,128)(2,1)}, u32[]{:S(2)}, u32[]{:S(2)}) collective-permute-start(bf16[5,128,512]{2,1,0:T(8,128)(2,1)} %get-tuple-element.55.refs_4_), channel_id=1, source_target_pairs={{0,3},{1,0},{2,1},{3,2},{4,7},{5,4},{6,5},{7,6},{8,11},{9,8},{10,9... | collective-permute-start | bytes 1966088 | tf_op jit(solution)/shard_map/ppermute | solution.py:348
  13.0 0.7 copy-done.3
  13.7 9.6 %all-to-all-start = ((bf16[32,8,640]{2,1,0:T(8,128)(2,1)}), bf16[32,8,640]{2,1,0:T(8,128)(2,1)}, u32[]{:S(2)}, u32[]{:S(2)}) async-start(bf16[32,8,640]{2,1,0:T(8,128)(2,1)} %bitcast.25), calls=%async_computation | async-start | bytes 655360 | tf_op jit(solution)/shard_map/all_to_all | solution.py:357
  23.3 4.6 %collective-permute-done.1.refs_2_.refs_7_ = bf16[5,128,512]{2,1,0:T(8,128)(2,1)S(1)} collective-permute-done((bf16[5,128,512]{2,1,0:T(8,128)(2,1)}, bf16[5,128,512]{2,1,0:T(8,128)(2,1)S(1)}, u32[]{:S(2)}, u32[]{:S(2)}) %collective-permute-start.1) | collective-permute-done | bytes 655392 | tf_op jit(solution)/shard_map/ppermute | solution.py:348
  28.0 1.3 collective-permute-start.3
  29.2 6.6 %all-to-all-done = bf16[32,8,640]{2,1,0:T(8,128)(2,1)} async-done(((bf16[32,8,640]{2,1,0:T(8,128)(2,1)}), bf16[32,8,640]{2,1,0:T(8,128)(2,1)}, u32[]{:S(2)}, u32[]{:S(2)}) %all-to-all-start) | async-done | bytes 327712 | tf_op jit(solution)/shard_map/all_to_all | solution.py:357
  35.9 1.1 shard.3
  37.0 0.6 copy-done.8
  37.6 0.7 copy-done.7
  38.3 5.0 %all-to-all-start.1 = ((bf16[32,8,512]{2,1,0:T(8,128)(2,1)}), bf16[32,8,512]{2,1,0:T(8,128)(2,1)S(1)}, u32[]{:S(2)}, u32[]{:S(2)}) async-start(bf16[32,8,512]{2,1,0:T(8,128)(2,1)} %bitcast.35), calls=%async_computation.1 | async-start | bytes 524288 | tf_op jit(solution)/shard_map/all_to_all | solution.py:357
  43.3 1.9 %collective-permute-done.3.refs_1_.refs_0_ = bf16[5,128,512]{2,1,0:T(8,128)(2,1)} collective-permute-done((bf16[5,128,512]{2,1,0:T(8,128)(2,1)}, bf16[5,128,512]{2,1,0:T(8,128)(2,1)}, u32[]{:S(2)}, u32[]{:S(2)}) %collective-permute-start.3) | collective-permute-done | bytes 655392 | tf_op jit(solution)/shard_map/ppermute | solution.py:348
  45.2 8.6 %all-to-all-done.1 = bf16[32,8,512]{2,1,0:T(8,128)(2,1)S(1)} async-done(((bf16[32,8,512]{2,1,0:T(8,128)(2,1)}), bf16[32,8,512]{2,1,0:T(8,128)(2,1)S(1)}, u32[]{:S(2)}, u32[]{:S(2)}) %all-to-all-start.1) | async-done | bytes 262176 | tf_op jit(solution)/shard_map/all_to_all | solution.py:357
  53.7 3.6 %collective-permute-start.4 = (bf16[256,512]{1,0:T(8,128)(2,1)S(1)}, bf16[256,512]{1,0:T(8,128)(2,1)S(1)}, u32[]{:S(2)}, u32[]{:S(2)}) collective-permute-start(bf16[256,512]{1,0:T(8,128)(2,1)S(1)} %hold.3.refs_2_.refs_0_), channel_id=1, source_target_pairs={{0,4},{4,0},{1,5},{5,1},{2,6},{6,2},{3,7},{7,3},{8,12},{12,8},{9,1... | collective-permute-start | bytes 786440 | tf_op jit(solution)/shard_map/ppermute | solution.py:352
  57.3 1.3 fetch.1
  58.6 1.2 forward.2
  59.9 2.4 %collective-permute-start.6 = (bf16[208,128]{1,0:T(8,128)(2,1)S(1)}, bf16[208,128]{1,0:T(8,128)(2,1)S(1)}, u32[]{:S(2)}, u32[]{:S(2)}) collective-permute-start(bf16[208,128]{1,0:T(8,128)(2,1)S(1)} %get-tuple-element.65), channel_id=1, source_target_pairs={{0,2},{1,3},{2,0},{3,1},{4,6},{5,7},{6,4},{7,5},{8,10},{9,11},{10,... | collective-permute-start | bytes 159752 | tf_op jit(solution)/shard_map/ppermute | solution.py:348
  62.4 1.2 collective-permute-start.7
  63.5 1.3 collective-permute-done.5.refs_1_
  65.1 0.9 collective-permute-done.7.refs_3_
  66.0 1.6 data.2
  67.5 2.4 %collective-permute-start.8 = (bf16[208,128]{1,0:T(8,128)(2,1)S(1)}, bf16[208,128]{1,0:T(8,128)(2,1)S(1)}, u32[]{:S(2)}, u32[]{:S(2)}) collective-permute-start(bf16[208,128]{1,0:T(8,128)(2,1)S(1)} %get-tuple-element.71), channel_id=1, source_target_pairs={{0,3},{1,0},{2,1},{3,2},{4,7},{5,4},{6,5},{7,6},{8,11},{9,8},{10,9... | collective-permute-start | bytes 159752 | tf_op jit(solution)/shard_map/ppermute | solution.py:348
  70.2 0.5 collective-permute-start.10
  70.6 0.5 collective-permute-done.8.refs_2_
  71.2 3.4 %collective-permute-done.9.refs_3_ = bf16[208,128]{1,0:T(8,128)(2,1)S(1)} collective-permute-done((bf16[208,128]{1,0:T(8,128)(2,1)S(1)}, bf16[208,128]{1,0:T(8,128)(2,1)S(1)}, u32[]{:S(2)}, u32[]{:S(2)}) %collective-permute-start.9) | collective-permute-done | bytes 53280 | tf_op jit(solution)/shard_map/ppermute | solution.py:348
  74.6 0.4 collective-permute-done.10.refs_4_
  75.0 0.9 back.2
  75.8 2.9 %collective-permute-start.11 = (bf16[256,640]{1,0:T(8,128)(2,1)S(1)}, bf16[256,640]{1,0:T(8,128)(2,1)S(1)}, u32[]{:S(2)}, u32[]{:S(2)}) collective-permute-start(bf16[256,640]{1,0:T(8,128)(2,1)S(1)} %get-tuple-element.75), channel_id=1, source_target_pairs={{0,4},{4,0},{1,5},{5,1},{2,6},{6,2},{3,7},{7,3},{8,12},{12,8},{9,1... | collective-permute-start | bytes 983048 | tf_op jit(solution)/shard_map/ppermute | solution.py:352
  78.8 1.3 collective-permute-done.11.refs_1_
  80.1 16.0 %all_to_all.30 = bf16[32,8,640]{2,1,0:T(8,128)(2,1)S(1)} all-to-all(bf16[32,8,640]{2,1,0:T(8,128)(2,1)S(1)} %bitcast.26), channel_id=1, replica_groups=mesh['z'=8,'y'=4,'c'=2,'x'=4] {'z','y'}, dimensions={0} | all-to-all | bytes 655360 | tf_op jit(solution)/shard_map/all_to_all | solution.py:357
  96.3 15.0 %all_to_all.31 = bf16[32,8,512]{2,1,0:T(8,128)(2,1)S(1)} all-to-all(bf16[32,8,512]{2,1,0:T(8,128)(2,1)S(1)} %bitcast.36), channel_id=1, replica_groups=mesh['z'=8,'y'=4,'c'=2,'x'=4] {'z','y'}, dimensions={0} | all-to-all | bytes 524288 | tf_op jit(solution)/shard_map/all_to_all | solution.py:357
  111.3 3.6 %collective-permute-start.12 = (bf16[256,512]{1,0:T(8,128)(2,1)S(1)}, bf16[256,512]{1,0:T(8,128)(2,1)S(1)}, u32[]{:S(2)}, u32[]{:S(2)}) collective-permute-start(bf16[256,512]{1,0:T(8,128)(2,1)S(1)} %bitcast.31), channel_id=1, source_target_pairs={{0,4},{4,0},{1,5},{5,1},{2,6},{6,2},{3,7},{7,3},{8,12},{12,8},{9,1... | collective-permute-start | bytes 786440 | tf_op jit(solution)/shard_map/ppermute | solution.py:352
  114.8 1.2 collective-permute-done.12.refs_1_
  116.0 1.2 forward.3
  117.3 1.5 collective-permute-start.14
  118.8 1.8 collective-permute-start.15
  120.6 2.1 %collective-permute-done.13.refs_1_ = bf16[208,128]{1,0:T(8,128)(2,1)S(1)} collective-permute-done((bf16[208,128]{1,0:T(8,128)(2,1)S(1)}, bf16[208,128]{1,0:T(8,128)(2,1)S(1)}, u32[]{:S(2)}, u32[]{:S(2)}) %collective-permute-start.13) | collective-permute-done | bytes 53280 | tf_op jit(solution)/shard_map/ppermute | solution.py:348
  123.0 1.5 data.3
  124.5 2.5 %collective-permute-start.16 = (bf16[208,128]{1,0:T(8,128)(2,1)S(1)}, bf16[208,128]{1,0:T(8,128)(2,1)S(1)}, u32[]{:S(2)}, u32[]{:S(2)}) collective-permute-start(bf16[208,128]{1,0:T(8,128)(2,1)S(1)} %get-tuple-element.87), channel_id=1, source_target_pairs={{0,3},{1,0},{2,1},{3,2},{4,7},{5,4},{6,5},{7,6},{8,11},{9,8},{10,9... | collective-permute-start | bytes 159752 | tf_op jit(solution)/shard_map/ppermute | solution.py:348
  127.0 0.6 collective-permute-start.17
  127.6 0.5 collective-permute-done.16.refs_2_
  128.2 3.3 %collective-permute-done.17.refs_3_ = bf16[208,128]{1,0:T(8,128)(2,1)S(1)} collective-permute-done((bf16[208,128]{1,0:T(8,128)(2,1)S(1)}, bf16[208,128]{1,0:T(8,128)(2,1)S(1)}, u32[]{:S(2)}, u32[]{:S(2)}) %collective-permute-start.17) | collective-permute-done | bytes 53280 | tf_op jit(solution)/shard_map/ppermute | solution.py:348
  131.5 0.5 collective-permute-done.18.refs_4_
  132.0 0.9 back.3
  132.9 3.0 %collective-permute-start.19 = (bf16[256,640]{1,0:T(8,128)(2,1)S(1)}, bf16[256,640]{1,0:T(8,128)(2,1)S(1)}, u32[]{:S(2)}, u32[]{:S(2)}) collective-permute-start(bf16[256,640]{1,0:T(8,128)(2,1)S(1)} %get-tuple-element.91), channel_id=1, source_target_pairs={{0,4},{4,0},{1,5},{5,1},{2,6},{6,2},{3,7},{7,3},{8,12},{12,8},{9,1... | collective-permute-start | bytes 983048 | tf_op jit(solution)/shard_map/ppermute | solution.py:352
  135.9 1.3 collective-permute-done.19.refs_1_
  137.3 16.0 %all_to_all.32 = bf16[32,8,640]{2,1,0:T(8,128)(2,1)S(1)} all-to-all(bf16[32,8,640]{2,1,0:T(8,128)(2,1)S(1)} %bitcast.27), channel_id=1, replica_groups=mesh['z'=8,'y'=4,'c'=2,'x'=4] {'z','y'}, dimensions={0} | all-to-all | bytes 655360 | tf_op jit(solution)/shard_map/all_to_all | solution.py:357
  153.5 15.0 %all_to_all.33 = bf16[32,8,512]{2,1,0:T(8,128)(2,1)S(1)} all-to-all(bf16[32,8,512]{2,1,0:T(8,128)(2,1)S(1)} %bitcast.37), channel_id=1, replica_groups=mesh['z'=8,'y'=4,'c'=2,'x'=4] {'z','y'}, dimensions={0} | all-to-all | bytes 524288 | tf_op jit(solution)/shard_map/all_to_all | solution.py:357
  168.5 3.6 %collective-permute-start.20 = (bf16[256,512]{1,0:T(8,128)(2,1)S(1)}, bf16[256,512]{1,0:T(8,128)(2,1)S(1)}, u32[]{:S(2)}, u32[]{:S(2)}) collective-permute-start(bf16[256,512]{1,0:T(8,128)(2,1)S(1)} %bitcast.33), channel_id=1, source_target_pairs={{0,4},{4,0},{1,5},{5,1},{2,6},{6,2},{3,7},{7,3},{8,12},{12,8},{9,1... | collective-permute-start | bytes 786440 | tf_op jit(solution)/shard_map/ppermute | solution.py:352
  172.0 1.2 collective-permute-done.20.refs_1_
  173.2 0.4 last_model.1
  173.6 0.6 collective-permute-start.23
  174.2 1.0 collective-permute-start.22
  175.2 0.8 collective-permute-start.21
  175.9 1.4 solve.1
  177.4 0.6 slice_reduce_fusion
  178.1 1.0 collective-permute-done.21.refs_6_
  179.1 1.3 direct.1
  (34 shorter events, 1.8 us)
Async XLA Ops:
  0.6 1.7 copy-start.1
  2.4 1.9 %copy-start.4 = (bf16[2,5,64,1024]{3,2,1,0:T(8,128)(2,1)S(1)}, bf16[2,5,64,1024]{3,2,1,0:T(8,128)(2,1)}, u32[]{:S(2)}) copy-start(bf16[2,5,64,1024]{3,2,1,0:T(8,128)(2,1)} %param.5) | copy-start | bytes 3932164
  4.3 1.7 copy-start
  5.4 7.7 %copy-start.5 = (bf16[5,64,512]{2,1,0:T(8,128)(2,1)}, bf16[5,64,512]{2,1,0:T(8,128)(2,1)S(1)}, u32[]{:S(2)}) copy-start(bf16[5,64,512]{2,1,0:T(8,128)(2,1)S(1)} %get-tuple-element.67.refs_4_) | copy-start | bytes 983044
  6.9 6.0 %collective-permute-start = (bf16[256,640]{1,0:T(8,128)(2,1)S(1)}, bf16[256,640]{1,0:T(8,128)(2,1)S(1)}, u32[]{:S(2)}, u32[]{:S(2)}) collective-permute-start(bf16[256,640]{1,0:T(8,128)(2,1)S(1)} %get-tuple-element.59), channel_id=1, source_target_pairs={{0,4},{4,0},{1,5},{5,1},{2,6},{6,2},{3,7},{7,3},{8,12},{12,8},{9,1... | collective-permute-start | bytes 983048 | tf_op jit(solution)/shard_map/ppermute | solution.py:352
  10.2 17.7 %collective-permute-start.1 = (bf16[5,128,512]{2,1,0:T(8,128)(2,1)}, bf16[5,128,512]{2,1,0:T(8,128)(2,1)S(1)}, u32[]{:S(2)}, u32[]{:S(2)}) collective-permute-start(bf16[5,128,512]{2,1,0:T(8,128)(2,1)} %get-tuple-element.53.refs_2_), channel_id=1, source_target_pairs={{0,1},{1,2},{2,3},{3,0},{4,5},{5,6},{6,7},{7,4},{8,9},{9,10},{10,1... | collective-permute-start | bytes 1966088 | tf_op jit(solution)/shard_map/ppermute | solution.py:348
  10.2 17.7 %collective-permute-start.2 = (bf16[5,128,512]{2,1,0:T(8,128)(2,1)}, bf16[5,128,512]{2,1,0:T(8,128)(2,1)}, u32[]{:S(2)}, u32[]{:S(2)}) collective-permute-start(bf16[5,128,512]{2,1,0:T(8,128)(2,1)} %get-tuple-element.55.refs_4_), channel_id=1, source_target_pairs={{0,3},{1,0},{2,1},{3,2},{4,7},{5,4},{6,5},{7,6},{8,11},{9,8},{10,9... | collective-permute-start | bytes 1966088 | tf_op jit(solution)/shard_map/ppermute | solution.py:348
  13.0 0.7 copy-start.3
  13.7 22.1 %all-to-all-start = ((bf16[32,8,640]{2,1,0:T(8,128)(2,1)}), bf16[32,8,640]{2,1,0:T(8,128)(2,1)}, u32[]{:S(2)}, u32[]{:S(2)}) async-start(bf16[32,8,640]{2,1,0:T(8,128)(2,1)} %bitcast.25), calls=%async_computation | async-start | bytes 655360 | tf_op jit(solution)/shard_map/all_to_all | solution.py:357
  28.0 17.2 %collective-permute-start.3 = (bf16[5,128,512]{2,1,0:T(8,128)(2,1)}, bf16[5,128,512]{2,1,0:T(8,128)(2,1)}, u32[]{:S(2)}, u32[]{:S(2)}) collective-permute-start(bf16[5,128,512]{2,1,0:T(8,128)(2,1)} %hold.2), channel_id=1, source_target_pairs={{0,2},{1,3},{2,0},{3,1},{4,6},{5,7},{6,4},{7,5},{8,10},{9,11},{10,... | collective-permute-start | bytes 1966088 | tf_op jit(solution)/shard_map/ppermute | solution.py:348
  37.0 0.6 copy-start.8
  37.6 0.7 copy-start.7
  38.3 15.4 %all-to-all-start.1 = ((bf16[32,8,512]{2,1,0:T(8,128)(2,1)}), bf16[32,8,512]{2,1,0:T(8,128)(2,1)S(1)}, u32[]{:S(2)}, u32[]{:S(2)}) async-start(bf16[32,8,512]{2,1,0:T(8,128)(2,1)} %bitcast.35), calls=%async_computation.1 | async-start | bytes 524288 | tf_op jit(solution)/shard_map/all_to_all | solution.py:357
  53.7 4.9 %collective-permute-start.4 = (bf16[256,512]{1,0:T(8,128)(2,1)S(1)}, bf16[256,512]{1,0:T(8,128)(2,1)S(1)}, u32[]{:S(2)}, u32[]{:S(2)}) collective-permute-start(bf16[256,512]{1,0:T(8,128)(2,1)S(1)} %hold.3.refs_2_.refs_0_), channel_id=1, source_target_pairs={{0,4},{4,0},{1,5},{5,1},{2,6},{6,2},{3,7},{7,3},{8,12},{12,8},{9,1... | collective-permute-start | bytes 786440 | tf_op jit(solution)/shard_map/ppermute | solution.py:352
  58.6 7.4 %copy-start.2 = (bf16[2,5,4,32,1024]{4,3,2,1,0:T(8,128)(2,1)S(1)}, bf16[2,5,4,32,1024]{4,3,2,1,0:T(8,128)(2,1)}, u32[]{:S(2)}) copy-start(bf16[2,5,4,32,1024]{4,3,2,1,0:T(8,128)(2,1)} %param.3) | copy-start | bytes 7864324
  58.6 7.4 %copy-start.6 = (bf16[5,64,512]{2,1,0:T(8,128)(2,1)S(1)}, bf16[5,64,512]{2,1,0:T(8,128)(2,1)}, u32[]{:S(2)}) copy-start(bf16[5,64,512]{2,1,0:T(8,128)(2,1)} %copy-done.5) | copy-start | bytes 983044
  58.6 7.4 %copy-start.9 = (f32[16,512]{1,0:T(8,128)S(1)}, f32[16,512]{1,0:T(8,128)}, u32[]{:S(2)}) copy-start(f32[16,512]{1,0:T(8,128)} %copy-done.8) | copy-start | bytes 98308
  59.9 5.0 %collective-permute-start.5 = (bf16[208,128]{1,0:T(8,128)(2,1)S(1)}, bf16[208,128]{1,0:T(8,128)(2,1)S(1)}, u32[]{:S(2)}, u32[]{:S(2)}) collective-permute-start(bf16[208,128]{1,0:T(8,128)(2,1)S(1)} %get-tuple-element.64), channel_id=1, source_target_pairs={{0,1},{1,2},{2,3},{3,0},{4,5},{5,6},{6,7},{7,4},{8,9},{9,10},{10,1... | collective-permute-start | bytes 159752 | tf_op jit(solution)/shard_map/ppermute | solution.py:348
  59.9 5.1 %collective-permute-start.6 = (bf16[208,128]{1,0:T(8,128)(2,1)S(1)}, bf16[208,128]{1,0:T(8,128)(2,1)S(1)}, u32[]{:S(2)}, u32[]{:S(2)}) collective-permute-start(bf16[208,128]{1,0:T(8,128)(2,1)S(1)} %get-tuple-element.65), channel_id=1, source_target_pairs={{0,2},{1,3},{2,0},{3,1},{4,6},{5,7},{6,4},{7,5},{8,10},{9,11},{10,... | collective-permute-start | bytes 159752 | tf_op jit(solution)/shard_map/ppermute | solution.py:348
  62.4 3.6 %collective-permute-start.7 = (bf16[208,128]{1,0:T(8,128)(2,1)S(1)}, bf16[208,128]{1,0:T(8,128)(2,1)S(1)}, u32[]{:S(2)}, u32[]{:S(2)}) collective-permute-start(bf16[208,128]{1,0:T(8,128)(2,1)S(1)} %get-tuple-element.66), channel_id=1, source_target_pairs={{0,3},{1,0},{2,1},{3,2},{4,7},{5,4},{6,5},{7,6},{8,11},{9,8},{10,9... | collective-permute-start | bytes 159752 | tf_op jit(solution)/shard_map/ppermute | solution.py:348
  67.5 3.6 %collective-permute-start.8 = (bf16[208,128]{1,0:T(8,128)(2,1)S(1)}, bf16[208,128]{1,0:T(8,128)(2,1)S(1)}, u32[]{:S(2)}, u32[]{:S(2)}) collective-permute-start(bf16[208,128]{1,0:T(8,128)(2,1)S(1)} %get-tuple-element.71), channel_id=1, source_target_pairs={{0,3},{1,0},{2,1},{3,2},{4,7},{5,4},{6,5},{7,6},{8,11},{9,8},{10,9... | collective-permute-start | bytes 159752 | tf_op jit(solution)/shard_map/ppermute | solution.py:348
  70.0 4.6 %collective-permute-start.9 = (bf16[208,128]{1,0:T(8,128)(2,1)S(1)}, bf16[208,128]{1,0:T(8,128)(2,1)S(1)}, u32[]{:S(2)}, u32[]{:S(2)}) collective-permute-start(bf16[208,128]{1,0:T(8,128)(2,1)S(1)} %get-tuple-element.72), channel_id=1, source_target_pairs={{0,2},{1,3},{2,0},{3,1},{4,6},{5,7},{6,4},{7,5},{8,10},{9,11},{10,... | collective-permute-start | bytes 159752 | tf_op jit(solution)/shard_map/ppermute | solution.py:348
  70.2 4.8 %collective-permute-start.10 = (bf16[208,128]{1,0:T(8,128)(2,1)S(1)}, bf16[208,128]{1,0:T(8,128)(2,1)S(1)}, u32[]{:S(2)}, u32[]{:S(2)}) collective-permute-start(bf16[208,128]{1,0:T(8,128)(2,1)S(1)} %get-tuple-element.73), channel_id=1, source_target_pairs={{0,1},{1,2},{2,3},{3,0},{4,5},{5,6},{6,7},{7,4},{8,9},{9,10},{10,1... | collective-permute-start | bytes 159752 | tf_op jit(solution)/shard_map/ppermute | solution.py:348
  75.8 4.2 %collective-permute-start.11 = (bf16[256,640]{1,0:T(8,128)(2,1)S(1)}, bf16[256,640]{1,0:T(8,128)(2,1)S(1)}, u32[]{:S(2)}, u32[]{:S(2)}) collective-permute-start(bf16[256,640]{1,0:T(8,128)(2,1)S(1)} %get-tuple-element.75), channel_id=1, source_target_pairs={{0,4},{4,0},{1,5},{5,1},{2,6},{6,2},{3,7},{7,3},{8,12},{12,8},{9,1... | collective-permute-start | bytes 983048 | tf_op jit(solution)/shard_map/ppermute | solution.py:352
  111.3 4.7 %collective-permute-start.12 = (bf16[256,512]{1,0:T(8,128)(2,1)S(1)}, bf16[256,512]{1,0:T(8,128)(2,1)S(1)}, u32[]{:S(2)}, u32[]{:S(2)}) collective-permute-start(bf16[256,512]{1,0:T(8,128)(2,1)S(1)} %bitcast.31), channel_id=1, source_target_pairs={{0,4},{4,0},{1,5},{5,1},{2,6},{6,2},{3,7},{7,3},{8,12},{12,8},{9,1... | collective-permute-start | bytes 786440 | tf_op jit(solution)/shard_map/ppermute | solution.py:352
  117.2 5.4 %collective-permute-start.13 = (bf16[208,128]{1,0:T(8,128)(2,1)S(1)}, bf16[208,128]{1,0:T(8,128)(2,1)S(1)}, u32[]{:S(2)}, u32[]{:S(2)}) collective-permute-start(bf16[208,128]{1,0:T(8,128)(2,1)S(1)} %get-tuple-element.79), channel_id=1, source_target_pairs={{0,1},{1,2},{2,3},{3,0},{4,5},{5,6},{6,7},{7,4},{8,9},{9,10},{10,1... | collective-permute-start | bytes 159752 | tf_op jit(solution)/shard_map/ppermute | solution.py:348
  117.3 5.3 %collective-permute-start.14 = (bf16[208,128]{1,0:T(8,128)(2,1)S(1)}, bf16[208,128]{1,0:T(8,128)(2,1)S(1)}, u32[]{:S(2)}, u32[]{:S(2)}) collective-permute-start(bf16[208,128]{1,0:T(8,128)(2,1)S(1)} %get-tuple-element.80), channel_id=1, source_target_pairs={{0,2},{1,3},{2,0},{3,1},{4,6},{5,7},{6,4},{7,5},{8,10},{9,11},{10,... | collective-permute-start | bytes 159752 | tf_op jit(solution)/shard_map/ppermute | solution.py:348
  118.8 4.2 %collective-permute-start.15 = (bf16[208,128]{1,0:T(8,128)(2,1)S(1)}, bf16[208,128]{1,0:T(8,128)(2,1)S(1)}, u32[]{:S(2)}, u32[]{:S(2)}) collective-permute-start(bf16[208,128]{1,0:T(8,128)(2,1)S(1)} %get-tuple-element.81), channel_id=1, source_target_pairs={{0,3},{1,0},{2,1},{3,2},{4,7},{5,4},{6,5},{7,6},{8,11},{9,8},{10,9... | collective-permute-start | bytes 159752 | tf_op jit(solution)/shard_map/ppermute | solution.py:348
  124.5 3.7 %collective-permute-start.16 = (bf16[208,128]{1,0:T(8,128)(2,1)S(1)}, bf16[208,128]{1,0:T(8,128)(2,1)S(1)}, u32[]{:S(2)}, u32[]{:S(2)}) collective-permute-start(bf16[208,128]{1,0:T(8,128)(2,1)S(1)} %get-tuple-element.87), channel_id=1, source_target_pairs={{0,3},{1,0},{2,1},{3,2},{4,7},{5,4},{6,5},{7,6},{8,11},{9,8},{10,9... | collective-permute-start | bytes 159752 | tf_op jit(solution)/shard_map/ppermute | solution.py:348
  127.0 4.5 %collective-permute-start.17 = (bf16[208,128]{1,0:T(8,128)(2,1)S(1)}, bf16[208,128]{1,0:T(8,128)(2,1)S(1)}, u32[]{:S(2)}, u32[]{:S(2)}) collective-permute-start(bf16[208,128]{1,0:T(8,128)(2,1)S(1)} %get-tuple-element.88), channel_id=1, source_target_pairs={{0,2},{1,3},{2,0},{3,1},{4,6},{5,7},{6,4},{7,5},{8,10},{9,11},{10,... | collective-permute-start | bytes 159752 | tf_op jit(solution)/shard_map/ppermute | solution.py:348
  127.5 4.5 %collective-permute-start.18 = (bf16[208,128]{1,0:T(8,128)(2,1)S(1)}, bf16[208,128]{1,0:T(8,128)(2,1)S(1)}, u32[]{:S(2)}, u32[]{:S(2)}) collective-permute-start(bf16[208,128]{1,0:T(8,128)(2,1)S(1)} %get-tuple-element.89), channel_id=1, source_target_pairs={{0,1},{1,2},{2,3},{3,0},{4,5},{5,6},{6,7},{7,4},{8,9},{9,10},{10,1... | collective-permute-start | bytes 159752 | tf_op jit(solution)/shard_map/ppermute | solution.py:348
  132.9 4.3 %collective-permute-start.19 = (bf16[256,640]{1,0:T(8,128)(2,1)S(1)}, bf16[256,640]{1,0:T(8,128)(2,1)S(1)}, u32[]{:S(2)}, u32[]{:S(2)}) collective-permute-start(bf16[256,640]{1,0:T(8,128)(2,1)S(1)} %get-tuple-element.91), channel_id=1, source_target_pairs={{0,4},{4,0},{1,5},{5,1},{2,6},{6,2},{3,7},{7,3},{8,12},{12,8},{9,1... | collective-permute-start | bytes 983048 | tf_op jit(solution)/shard_map/ppermute | solution.py:352
  168.5 4.7 %collective-permute-start.20 = (bf16[256,512]{1,0:T(8,128)(2,1)S(1)}, bf16[256,512]{1,0:T(8,128)(2,1)S(1)}, u32[]{:S(2)}, u32[]{:S(2)}) collective-permute-start(bf16[256,512]{1,0:T(8,128)(2,1)S(1)} %bitcast.33), channel_id=1, source_target_pairs={{0,4},{4,0},{1,5},{5,1},{2,6},{6,2},{3,7},{7,3},{8,12},{12,8},{9,1... | collective-permute-start | bytes 786440 | tf_op jit(solution)/shard_map/ppermute | solution.py:352
  173.6 4.4 %collective-permute-start.23 = (f32[8,128]{1,0:T(8,128)S(1)}, f32[8,128]{1,0:T(8,128)S(1)}, u32[]{:S(2)}, u32[]{:S(2)}) collective-permute-start(f32[8,128]{1,0:T(8,128)S(1)} %get-tuple-element.98.refs_7_.refs_5_), channel_id=1, source_target_pairs={{0,3},{1,0},{2,1},{3,2},{4,7},{5,4},{6,5},{7,6},{8,11},{9,8},{10,9... | collective-permute-start | bytes 12296 | tf_op jit(solution)/shard_map/ppermute | solution.py:348
  174.2 4.0 %collective-permute-start.22 = (f32[8,128]{1,0:T(8,128)S(1)}, f32[8,128]{1,0:T(8,128)S(1)}, u32[]{:S(2)}, u32[]{:S(2)}) collective-permute-start(f32[8,128]{1,0:T(8,128)S(1)} %get-tuple-element.98.refs_7_.refs_5_), channel_id=1, source_target_pairs={{0,2},{1,3},{2,0},{3,1},{4,6},{5,7},{6,4},{7,5},{8,10},{9,11},{10,... | collective-permute-start | bytes 12296 | tf_op jit(solution)/shard_map/ppermute | solution.py:348
  175.2 4.0 %collective-permute-start.21 = (f32[8,128]{1,0:T(8,128)S(1)}, f32[8,128]{1,0:T(8,128)S(1)}, u32[]{:S(2)}, u32[]{:S(2)}) collective-permute-start(f32[8,128]{1,0:T(8,128)S(1)} %get-tuple-element.98.refs_7_.refs_5_), channel_id=1, source_target_pairs={{0,1},{1,2},{2,3},{3,0},{4,5},{5,6},{6,7},{7,4},{8,9},{9,10},{10,1... | collective-permute-start | bytes 12296 | tf_op jit(solution)/shard_map/ppermute | solution.py:348

commit v8 on v7

--- a/solution.py
+++ b/solution.py
@@ -15,7 +15,7 @@
 VMEM_LIMIT = 20 * 1024 * 1024
 
 
-def call(kernel, outs, scratch=(), name=None, after=(), anywhere=False):
+def call(kernel, outs, scratch=(), name=None, after=(), anywhere=False, out_space=pltpu.VMEM):
     given = kernel
 
     def run(*operands):
@@ -33,7 +33,7 @@
             in_specs=[pl.BlockSpec(memory_space=pl.ANY if anywhere else pltpu.VMEM)]
             * len(operands)
             + [pl.BlockSpec(memory_space=pl.ANY)] * len(after),
-            out_specs=[pl.BlockSpec(memory_space=pltpu.VMEM)] * len(outs),
+            out_specs=[pl.BlockSpec(memory_space=out_space)] * len(outs),
             scratch_shapes=[
                 pltpu.VMEM(*entry) if isinstance(entry, tuple) else entry
                 for entry in scratch
@@ -208,6 +208,18 @@
     state[8:16, 0:128] = jnp.broadcast_to(data_len, (8, 128))
     state[8:16, 128:512] = jnp.zeros((8, 384), F32)
     send[...] = jnp.concatenate([value] * 32, axis=0).astype(BF)
+
+
+def first_shard_kernel(places, got, state, send, state_here, send_here, sems):
+    shard_kernel(True, places, got, state_here, send_here)
+    copies = [
+        pltpu.make_async_copy(send_here, send, sems.at[0]),
+        pltpu.make_async_copy(state_here, state, sems.at[1]),
+    ]
+    for copy in copies:
+        copy.start()
+    for copy in copies:
+        copy.wait()
 
 
 def length_column(state):
@@ -373,11 +385,15 @@
     observations = observations.reshape(10, 64, 1024)
 
     def sum_dp(whole, extra, before_gather=()):
-        state, send = call(
-            functools.partial(shard_kernel, not extra),
-            [((16, 512), F32), ((256, 512), BF)],
-            name="shard",
-        )(exchange(whole), *extra)
+        shard = [((16, 512), F32), ((256, 512), BF)]
+        if extra:
+            kernel, scratch, space = functools.partial(shard_kernel, False), [], pltpu.VMEM
+        else:
+            kernel, space = first_shard_kernel, pltpu.HBM
+            scratch = shard + [pltpu.SemaphoreType.DMA((2,))]
+        state, send = call(kernel, shard, scratch, name="shard", out_space=space)(
+            exchange(whole), *extra
+        )
         mine = exchange(send)
         if before_gather:
             mine = hold(mine, (), before_gather)

time: 181 us -> 181 us (level)
  no operation moved by 1% of the time
where the time goes in v8:
time: 181 us
  blocking collectives  62 us (34%)
  starting transfers between devices  54.1 us (30%)
  waiting for transfers between devices  41.1 us (23%)
  Pallas kernels  16.8 us (9%)
  local copies, waits for them, and re-layouts  5.62 us (3%)
    all_to_all x4, blocking collectives, exchange(): lax.all_to_all(value.reshape(32, 8, width), ('z', 'y'), split_axis=0, con...  62 us
    ppermute x18, waiting for transfers between devices, shift(): return lax.ppermute(value, 'x', [(i, (i + step) % 4) for i in range(4)])  21 us
    ppermute x6, starting transfers between devices, swap_core(): return lax.ppermute(value, 'c', [(0, 1), (1, 0)])  19.9 us
    ppermute x18, starting transfers between devices, shift(): return lax.ppermute(value, 'x', [(i, (i + step) % 4) for i in range(4)])  19.6 us
    pallas_call x19, Pallas kernels, run(): pl.pallas_call(kernel, out_shape=[jax.ShapeDtypeStruct(out[0], out[1]) fo...  16.8 us
    all_to_all x2, waiting for transfers between devices, exchange(): lax.all_to_all(value.reshape(32, 8, width), ('z', 'y'), split_axis=0, con...  15.3 us
    all_to_all x2, starting transfers between devices, exchange(): lax.all_to_all(value.reshape(32, 8, width), ('z', 'y'), split_axis=0, con...  14.6 us
    unnamed x20, local copies, waits for them, and re-layouts  4.99 us
  transfers between devices with their start and end apart: 26, of which 21 were waited for; matrix products, arithmetic and copies ran while one was open for 0% of the time, Pallas kernels for 2%

profile of v8, /device:TPU:1, one launch (start us, length us, event | category | flops | bytes accessed | tf_op | source)
XLA Modules:
  0.0 180.5 jit_solution(13859036260118034317)
XLA Ops:
  0.6 1.7 copy-done.1
  2.4 1.4 pack.1
  3.8 0.5 copy-done.4
  4.3 1.0 start.1
  5.4 0.7 copy-done
  6.0 0.9 start_sum.1
  6.9 3.3 %collective-permute-start = (bf16[256,640]{1,0:T(8,128)(2,1)S(1)}, bf16[256,640]{1,0:T(8,128)(2,1)S(1)}, u32[]{:S(2)}, u32[]{:S(2)}) collective-permute-start(bf16[256,640]{1,0:T(8,128)(2,1)S(1)} %get-tuple-element.59), channel_id=1, source_target_pairs={{0,4},{4,0},{1,5},{5,1},{2,6},{6,2},{3,7},{7,3},{8,12},{12,8},{9,1... | collective-permute-start | bytes 983048 | tf_op jit(solution)/shard_map/ppermute | solution.py:364
  10.2 2.7 %collective-permute-start.2 = (bf16[5,128,512]{2,1,0:T(8,128)(2,1)}, bf16[5,128,512]{2,1,0:T(8,128)(2,1)}, u32[]{:S(2)}, u32[]{:S(2)}) collective-permute-start(bf16[5,128,512]{2,1,0:T(8,128)(2,1)} %get-tuple-element.55.refs_4_), channel_id=1, source_target_pairs={{0,3},{1,0},{2,1},{3,2},{4,7},{5,4},{6,5},{7,6},{8,11},{9,8},{10,9... | collective-permute-start | bytes 1966088 | tf_op jit(solution)/shard_map/ppermute | solution.py:360
  13.0 0.7 copy-done.3
  13.7 9.6 %all-to-all-start = ((bf16[32,8,640]{2,1,0:T(8,128)(2,1)}), bf16[32,8,640]{2,1,0:T(8,128)(2,1)}, u32[]{:S(2)}, u32[]{:S(2)}) async-start(bf16[32,8,640]{2,1,0:T(8,128)(2,1)} %bitcast.25), calls=%async_computation | async-start | bytes 655360 | tf_op jit(solution)/shard_map/all_to_all | solution.py:369
  23.3 4.6 %collective-permute-done.1.refs_2_.refs_7_ = bf16[5,128,512]{2,1,0:T(8,128)(2,1)S(1)} collective-permute-done((bf16[5,128,512]{2,1,0:T(8,128)(2,1)}, bf16[5,128,512]{2,1,0:T(8,128)(2,1)S(1)}, u32[]{:S(2)}, u32[]{:S(2)}) %collective-permute-start.1) | collective-permute-done | bytes 655392 | tf_op jit(solution)/shard_map/ppermute | solution.py:360
  28.0 1.3 collective-permute-start.3
  29.2 6.6 %all-to-all-done = bf16[32,8,640]{2,1,0:T(8,128)(2,1)} async-done(((bf16[32,8,640]{2,1,0:T(8,128)(2,1)}), bf16[32,8,640]{2,1,0:T(8,128)(2,1)}, u32[]{:S(2)}, u32[]{:S(2)}) %all-to-all-start) | async-done | bytes 327712 | tf_op jit(solution)/shard_map/all_to_all | solution.py:369
  35.9 1.2 shard.3
  37.1 0.6 copy-done.8
  37.7 0.7 copy-done.7
  38.4 5.0 %all-to-all-start.1 = ((bf16[32,8,512]{2,1,0:T(8,128)(2,1)}), bf16[32,8,512]{2,1,0:T(8,128)(2,1)S(1)}, u32[]{:S(2)}, u32[]{:S(2)}) async-start(bf16[32,8,512]{2,1,0:T(8,128)(2,1)} %bitcast.35), calls=%async_computation.1 | async-start | bytes 524288 | tf_op jit(solution)/shard_map/all_to_all | solution.py:369
  43.4 1.8 collective-permute-done.3.refs_1_.refs_0_
  45.2 8.6 %all-to-all-done.1 = bf16[32,8,512]{2,1,0:T(8,128)(2,1)S(1)} async-done(((bf16[32,8,512]{2,1,0:T(8,128)(2,1)}), bf16[32,8,512]{2,1,0:T(8,128)(2,1)S(1)}, u32[]{:S(2)}, u32[]{:S(2)}) %all-to-all-start.1) | async-done | bytes 262176 | tf_op jit(solution)/shard_map/all_to_all | solution.py:369
  53.8 3.6 %collective-permute-start.4 = (bf16[256,512]{1,0:T(8,128)(2,1)S(1)}, bf16[256,512]{1,0:T(8,128)(2,1)S(1)}, u32[]{:S(2)}, u32[]{:S(2)}) collective-permute-start(bf16[256,512]{1,0:T(8,128)(2,1)S(1)} %hold.3.refs_2_.refs_0_), channel_id=1, source_target_pairs={{0,4},{4,0},{1,5},{5,1},{2,6},{6,2},{3,7},{7,3},{8,12},{12,8},{9,1... | collective-permute-start | bytes 786440 | tf_op jit(solution)/shard_map/ppermute | solution.py:364
  57.4 1.3 fetch.1
  58.7 1.2 forward.2
  60.0 2.4 %collective-permute-start.6 = (bf16[208,128]{1,0:T(8,128)(2,1)S(1)}, bf16[208,128]{1,0:T(8,128)(2,1)S(1)}, u32[]{:S(2)}, u32[]{:S(2)}) collective-permute-start(bf16[208,128]{1,0:T(8,128)(2,1)S(1)} %get-tuple-element.65), channel_id=1, source_target_pairs={{0,2},{1,3},{2,0},{3,1},{4,6},{5,7},{6,4},{7,5},{8,10},{9,11},{10,... | collective-permute-start | bytes 159752 | tf_op jit(solution)/shard_map/ppermute | solution.py:360
  62.5 1.2 collective-permute-start.7
  63.6 1.3 collective-permute-done.5.refs_1_
  65.2 0.9 collective-permute-done.7.refs_3_
  66.1 1.6 data.2
  67.6 2.4 %collective-permute-start.8 = (bf16[208,128]{1,0:T(8,128)(2,1)S(1)}, bf16[208,128]{1,0:T(8,128)(2,1)S(1)}, u32[]{:S(2)}, u32[]{:S(2)}) collective-permute-start(bf16[208,128]{1,0:T(8,128)(2,1)S(1)} %get-tuple-element.71), channel_id=1, source_target_pairs={{0,3},{1,0},{2,1},{3,2},{4,7},{5,4},{6,5},{7,6},{8,11},{9,8},{10,9... | collective-permute-start | bytes 159752 | tf_op jit(solution)/shard_map/ppermute | solution.py:360
  70.3 0.5 collective-permute-start.10
  70.7 0.5 collective-permute-done.8.refs_2_
  71.3 3.4 %collective-permute-done.9.refs_3_ = bf16[208,128]{1,0:T(8,128)(2,1)S(1)} collective-permute-done((bf16[208,128]{1,0:T(8,128)(2,1)S(1)}, bf16[208,128]{1,0:T(8,128)(2,1)S(1)}, u32[]{:S(2)}, u32[]{:S(2)}) %collective-permute-start.9) | collective-permute-done | bytes 53280 | tf_op jit(solution)/shard_map/ppermute | solution.py:360
  74.7 0.4 collective-permute-done.10.refs_4_
  75.0 0.9 back.2
  75.9 2.9 %collective-permute-start.11 = (bf16[256,640]{1,0:T(8,128)(2,1)S(1)}, bf16[256,640]{1,0:T(8,128)(2,1)S(1)}, u32[]{:S(2)}, u32[]{:S(2)}) collective-permute-start(bf16[256,640]{1,0:T(8,128)(2,1)S(1)} %get-tuple-element.75), channel_id=1, source_target_pairs={{0,4},{4,0},{1,5},{5,1},{2,6},{6,2},{3,7},{7,3},{8,12},{12,8},{9,1... | collective-permute-start | bytes 983048 | tf_op jit(solution)/shard_map/ppermute | solution.py:364
  78.8 1.3 collective-permute-done.11.refs_1_
  80.2 16.0 %all_to_all.30 = bf16[32,8,640]{2,1,0:T(8,128)(2,1)S(1)} all-to-all(bf16[32,8,640]{2,1,0:T(8,128)(2,1)S(1)} %bitcast.26), channel_id=1, replica_groups=mesh['z'=8,'y'=4,'c'=2,'x'=4] {'z','y'}, dimensions={0} | all-to-all | bytes 655360 | tf_op jit(solution)/shard_map/all_to_all | solution.py:369
  96.4 15.0 %all_to_all.31 = bf16[32,8,512]{2,1,0:T(8,128)(2,1)S(1)} all-to-all(bf16[32,8,512]{2,1,0:T(8,128)(2,1)S(1)} %bitcast.36), channel_id=1, replica_groups=mesh['z'=8,'y'=4,'c'=2,'x'=4] {'z','y'}, dimensions={0} | all-to-all | bytes 524288 | tf_op jit(solution)/shard_map/all_to_all | solution.py:369
  111.4 3.6 %collective-permute-start.12 = (bf16[256,512]{1,0:T(8,128)(2,1)S(1)}, bf16[256,512]{1,0:T(8,128)(2,1)S(1)}, u32[]{:S(2)}, u32[]{:S(2)}) collective-permute-start(bf16[256,512]{1,0:T(8,128)(2,1)S(1)} %bitcast.31), channel_id=1, source_target_pairs={{0,4},{4,0},{1,5},{5,1},{2,6},{6,2},{3,7},{7,3},{8,12},{12,8},{9,1... | collective-permute-start | bytes 786440 | tf_op jit(solution)/shard_map/ppermute | solution.py:364
  114.9 1.2 collective-permute-done.12.refs_1_
  116.1 1.2 forward.3
  117.4 1.5 collective-permute-start.14
  118.9 1.8 collective-permute-start.15
  120.7 2.1 %collective-permute-done.13.refs_1_ = bf16[208,128]{1,0:T(8,128)(2,1)S(1)} collective-permute-done((bf16[208,128]{1,0:T(8,128)(2,1)S(1)}, bf16[208,128]{1,0:T(8,128)(2,1)S(1)}, u32[]{:S(2)}, u32[]{:S(2)}) %collective-permute-start.13) | collective-permute-done | bytes 53280 | tf_op jit(solution)/shard_map/ppermute | solution.py:360
  123.1 1.5 data.3
  124.6 2.5 %collective-permute-start.16 = (bf16[208,128]{1,0:T(8,128)(2,1)S(1)}, bf16[208,128]{1,0:T(8,128)(2,1)S(1)}, u32[]{:S(2)}, u32[]{:S(2)}) collective-permute-start(bf16[208,128]{1,0:T(8,128)(2,1)S(1)} %get-tuple-element.87), channel_id=1, source_target_pairs={{0,3},{1,0},{2,1},{3,2},{4,7},{5,4},{6,5},{7,6},{8,11},{9,8},{10,9... | collective-permute-start | bytes 159752 | tf_op jit(solution)/shard_map/ppermute | solution.py:360
  127.0 0.6 collective-permute-start.17
  127.7 0.5 collective-permute-done.16.refs_2_
  128.3 3.3 %collective-permute-done.17.refs_3_ = bf16[208,128]{1,0:T(8,128)(2,1)S(1)} collective-permute-done((bf16[208,128]{1,0:T(8,128)(2,1)S(1)}, bf16[208,128]{1,0:T(8,128)(2,1)S(1)}, u32[]{:S(2)}, u32[]{:S(2)}) %collective-permute-start.17) | collective-permute-done | bytes 53280 | tf_op jit(solution)/shard_map/ppermute | solution.py:360
  131.6 0.5 collective-permute-done.18.refs_4_
  132.1 0.9 back.3
  133.0 3.0 %collective-permute-start.19 = (bf16[256,640]{1,0:T(8,128)(2,1)S(1)}, bf16[256,640]{1,0:T(8,128)(2,1)S(1)}, u32[]{:S(2)}, u32[]{:S(2)}) collective-permute-start(bf16[256,640]{1,0:T(8,128)(2,1)S(1)} %get-tuple-element.91), channel_id=1, source_target_pairs={{0,4},{4,0},{1,5},{5,1},{2,6},{6,2},{3,7},{7,3},{8,12},{12,8},{9,1... | collective-permute-start | bytes 983048 | tf_op jit(solution)/shard_map/ppermute | solution.py:364
  136.0 1.3 collective-permute-done.19.refs_1_
  137.4 16.0 %all_to_all.32 = bf16[32,8,640]{2,1,0:T(8,128)(2,1)S(1)} all-to-all(bf16[32,8,640]{2,1,0:T(8,128)(2,1)S(1)} %bitcast.27), channel_id=1, replica_groups=mesh['z'=8,'y'=4,'c'=2,'x'=4] {'z','y'}, dimensions={0} | all-to-all | bytes 655360 | tf_op jit(solution)/shard_map/all_to_all | solution.py:369
  153.6 15.0 %all_to_all.33 = bf16[32,8,512]{2,1,0:T(8,128)(2,1)S(1)} all-to-all(bf16[32,8,512]{2,1,0:T(8,128)(2,1)S(1)} %bitcast.37), channel_id=1, replica_groups=mesh['z'=8,'y'=4,'c'=2,'x'=4] {'z','y'}, dimensions={0} | all-to-all | bytes 524288 | tf_op jit(solution)/shard_map/all_to_all | solution.py:369
  168.6 3.6 %collective-permute-start.20 = (bf16[256,512]{1,0:T(8,128)(2,1)S(1)}, bf16[256,512]{1,0:T(8,128)(2,1)S(1)}, u32[]{:S(2)}, u32[]{:S(2)}) collective-permute-start(bf16[256,512]{1,0:T(8,128)(2,1)S(1)} %bitcast.33), channel_id=1, source_target_pairs={{0,4},{4,0},{1,5},{5,1},{2,6},{6,2},{3,7},{7,3},{8,12},{12,8},{9,1... | collective-permute-start | bytes 786440 | tf_op jit(solution)/shard_map/ppermute | solution.py:364
  172.1 1.2 collective-permute-done.20.refs_1_
  173.3 0.4 last_model.1
  173.7 0.6 collective-permute-start.23
  174.3 1.0 collective-permute-start.22
  175.3 0.8 collective-permute-start.21
  176.0 1.4 solve.1
  177.4 0.6 slice_reduce_fusion
  178.2 1.0 collective-permute-done.21.refs_6_
  179.2 1.3 direct.1
  (34 shorter events, 1.8 us)
Async XLA Ops:
  0.6 1.7 copy-start.1
  2.4 1.9 %copy-start.4 = (bf16[2,5,64,1024]{3,2,1,0:T(8,128)(2,1)S(1)}, bf16[2,5,64,1024]{3,2,1,0:T(8,128)(2,1)}, u32[]{:S(2)}) copy-start(bf16[2,5,64,1024]{3,2,1,0:T(8,128)(2,1)} %param.5) | copy-start | bytes 3932164
  4.3 1.7 copy-start
  5.4 7.7 %copy-start.5 = (bf16[5,64,512]{2,1,0:T(8,128)(2,1)}, bf16[5,64,512]{2,1,0:T(8,128)(2,1)S(1)}, u32[]{:S(2)}) copy-start(bf16[5,64,512]{2,1,0:T(8,128)(2,1)S(1)} %get-tuple-element.67.refs_4_) | copy-start | bytes 983044
  6.9 6.0 %collective-permute-start = (bf16[256,640]{1,0:T(8,128)(2,1)S(1)}, bf16[256,640]{1,0:T(8,128)(2,1)S(1)}, u32[]{:S(2)}, u32[]{:S(2)}) collective-permute-start(bf16[256,640]{1,0:T(8,128)(2,1)S(1)} %get-tuple-element.59), channel_id=1, source_target_pairs={{0,4},{4,0},{1,5},{5,1},{2,6},{6,2},{3,7},{7,3},{8,12},{12,8},{9,1... | collective-permute-start | bytes 983048 | tf_op jit(solution)/shard_map/ppermute | solution.py:364
  10.2 17.7 %collective-permute-start.1 = (bf16[5,128,512]{2,1,0:T(8,128)(2,1)}, bf16[5,128,512]{2,1,0:T(8,128)(2,1)S(1)}, u32[]{:S(2)}, u32[]{:S(2)}) collective-permute-start(bf16[5,128,512]{2,1,0:T(8,128)(2,1)} %get-tuple-element.53.refs_2_), channel_id=1, source_target_pairs={{0,1},{1,2},{2,3},{3,0},{4,5},{5,6},{6,7},{7,4},{8,9},{9,10},{10,1... | collective-permute-start | bytes 1966088 | tf_op jit(solution)/shard_map/ppermute | solution.py:360
  10.2 17.7 %collective-permute-start.2 = (bf16[5,128,512]{2,1,0:T(8,128)(2,1)}, bf16[5,128,512]{2,1,0:T(8,128)(2,1)}, u32[]{:S(2)}, u32[]{:S(2)}) collective-permute-start(bf16[5,128,512]{2,1,0:T(8,128)(2,1)} %get-tuple-element.55.refs_4_), channel_id=1, source_target_pairs={{0,3},{1,0},{2,1},{3,2},{4,7},{5,4},{6,5},{7,6},{8,11},{9,8},{10,9... | collective-permute-start | bytes 1966088 | tf_op jit(solution)/shard_map/ppermute | solution.py:360
  13.0 0.7 copy-start.3
  13.7 22.1 %all-to-all-start = ((bf16[32,8,640]{2,1,0:T(8,128)(2,1)}), bf16[32,8,640]{2,1,0:T(8,128)(2,1)}, u32[]{:S(2)}, u32[]{:S(2)}) async-start(bf16[32,8,640]{2,1,0:T(8,128)(2,1)} %bitcast.25), calls=%async_computation | async-start | bytes 655360 | tf_op jit(solution)/shard_map/all_to_all | solution.py:369
  28.0 17.2 %collective-permute-start.3 = (bf16[5,128,512]{2,1,0:T(8,128)(2,1)}, bf16[5,128,512]{2,1,0:T(8,128)(2,1)}, u32[]{:S(2)}, u32[]{:S(2)}) collective-permute-start(bf16[5,128,512]{2,1,0:T(8,128)(2,1)} %hold.2), channel_id=1, source_target_pairs={{0,2},{1,3},{2,0},{3,1},{4,6},{5,7},{6,4},{7,5},{8,10},{9,11},{10,... | collective-permute-start | bytes 1966088 | tf_op jit(solution)/shard_map/ppermute | solution.py:360
  37.1 0.6 copy-start.8
  37.7 0.7 copy-start.7
  38.4 15.4 %all-to-all-start.1 = ((bf16[32,8,512]{2,1,0:T(8,128)(2,1)}), bf16[32,8,512]{2,1,0:T(8,128)(2,1)S(1)}, u32[]{:S(2)}, u32[]{:S(2)}) async-start(bf16[32,8,512]{2,1,0:T(8,128)(2,1)} %bitcast.35), calls=%async_computation.1 | async-start | bytes 524288 | tf_op jit(solution)/shard_map/all_to_all | solution.py:369
  53.8 4.9 %collective-permute-start.4 = (bf16[256,512]{1,0:T(8,128)(2,1)S(1)}, bf16[256,512]{1,0:T(8,128)(2,1)S(1)}, u32[]{:S(2)}, u32[]{:S(2)}) collective-permute-start(bf16[256,512]{1,0:T(8,128)(2,1)S(1)} %hold.3.refs_2_.refs_0_), channel_id=1, source_target_pairs={{0,4},{4,0},{1,5},{5,1},{2,6},{6,2},{3,7},{7,3},{8,12},{12,8},{9,1... | collective-permute-start | bytes 786440 | tf_op jit(solution)/shard_map/ppermute | solution.py:364
  58.7 7.4 %copy-start.2 = (bf16[2,5,4,32,1024]{4,3,2,1,0:T(8,128)(2,1)S(1)}, bf16[2,5,4,32,1024]{4,3,2,1,0:T(8,128)(2,1)}, u32[]{:S(2)}) copy-start(bf16[2,5,4,32,1024]{4,3,2,1,0:T(8,128)(2,1)} %param.3) | copy-start | bytes 7864324
  58.7 7.4 %copy-start.6 = (bf16[5,64,512]{2,1,0:T(8,128)(2,1)S(1)}, bf16[5,64,512]{2,1,0:T(8,128)(2,1)}, u32[]{:S(2)}) copy-start(bf16[5,64,512]{2,1,0:T(8,128)(2,1)} %copy-done.5) | copy-start | bytes 983044
  58.7 7.4 %copy-start.9 = (f32[16,512]{1,0:T(8,128)S(1)}, f32[16,512]{1,0:T(8,128)}, u32[]{:S(2)}) copy-start(f32[16,512]{1,0:T(8,128)} %copy-done.8) | copy-start | bytes 98308
  59.9 5.0 %collective-permute-start.5 = (bf16[208,128]{1,0:T(8,128)(2,1)S(1)}, bf16[208,128]{1,0:T(8,128)(2,1)S(1)}, u32[]{:S(2)}, u32[]{:S(2)}) collective-permute-start(bf16[208,128]{1,0:T(8,128)(2,1)S(1)} %get-tuple-element.64), channel_id=1, source_target_pairs={{0,1},{1,2},{2,3},{3,0},{4,5},{5,6},{6,7},{7,4},{8,9},{9,10},{10,1... | collective-permute-start | bytes 159752 | tf_op jit(solution)/shard_map/ppermute | solution.py:360
  60.0 5.1 %collective-permute-start.6 = (bf16[208,128]{1,0:T(8,128)(2,1)S(1)}, bf16[208,128]{1,0:T(8,128)(2,1)S(1)}, u32[]{:S(2)}, u32[]{:S(2)}) collective-permute-start(bf16[208,128]{1,0:T(8,128)(2,1)S(1)} %get-tuple-element.65), channel_id=1, source_target_pairs={{0,2},{1,3},{2,0},{3,1},{4,6},{5,7},{6,4},{7,5},{8,10},{9,11},{10,... | collective-permute-start | bytes 159752 | tf_op jit(solution)/shard_map/ppermute | solution.py:360
  62.5 3.6 %collective-permute-start.7 = (bf16[208,128]{1,0:T(8,128)(2,1)S(1)}, bf16[208,128]{1,0:T(8,128)(2,1)S(1)}, u32[]{:S(2)}, u32[]{:S(2)}) collective-permute-start(bf16[208,128]{1,0:T(8,128)(2,1)S(1)} %get-tuple-element.66), channel_id=1, source_target_pairs={{0,3},{1,0},{2,1},{3,2},{4,7},{5,4},{6,5},{7,6},{8,11},{9,8},{10,9... | collective-permute-start | bytes 159752 | tf_op jit(solution)/shard_map/ppermute | solution.py:360
  67.6 3.6 %collective-permute-start.8 = (bf16[208,128]{1,0:T(8,128)(2,1)S(1)}, bf16[208,128]{1,0:T(8,128)(2,1)S(1)}, u32[]{:S(2)}, u32[]{:S(2)}) collective-permute-start(bf16[208,128]{1,0:T(8,128)(2,1)S(1)} %get-tuple-element.71), channel_id=1, source_target_pairs={{0,3},{1,0},{2,1},{3,2},{4,7},{5,4},{6,5},{7,6},{8,11},{9,8},{10,9... | collective-permute-start | bytes 159752 | tf_op jit(solution)/shard_map/ppermute | solution.py:360
  70.1 4.6 %collective-permute-start.9 = (bf16[208,128]{1,0:T(8,128)(2,1)S(1)}, bf16[208,128]{1,0:T(8,128)(2,1)S(1)}, u32[]{:S(2)}, u32[]{:S(2)}) collective-permute-start(bf16[208,128]{1,0:T(8,128)(2,1)S(1)} %get-tuple-element.72), channel_id=1, source_target_pairs={{0,2},{1,3},{2,0},{3,1},{4,6},{5,7},{6,4},{7,5},{8,10},{9,11},{10,... | collective-permute-start | bytes 159752 | tf_op jit(solution)/shard_map/ppermute | solution.py:360
  70.3 4.8 %collective-permute-start.10 = (bf16[208,128]{1,0:T(8,128)(2,1)S(1)}, bf16[208,128]{1,0:T(8,128)(2,1)S(1)}, u32[]{:S(2)}, u32[]{:S(2)}) collective-permute-start(bf16[208,128]{1,0:T(8,128)(2,1)S(1)} %get-tuple-element.73), channel_id=1, source_target_pairs={{0,1},{1,2},{2,3},{3,0},{4,5},{5,6},{6,7},{7,4},{8,9},{9,10},{10,1... | collective-permute-start | bytes 159752 | tf_op jit(solution)/shard_map/ppermute | solution.py:360
  75.9 4.2 %collective-permute-start.11 = (bf16[256,640]{1,0:T(8,128)(2,1)S(1)}, bf16[256,640]{1,0:T(8,128)(2,1)S(1)}, u32[]{:S(2)}, u32[]{:S(2)}) collective-permute-start(bf16[256,640]{1,0:T(8,128)(2,1)S(1)} %get-tuple-element.75), channel_id=1, source_target_pairs={{0,4},{4,0},{1,5},{5,1},{2,6},{6,2},{3,7},{7,3},{8,12},{12,8},{9,1... | collective-permute-start | bytes 983048 | tf_op jit(solution)/shard_map/ppermute | solution.py:364
  111.4 4.7 %collective-permute-start.12 = (bf16[256,512]{1,0:T(8,128)(2,1)S(1)}, bf16[256,512]{1,0:T(8,128)(2,1)S(1)}, u32[]{:S(2)}, u32[]{:S(2)}) collective-permute-start(bf16[256,512]{1,0:T(8,128)(2,1)S(1)} %bitcast.31), channel_id=1, source_target_pairs={{0,4},{4,0},{1,5},{5,1},{2,6},{6,2},{3,7},{7,3},{8,12},{12,8},{9,1... | collective-permute-start | bytes 786440 | tf_op jit(solution)/shard_map/ppermute | solution.py:364
  117.3 5.4 %collective-permute-start.13 = (bf16[208,128]{1,0:T(8,128)(2,1)S(1)}, bf16[208,128]{1,0:T(8,128)(2,1)S(1)}, u32[]{:S(2)}, u32[]{:S(2)}) collective-permute-start(bf16[208,128]{1,0:T(8,128)(2,1)S(1)} %get-tuple-element.79), channel_id=1, source_target_pairs={{0,1},{1,2},{2,3},{3,0},{4,5},{5,6},{6,7},{7,4},{8,9},{9,10},{10,1... | collective-permute-start | bytes 159752 | tf_op jit(solution)/shard_map/ppermute | solution.py:360
  117.4 5.3 %collective-permute-start.14 = (bf16[208,128]{1,0:T(8,128)(2,1)S(1)}, bf16[208,128]{1,0:T(8,128)(2,1)S(1)}, u32[]{:S(2)}, u32[]{:S(2)}) collective-permute-start(bf16[208,128]{1,0:T(8,128)(2,1)S(1)} %get-tuple-element.80), channel_id=1, source_target_pairs={{0,2},{1,3},{2,0},{3,1},{4,6},{5,7},{6,4},{7,5},{8,10},{9,11},{10,... | collective-permute-start | bytes 159752 | tf_op jit(solution)/shard_map/ppermute | solution.py:360
  118.9 4.2 %collective-permute-start.15 = (bf16[208,128]{1,0:T(8,128)(2,1)S(1)}, bf16[208,128]{1,0:T(8,128)(2,1)S(1)}, u32[]{:S(2)}, u32[]{:S(2)}) collective-permute-start(bf16[208,128]{1,0:T(8,128)(2,1)S(1)} %get-tuple-element.81), channel_id=1, source_target_pairs={{0,3},{1,0},{2,1},{3,2},{4,7},{5,4},{6,5},{7,6},{8,11},{9,8},{10,9... | collective-permute-start | bytes 159752 | tf_op jit(solution)/shard_map/ppermute | solution.py:360
  124.6 3.7 %collective-permute-start.16 = (bf16[208,128]{1,0:T(8,128)(2,1)S(1)}, bf16[208,128]{1,0:T(8,128)(2,1)S(1)}, u32[]{:S(2)}, u32[]{:S(2)}) collective-permute-start(bf16[208,128]{1,0:T(8,128)(2,1)S(1)} %get-tuple-element.87), channel_id=1, source_target_pairs={{0,3},{1,0},{2,1},{3,2},{4,7},{5,4},{6,5},{7,6},{8,11},{9,8},{10,9... | collective-permute-start | bytes 159752 | tf_op jit(solution)/shard_map/ppermute | solution.py:360
  127.0 4.5 %collective-permute-start.17 = (bf16[208,128]{1,0:T(8,128)(2,1)S(1)}, bf16[208,128]{1,0:T(8,128)(2,1)S(1)}, u32[]{:S(2)}, u32[]{:S(2)}) collective-permute-start(bf16[208,128]{1,0:T(8,128)(2,1)S(1)} %get-tuple-element.88), channel_id=1, source_target_pairs={{0,2},{1,3},{2,0},{3,1},{4,6},{5,7},{6,4},{7,5},{8,10},{9,11},{10,... | collective-permute-start | bytes 159752 | tf_op jit(solution)/shard_map/ppermute | solution.py:360
  127.6 4.5 %collective-permute-start.18 = (bf16[208,128]{1,0:T(8,128)(2,1)S(1)}, bf16[208,128]{1,0:T(8,128)(2,1)S(1)}, u32[]{:S(2)}, u32[]{:S(2)}) collective-permute-start(bf16[208,128]{1,0:T(8,128)(2,1)S(1)} %get-tuple-element.89), channel_id=1, source_target_pairs={{0,1},{1,2},{2,3},{3,0},{4,5},{5,6},{6,7},{7,4},{8,9},{9,10},{10,1... | collective-permute-start | bytes 159752 | tf_op jit(solution)/shard_map/ppermute | solution.py:360
  133.0 4.3 %collective-permute-start.19 = (bf16[256,640]{1,0:T(8,128)(2,1)S(1)}, bf16[256,640]{1,0:T(8,128)(2,1)S(1)}, u32[]{:S(2)}, u32[]{:S(2)}) collective-permute-start(bf16[256,640]{1,0:T(8,128)(2,1)S(1)} %get-tuple-element.91), channel_id=1, source_target_pairs={{0,4},{4,0},{1,5},{5,1},{2,6},{6,2},{3,7},{7,3},{8,12},{12,8},{9,1... | collective-permute-start | bytes 983048 | tf_op jit(solution)/shard_map/ppermute | solution.py:364
  168.6 4.7 %collective-permute-start.20 = (bf16[256,512]{1,0:T(8,128)(2,1)S(1)}, bf16[256,512]{1,0:T(8,128)(2,1)S(1)}, u32[]{:S(2)}, u32[]{:S(2)}) collective-permute-start(bf16[256,512]{1,0:T(8,128)(2,1)S(1)} %bitcast.33), channel_id=1, source_target_pairs={{0,4},{4,0},{1,5},{5,1},{2,6},{6,2},{3,7},{7,3},{8,12},{12,8},{9,1... | collective-permute-start | bytes 786440 | tf_op jit(solution)/shard_map/ppermute | solution.py:364
  173.7 4.4 %collective-permute-start.23 = (f32[8,128]{1,0:T(8,128)S(1)}, f32[8,128]{1,0:T(8,128)S(1)}, u32[]{:S(2)}, u32[]{:S(2)}) collective-permute-start(f32[8,128]{1,0:T(8,128)S(1)} %get-tuple-element.98.refs_7_.refs_5_), channel_id=1, source_target_pairs={{0,3},{1,0},{2,1},{3,2},{4,7},{5,4},{6,5},{7,6},{8,11},{9,8},{10,9... | collective-permute-start | bytes 12296 | tf_op jit(solution)/shard_map/ppermute | solution.py:360
  174.3 4.0 %collective-permute-start.22 = (f32[8,128]{1,0:T(8,128)S(1)}, f32[8,128]{1,0:T(8,128)S(1)}, u32[]{:S(2)}, u32[]{:S(2)}) collective-permute-start(f32[8,128]{1,0:T(8,128)S(1)} %get-tuple-element.98.refs_7_.refs_5_), channel_id=1, source_target_pairs={{0,2},{1,3},{2,0},{3,1},{4,6},{5,7},{6,4},{7,5},{8,10},{9,11},{10,... | collective-permute-start | bytes 12296 | tf_op jit(solution)/shard_map/ppermute | solution.py:360
  175.3 4.0 %collective-permute-start.21 = (f32[8,128]{1,0:T(8,128)S(1)}, f32[8,128]{1,0:T(8,128)S(1)}, u32[]{:S(2)}, u32[]{:S(2)}) collective-permute-start(f32[8,128]{1,0:T(8,128)S(1)} %get-tuple-element.98.refs_7_.refs_5_), channel_id=1, source_target_pairs={{0,1},{1,2},{2,3},{3,0},{4,5},{5,6},{6,7},{7,4},{8,9},{9,10},{10,1... | collective-permute-start | bytes 12296 | tf_op jit(solution)/shard_map/ppermute | solution.py:360
